TPU v7x, 256 devices: a whole 4x4x8 slice. The times are simulated.
256 devices in a mesh: theta: 128 (over x, y_hi, z, core), rad: 2 (over y_lo).
Axes of the slice: x: 4, y: 4 (y_hi: 2, y_lo: 2; y = y_hi * 2 + y_lo), z: 8, core: 2. Of those that a mesh axis runs over, the one named last changes fastest.
Arguments:
- q_level: float32 [5, 32, 1024, 256], P(None, 'rad', 'theta'), as said below
- q_prev: float32 [5, 32, 1024, 256], P(None, 'rad', 'theta'), as said below
- blade_row: int32 [256], replicated, may hold values from 0 to 2, as said below
Outputs:
- flow_state: float32 [5, 32, 1024, 256], P(None, 'rad', 'theta')
- spectra: float32 [256, 32, 256], P('theta', 'rad')
Inputs may be any that keep to these rules, and one draw needn't show every extreme that they name: q_level holds conserved variables of a state whose density lies within 0.8 to 1.25, pressure within 0.55 to 0.9, axial velocity within 0.05 to 0.95, radial velocity within -0.3 to 0.3 and swirl velocity within -0.6 to 0.6. q_prev holds conserved variables of a state within the same bounds as q_level. `blade_row`: 0 marks a gap, 1 the rotor, 2 a stator; along the axial stations the rows come in contiguous runs: gap, stator, gap, rotor, gap, stator, gap.
All inputs are finite; a program needn't handle non-finite values.
Results may differ from a plain program's by a relative error of at most 0.0003.
Values sent between devices are 32-bit elements; how exact they have to be, the bound alone decides.
No kernel may reach another device: no remote copies, remote signals or barrier semaphores. Data moves between devices by JAX's collectives and lax.ppermute only.
A program may use at most 64 MiB of HBM per device.

v0:
```python
import math

import jax
import jax.numpy as jnp
from jax import lax
from jax.sharding import PartitionSpec as P

MODES = 64


GAMMA = 1.4
CFL = 0.5
DT_PHYS = 0.1
KAPPA = 2.0


def extended_2(cells, sides, width, closed):
    for axis, dim in sides:
        count = lax.axis_size(axis)
        ends = count if closed else count - 1
        head = lax.slice_in_dim(cells, 0, width, axis=dim)
        tail = lax.slice_in_dim(cells, cells.shape[dim] - width, cells.shape[dim], axis=dim)
        cells = jnp.concatenate(
            [
                lax.ppermute(tail, axis, [(i, (i + 1) % count) for i in range(ends)]),
                cells,
                lax.ppermute(head, axis, [((i + 1) % count, i) for i in range(ends)]),
            ],
            axis=dim,
        )
    return cells


def take_range(values, along, first_index, stop_index):
    return lax.slice_in_dim(values, first_index, stop_index, axis=along)


def primitive_of(flow):
    density = flow[0]
    axial_speed = flow[1] / density
    radial_speed = flow[2] / density
    swirl_speed = flow[3] / density
    kinetic = 0.5 * (flow[1] * axial_speed + flow[2] * radial_speed + flow[3] * swirl_speed)
    pressure = (GAMMA - 1.0) * (flow[4] - kinetic)
    sound_speed = jnp.sqrt(GAMMA * pressure / density)
    return jnp.stack([axial_speed, radial_speed, swirl_speed, pressure, sound_speed])


def face_flux(flow, primitive, component, along):
    normal = primitive[component - 1]
    flux_term = flow * normal[None]
    flux_term = flux_term.at[component].add(primitive[3])
    flux_term = flux_term.at[4].add(primitive[3] * normal)
    wave_speed = jnp.abs(normal) + primitive[4]
    length = flow.shape[along]
    left_flow = take_range(flow, along, 0, length - 1)
    right_flow = take_range(flow, along, 1, length)
    mean_flux = 0.5 * (
        take_range(flux_term, along, 0, length - 1) + take_range(flux_term, along, 1, length)
    )
    fastest = jnp.maximum(
        take_range(wave_speed, along - 1, 0, length - 1),
        take_range(wave_speed, along - 1, 1, length),
    )
    return mean_flux - 0.5 * fastest[None] * (right_flow - left_flow)


def geometry(total_rows, circle_cells, first_row, band_rows):
    mean_radius = circle_cells / (2.0 * math.pi)
    row_index = jnp.arange(band_rows, dtype=jnp.float32) + jnp.asarray(first_row).astype(
        jnp.float32
    )
    radius = mean_radius * (0.8 + 0.4 * (row_index + 0.5) / total_rows)
    inner_face = mean_radius * (0.8 + 0.4 * row_index / total_rows)
    outer_face = mean_radius * (0.8 + 0.4 * (row_index + 1.0) / total_rows)
    theta_step = 2.0 * math.pi / circle_cells
    spin_rate = 1.0 / (1.2 * mean_radius)
    return (radius, inner_face, outer_face, theta_step, spin_rate)


def pseudo_step(
    extended, source, radius, inner_face, outer_face, theta_step, spin_rate, rotor_frame, bladed
):
    primitive = primitive_of(extended)
    center = extended[:, 1:-1, 1:-1, :]
    center_prim = primitive[:, 1:-1, 1:-1, :]
    axial_flow = jnp.concatenate([center[..., :1], center, center[..., -1:]], axis=3)
    axial_prim = jnp.concatenate([center_prim[..., :1], center_prim, center_prim[..., -1:]], axis=3)
    axial_faces = face_flux(axial_flow, axial_prim, 1, 3)
    radial_faces = face_flux(extended[:, :, 1:-1, :], primitive[:, :, 1:-1, :], 2, 1)
    circ_faces = face_flux(extended[:, 1:-1], primitive[:, 1:-1], 3, 2)
    radius_col = radius[:, None, None]
    spacing = radius_col * theta_step
    divergence = axial_faces[..., 1:] - axial_faces[..., :-1]
    divergence = (
        divergence
        + (
            outer_face[:, None, None] * radial_faces[:, 1:]
            - inner_face[:, None, None] * radial_faces[:, :-1]
        )
        / radius_col
    )
    divergence = divergence + (circ_faces[:, :, 1:] - circ_faces[:, :, :-1]) / spacing
    density = center[0]
    axial_speed = center_prim[0]
    radial_speed = center_prim[1]
    swirl_speed = center_prim[2]
    pressure = center_prim[3]
    sound_speed = center_prim[4]
    blade_force = -KAPPA * bladed * density * (swirl_speed - rotor_frame * spin_rate * radius_col)
    zeros_field = jnp.zeros_like(density)
    sources = jnp.stack(
        [
            zeros_field,
            zeros_field,
            (density * swirl_speed * swirl_speed + pressure) / radius_col,
            blade_force - density * radial_speed * swirl_speed / radius_col,
            swirl_speed * blade_force,
        ]
    )
    pseudo_dt = CFL / (
        jnp.abs(axial_speed)
        + jnp.abs(radial_speed)
        + jnp.abs(swirl_speed) / spacing
        + sound_speed * (2.0 + 1.0 / spacing)
    )
    return (center + pseudo_dt[None] * (source - divergence + sources)) / (
        1.0 + 1.5 * pseudo_dt[None] / DT_PHYS
    )


def reflect_rows(rows):
    return rows * jnp.array([1.0, 1.0, -1.0, 1.0, 1.0], dtype=rows.dtype)[:, None, None, None]


def field_pair(flow):
    density = flow[0]
    kinetic = 0.5 * (flow[1] * flow[1] + flow[2] * flow[2] + flow[3] * flow[3]) / density
    pressure = (GAMMA - 1.0) * (flow[4] - kinetic)
    return jnp.stack([pressure, flow[1] / density])


def mode_basis(circle_cells):
    cells = jnp.arange(circle_cells, dtype=jnp.int32)
    orders = jnp.arange(1, MODES + 1, dtype=jnp.int32)
    phase = (cells[:, None] * orders[None, :] % circle_cells).astype(jnp.float32) * (
        2.0 * math.pi / circle_cells
    )
    return jnp.concatenate([jnp.cos(phase), -jnp.sin(phase)], axis=1) / math.sqrt(circle_cells)


def per_device(q_level, q_prev, blade_row):
    band_rows = q_level.shape[1]
    sector_cells = q_level.shape[2]
    band_count = lax.axis_size("rad")
    sectors = lax.axis_size("theta")
    band_index = lax.axis_index("rad")
    circle_cells = sector_cells * sectors
    radius, inner_face, outer_face, theta_step, spin_rate = geometry(
        band_rows * band_count, circle_cells, band_index * band_rows, band_rows
    )
    rotor_frame = (blade_row == 1).astype(jnp.float32)
    bladed = (blade_row > 0).astype(jnp.float32)
    source = (4.0 * q_level - q_prev) / (2.0 * DT_PHYS)
    flow_state = q_level
    for sweep in range(2):
        wrapped_state = extended_2(flow_state, (("theta", 2),), 1, True)
        padded = extended_2(wrapped_state, (("rad", 1),), 1, False)
        hub_ghost = jnp.where(band_index == 0, reflect_rows(padded[:, 1:2]), padded[:, :1])
        tip_ghost = jnp.where(
            band_index == band_count - 1, reflect_rows(padded[:, -2:-1]), padded[:, -1:]
        )
        flow_state = pseudo_step(
            jnp.concatenate([hub_ghost, padded[:, 1:-1], tip_ghost], axis=1),
            source,
            radius,
            inner_face,
            outer_face,
            theta_step,
            spin_rate,
            rotor_frame,
            bladed,
        )
    fields = field_pair(flow_state)
    basis = mode_basis(circle_cells)
    product = jnp.einsum(
        "frsa,sc->arfc",
        lax.all_to_all(fields, "theta", split_axis=3, concat_axis=2, tiled=True),
        basis,
        precision=lax.Precision.HIGHEST,
    )
    spectra = product.reshape(product.shape[0], product.shape[1], 4 * MODES)
    return (flow_state, spectra)


def solution(mesh):
    in_specs = (P(None, "rad", "theta", None), P(None, "rad", "theta", None), P())
    out_specs = (P(None, "rad", "theta", None), P("theta", "rad", None))
    return jax.shard_map(
        per_device, mesh=mesh, in_specs=in_specs, out_specs=out_specs, check_vma=False
    )
```

profile of v0, /device:TPU:1, one launch (start us, length us, event | category | flops | bytes accessed | tf_op | source)
XLA Modules:
  0.0 92.4 jit_solution(16527426441448339947)
XLA Ops:
  0.6 1.4 %copy.146 = f32[5,16,8,256]{3,1,2,0:T(8,128)S(1)} copy(f32[5,16,8,256]{3,2,1,0:T(8,128)} %param.31) | data formatting | bytes 1310720 | tf_op args[0]
  2.0 3.1 %collective-permute-start = (f32[5,16,1,256]{3,1,2,0:T(8,128)S(1)}, f32[5,16,1,256]{3,1,2,0:T(8,128)S(1)}, u32[]{:S(2)}, u32[]{:S(2)}) collective-permute-start(f32[5,16,1,256]{3,1,2,0:T(8,128)S(1)} %get-tuple-element.213), channel_id=1, source_target_pairs={{0,2},{2,4},{4,6},{6,8},{8,10},{10,12},{12,14},{14,16},{16,18},{18... | collective-permute-start | bytes 245768 | tf_op jit(solution)/shard_map/ppermute | solution.py:25
  5.1 0.3 collective-permute-start.1
  5.6 1.4 %pad_maximum_fusion.10 = f32[5,16,8,258]{3,2,1,0:T(8,128)} fusion(f32[5,16,8,1]{3,2,1,0:T(8,128)S(1)} %get-tuple-element.211, f32[5,16,8,256]{3,2,1,0:T(8,128)S(1)} %copy-done, f32[5,16,8,1]{3,2,1,0:T(8,128)S(1)} %get-tuple-element.210), kind=kLoop, calls=%fused_computation.32 | loop fusion | flops 330240 | bytes 1320960 | tf_op jit(solution)/shard_map/concatenate | solution.py:87
  7.0 1.3 %pad_maximum_fusion.11 = (f32[5,16,8,257]{3,2,1,0:T(8,128)S(1)}, f32[5,16,8,257]{3,2,1,0:T(8,128)}) fusion(f32[5,16,8,1]{3,2,1,0:T(8,128)S(1)} %get-tuple-element.211, f32[5,16,8,256]{3,2,1,0:T(8,128)S(1)} %copy-done, f32[5,16,8,1]{3,2,1,0:T(8,128)S(1)} %get-tuple-element.210), kind=kLoop, calls=%fused_computation.33 | loop fusion | flops 328960 | bytes 1976320 | tf_op jit(solution)/shard_map/concatenate | solution.py:87
  8.4 0.2 constant_dynamic-update-slice_fusion.1
  8.6 0.4 collective-permute-done.1
  9.1 3.2 %collective-permute-start.2 = (f32[5,1,10,256]{3,1,2,0:T(1,128)S(1)}, f32[5,1,10,256]{3,1,2,0:T(1,128)S(1)}, u32[]{:S(2)}, u32[]{:S(2)}) collective-permute-start(f32[5,1,10,256]{3,1,2,0:T(1,128)S(1)} %get-tuple-element.200), channel_id=1, source_target_pairs={{0,1},{2,3},{4,5},{6,7},{8,9},{10,11},{12,13},{14,15},{16,17},{18,... | collective-permute-start | bytes 153608 | tf_op jit(solution)/shard_map/ppermute | solution.py:25
  12.3 1.3 %collective-permute-start.3 = (f32[5,1,10,256]{3,1,2,0:T(1,128)S(1)}, f32[5,1,10,256]{3,1,2,0:T(1,128)S(1)}, u32[]{:S(2)}, u32[]{:S(2)}) collective-permute-start(f32[5,1,10,256]{3,1,2,0:T(1,128)S(1)} %get-tuple-element.201), channel_id=1, source_target_pairs={{1,0},{3,2},{5,4},{7,6},{9,8},{11,10},{13,12},{15,14},{17,16},{19,... | collective-permute-start | bytes 153608 | tf_op jit(solution)/shard_map/ppermute | solution.py:27
  13.6 3.5 %collective-permute-done.3 = f32[5,1,10,256]{3,1,2,0:T(1,128)S(1)} collective-permute-done((f32[5,1,10,256]{3,1,2,0:T(1,128)S(1)}, f32[5,1,10,256]{3,1,2,0:T(1,128)S(1)}, u32[]{:S(2)}, u32[]{:S(2)}) %collective-permute-start.3) | collective-permute-done | bytes 51232 | tf_op jit(solution)/shard_map/ppermute | solution.py:27
  17.3 0.2 pad_maximum_fusion
  18.9 0.2 fusion.74
  19.1 0.9 %copy-done.2 = f32[5,16,8,258]{3,2,1,0:T(8,128)S(1)} copy-done((f32[5,16,8,258]{3,2,1,0:T(8,128)S(1)}, f32[5,16,8,258]{3,2,1,0:T(8,128)}, u32[]{:S(2)}) %copy-start.2) | copy-done | bytes 660504
  20.0 0.2 copy_multiply_fusion
  20.5 0.4 fusion.14
  21.0 0.2 divide_subtract_fusion.1
  21.2 0.9 %copy-done.1 = f32[5,16,8,257]{3,2,1,0:T(8,128)S(1)} copy-done((f32[5,16,8,257]{3,2,1,0:T(8,128)S(1)}, f32[5,16,8,257]{3,2,1,0:T(8,128)}, u32[]{:S(2)}) %copy-start.1) | copy-done | bytes 657944
  22.1 0.5 fusion.17
  22.6 0.2 fusion.23
  22.8 0.9 copy-done.3
  23.7 1.0 %fusion.45 = f32[5,16,8,256]{3,1,2,0:T(8,128)S(1)} fusion(f32[1,16,8,256]{3,1,2,0:T(8,128)S(1)} %get-tuple-element.191, f32[1,16,8,256]{3,1,2,0:T(8,128)S(1)} %get-tuple-element.190, f32[1,16,8,256]{3,1,2,0:T(8,128)S(1)} %get-tuple-element.193, f32[5,16,9,256]{3,1,2,0:T(8,128)S(1)} %fusion.23, f32[5,17,8,256]{3,1,2,0:T(8,128)S(1)} %fusion.14, ...), kind=kLoop, calls=%fused_computation.83 | loop fusion | flops 3276800 | bytes 6553876 | tf_op jit(solution)/shard_map/div | solution.py:127
  24.7 8.6 %collective-permute-start.5 = (f32[5,16,1,256]{3,1,2,0:T(8,128)S(1)}, f32[5,16,1,256]{3,1,2,0:T(8,128)S(1)}, u32[]{:S(2)}, u32[]{:S(2)}) collective-permute-start(f32[5,16,1,256]{3,1,2,0:T(8,128)S(1)} %get-tuple-element.207), channel_id=1, source_target_pairs={{2,0},{4,2},{6,4},{8,6},{10,8},{12,10},{14,12},{16,14},{18,16},{20... | collective-permute-start | bytes 245768 | tf_op jit(solution)/shard_map/ppermute | solution.py:27
  33.3 0.9 collective-permute-done.5
  34.3 5.4 %collective-permute-done.4 = f32[5,16,1,256]{3,1,2,0:T(8,128)S(1)} collective-permute-done((f32[5,16,1,256]{3,1,2,0:T(8,128)S(1)}, f32[5,16,1,256]{3,1,2,0:T(8,128)S(1)}, u32[]{:S(2)}, u32[]{:S(2)}) %collective-permute-start.4) | collective-permute-done | bytes 81952 | tf_op jit(solution)/shard_map/ppermute | solution.py:25
  39.8 1.3 %collective-permute-start.6 = (f32[5,1,10,256]{3,1,2,0:T(1,128)S(1)}, f32[5,1,10,256]{3,1,2,0:T(1,128)S(1)}, u32[]{:S(2)}, u32[]{:S(2)}) collective-permute-start(f32[5,1,10,256]{3,1,2,0:T(1,128)S(1)} %get-tuple-element.198), channel_id=1, source_target_pairs={{0,1},{2,3},{4,5},{6,7},{8,9},{10,11},{12,13},{14,15},{16,17},{18,... | collective-permute-start | bytes 153608 | tf_op jit(solution)/shard_map/ppermute | solution.py:25
  41.1 1.5 %collective-permute-start.7 = (f32[5,1,10,256]{3,1,2,0:T(1,128)S(1)}, f32[5,1,10,256]{3,1,2,0:T(1,128)S(1)}, u32[]{:S(2)}, u32[]{:S(2)}) collective-permute-start(f32[5,1,10,256]{3,1,2,0:T(1,128)S(1)} %get-tuple-element.199), channel_id=1, source_target_pairs={{1,0},{3,2},{5,4},{7,6},{9,8},{11,10},{13,12},{15,14},{17,16},{19,... | collective-permute-start | bytes 153608 | tf_op jit(solution)/shard_map/ppermute | solution.py:27
  42.7 3.5 %collective-permute-done.7 = f32[5,1,10,256]{3,1,2,0:T(1,128)S(1)} collective-permute-done((f32[5,1,10,256]{3,1,2,0:T(1,128)S(1)}, f32[5,1,10,256]{3,1,2,0:T(1,128)S(1)}, u32[]{:S(2)}, u32[]{:S(2)}) %collective-permute-start.7) | collective-permute-done | bytes 51232 | tf_op jit(solution)/shard_map/ppermute | solution.py:27
  46.3 0.2 broadcast_select_fusion.2
  46.4 0.2 pad_maximum_fusion.1
  47.4 0.2 divide_subtract_fusion
  48.2 0.2 fusion.65
  48.4 0.4 maximum_multiply_fusion
  49.2 0.6 fusion.11
  49.8 0.2 fusion.21
  50.0 0.4 fusion.8
  50.4 1.0 %fusion.46 = f32[5,16,8,256]{3,1,2,0:T(8,128)S(1)} fusion(f32[5,16,8,256]{3,1,2,0:T(8,128)S(1)} %fusion.45, f32[1,16,8,256]{3,1,2,0:T(8,128)S(1)} %get-tuple-element.189, f32[1,16,8,256]{3,1,2,0:T(8,128)S(1)} %get-tuple-element.188, f32[1,16,8,256]{3,1,2,0:T(8,128)S(1)} %get-tuple-element.192, f32[5,16,9,256]{3,1,2,0:T(8,128)S(1)} %fusion.21, ...), kind=kLoop, calls=%fused_computation.84 | loop fusion | flops 3276800 | bytes 7209236 | tf_op jit(solution)/shard_map/div | solution.py:127
  51.5 1.3 %copy.147 = f32[2,16,8,256]{1,2,0,3:T(8,128)S(1)} copy(f32[2,16,8,256]{3,1,2,0:T(8,128)S(1)} %pad_maximum_fusion.14) | data formatting | bytes 524288 | tf_op jit(solution)/shard_map/stack | solution.py:140
  52.8 1.5 %reshape.492 = f32[128,1,512]{2,1,0:T(1,128)} reshape(f32[256,2,8,16]{3,2,1,0:T(8,128)S(1)} %bitcast.72) | data formatting | bytes 524288
  54.3 14.8 %all-to-all-start = ((f32[128,1,512]{2,1,0:T(1,128)}), f32[128,1,512]{2,1,0:T(1,128)S(1)}, u32[]{:S(2)}, u32[]{:S(2)}) async-start(f32[128,1,512]{2,1,0:T(1,128)} %reshape.492), calls=%async_computation | async-start | bytes 524288 | tf_op jit(solution)/shard_map/all_to_all | solution.py:188
  69.2 2.9 %fusion.58 = (f32[1024,64]{1,0:T(8,128)S(1)}, f32[1024,64]{1,0:T(8,128)}) fusion(s32[64]{0:T(128)S(1)} %iota_add_fusion), kind=kLoop, calls=%fused_computation.100 | loop fusion | flops 983040 | bytes 524544 | tf_op jit(solution)/shard_map/cos | solution.py:149
  72.1 1.2 %copy.152 = f32[5,16,8,256]{3,2,1,0:T(8,128)} copy(f32[5,16,8,256]{3,1,2,0:T(8,128)S(1)} %fusion.46) | data formatting | bytes 1310720
  73.3 12.1 %all-to-all-done = f32[128,1,512]{2,1,0:T(1,128)S(1)} async-done(((f32[128,1,512]{2,1,0:T(1,128)}), f32[128,1,512]{2,1,0:T(1,128)S(1)}, u32[]{:S(2)}, u32[]{:S(2)}) %all-to-all-start) | async-done | bytes 262176 | tf_op jit(solution)/shard_map/all_to_all | solution.py:188
  85.4 0.5 broadcast.523
  85.9 1.3 %reduce.24 = f32[128,512]{1,0:T(8,128)S(1)} reduce(f32[128,1,512]{2,1,0:T(1,128)S(1)} %all-to-all-done, f32[]{:T(128)} %broadcast.523), dimensions={1}, to_apply=%all_to_all.13.reduce_sub_computation | reduce | bytes 524292 | tf_op jit(solution)/shard_map/all_to_all | solution.py:188
  87.2 0.7 reshape.493
  87.9 0.3 copy-done.4
  88.2 3.5 %fusion.3 = f32[2,2,2,8,128]{4,3,2,1,0:T(8,128)S(1)} fusion(f32[2,16,128,8,2]{1,3,0,4,2:T(8,128)S(1)} %bitcast.71, f32[1024,64]{1,0:T(8,128)S(1)} %copy-done.4, f32[1024,64]{1,0:T(8,128)S(1)} %get-tuple-element.222), kind=kOutput, calls=%fused_computation.5 | convolution fusion | flops 100925440 | bytes 819200 | tf_op jit(solution)/shard_map/frsa,sc->arfc/dot_general | solution.py:186
  91.8 0.6 copy.181
  (78 shorter events, 4.0 us)
Async XLA Ops:
  0.6 4.8 %copy-start = (f32[5,16,8,256]{3,2,1,0:T(8,128)S(1)}, f32[5,16,8,256]{3,2,1,0:T(8,128)}, u32[]{:S(2)}) copy-start(f32[5,16,8,256]{3,2,1,0:T(8,128)} %param.31) | copy-start | bytes 1966084
  2.0 6.4 %collective-permute-start = (f32[5,16,1,256]{3,1,2,0:T(8,128)S(1)}, f32[5,16,1,256]{3,1,2,0:T(8,128)S(1)}, u32[]{:S(2)}, u32[]{:S(2)}) collective-permute-start(f32[5,16,1,256]{3,1,2,0:T(8,128)S(1)} %get-tuple-element.213), channel_id=1, source_target_pairs={{0,2},{2,4},{4,6},{6,8},{8,10},{10,12},{12,14},{14,16},{16,18},{18... | collective-permute-start | bytes 245768 | tf_op jit(solution)/shard_map/ppermute | solution.py:25
  5.1 3.9 %collective-permute-start.1 = (f32[5,16,1,256]{3,1,2,0:T(8,128)S(1)}, f32[5,16,1,256]{3,1,2,0:T(8,128)S(1)}, u32[]{:S(2)}, u32[]{:S(2)}) collective-permute-start(f32[5,16,1,256]{3,1,2,0:T(8,128)S(1)} %get-tuple-element.212), channel_id=1, source_target_pairs={{2,0},{4,2},{6,4},{8,6},{10,8},{12,10},{14,12},{16,14},{18,16},{20... | collective-permute-start | bytes 245768 | tf_op jit(solution)/shard_map/ppermute | solution.py:27
  7.0 1.3 %copy-start.6 = (s32[256]{0:T(256)S(1)}, s32[256]{0:T(256)}, u32[]{:S(2)}) copy-start(s32[256]{0:T(256)} %param.33) | copy-start | bytes 3076
  8.3 8.9 %copy-start.5 = (f32[5]{0:T(128)S(1)}, f32[5]{0:T(128)}, u32[]{:S(2)}) copy-start(f32[5]{0:T(128)} %constant.370.clone) | copy-start | bytes 64
  9.1 4.6 %collective-permute-start.2 = (f32[5,1,10,256]{3,1,2,0:T(1,128)S(1)}, f32[5,1,10,256]{3,1,2,0:T(1,128)S(1)}, u32[]{:S(2)}, u32[]{:S(2)}) collective-permute-start(f32[5,1,10,256]{3,1,2,0:T(1,128)S(1)} %get-tuple-element.200), channel_id=1, source_target_pairs={{0,1},{2,3},{4,5},{6,7},{8,9},{10,11},{12,13},{14,15},{16,17},{18,... | collective-permute-start | bytes 153608 | tf_op jit(solution)/shard_map/ppermute | solution.py:25
  12.3 4.9 %collective-permute-start.3 = (f32[5,1,10,256]{3,1,2,0:T(1,128)S(1)}, f32[5,1,10,256]{3,1,2,0:T(1,128)S(1)}, u32[]{:S(2)}, u32[]{:S(2)}) collective-permute-start(f32[5,1,10,256]{3,1,2,0:T(1,128)S(1)} %get-tuple-element.201), channel_id=1, source_target_pairs={{1,0},{3,2},{5,4},{7,6},{9,8},{11,10},{13,12},{15,14},{17,16},{19,... | collective-permute-start | bytes 153608 | tf_op jit(solution)/shard_map/ppermute | solution.py:27
  18.8 1.2 %copy-start.2 = (f32[5,16,8,258]{3,2,1,0:T(8,128)S(1)}, f32[5,16,8,258]{3,2,1,0:T(8,128)}, u32[]{:S(2)}) copy-start(f32[5,16,8,258]{3,2,1,0:T(8,128)} %pad_maximum_fusion.10) | copy-start | bytes 1981444
  20.9 1.2 %copy-start.1 = (f32[5,16,8,257]{3,2,1,0:T(8,128)S(1)}, f32[5,16,8,257]{3,2,1,0:T(8,128)}, u32[]{:S(2)}) copy-start(f32[5,16,8,257]{3,2,1,0:T(8,128)} %get-tuple-element.209) | copy-start | bytes 1973764
  22.6 1.1 %copy-start.3 = (f32[5,16,8,256]{3,2,1,0:T(8,128)S(1)}, f32[5,16,8,256]{3,2,1,0:T(8,128)}, u32[]{:S(2)}) copy-start(f32[5,16,8,256]{3,2,1,0:T(8,128)} %param.32) | copy-start | bytes 1966084
  24.7 9.6 %collective-permute-start.5 = (f32[5,16,1,256]{3,1,2,0:T(8,128)S(1)}, f32[5,16,1,256]{3,1,2,0:T(8,128)S(1)}, u32[]{:S(2)}, u32[]{:S(2)}) collective-permute-start(f32[5,16,1,256]{3,1,2,0:T(8,128)S(1)} %get-tuple-element.207), channel_id=1, source_target_pairs={{2,0},{4,2},{6,4},{8,6},{10,8},{12,10},{14,12},{16,14},{18,16},{20... | collective-permute-start | bytes 245768 | tf_op jit(solution)/shard_map/ppermute | solution.py:27
  33.3 6.3 %collective-permute-start.4 = (f32[5,16,1,256]{3,1,2,0:T(8,128)S(1)}, f32[5,16,1,256]{3,1,2,0:T(8,128)S(1)}, u32[]{:S(2)}, u32[]{:S(2)}) collective-permute-start(f32[5,16,1,256]{3,1,2,0:T(8,128)S(1)} %get-tuple-element.206), channel_id=1, source_target_pairs={{0,2},{2,4},{4,6},{6,8},{8,10},{10,12},{12,14},{14,16},{16,18},{18... | collective-permute-start | bytes 245768 | tf_op jit(solution)/shard_map/ppermute | solution.py:25
  39.8 2.9 %collective-permute-start.6 = (f32[5,1,10,256]{3,1,2,0:T(1,128)S(1)}, f32[5,1,10,256]{3,1,2,0:T(1,128)S(1)}, u32[]{:S(2)}, u32[]{:S(2)}) collective-permute-start(f32[5,1,10,256]{3,1,2,0:T(1,128)S(1)} %get-tuple-element.198), channel_id=1, source_target_pairs={{0,1},{2,3},{4,5},{6,7},{8,9},{10,11},{12,13},{14,15},{16,17},{18,... | collective-permute-start | bytes 153608 | tf_op jit(solution)/shard_map/ppermute | solution.py:25
  41.1 5.2 %collective-permute-start.7 = (f32[5,1,10,256]{3,1,2,0:T(1,128)S(1)}, f32[5,1,10,256]{3,1,2,0:T(1,128)S(1)}, u32[]{:S(2)}, u32[]{:S(2)}) collective-permute-start(f32[5,1,10,256]{3,1,2,0:T(1,128)S(1)} %get-tuple-element.199), channel_id=1, source_target_pairs={{1,0},{3,2},{5,4},{7,6},{9,8},{11,10},{13,12},{15,14},{17,16},{19,... | collective-permute-start | bytes 153608 | tf_op jit(solution)/shard_map/ppermute | solution.py:27
  54.3 31.1 %all-to-all-start = ((f32[128,1,512]{2,1,0:T(1,128)}), f32[128,1,512]{2,1,0:T(1,128)S(1)}, u32[]{:S(2)}, u32[]{:S(2)}) async-start(f32[128,1,512]{2,1,0:T(1,128)} %reshape.492), calls=%async_computation | async-start | bytes 524288 | tf_op jit(solution)/shard_map/all_to_all | solution.py:188
  87.2 1.0 %copy-start.4 = (f32[1024,64]{1,0:T(8,128)S(1)}, f32[1024,64]{1,0:T(8,128)}, u32[]{:S(2)}) copy-start(f32[1024,64]{1,0:T(8,128)} %get-tuple-element.223) | copy-start | bytes 786436
where the time goes:
time: 92.8 us; the launch traced here: 92.4 us
  starting transfers between devices  34.2 us (37%)
  waiting for transfers between devices  25.8 us (28%)
  other arithmetic  16.1 us (17%)
  local copies, waits for them, and re-layouts  11.5 us (12%)
  matrix products  3.54 us (4%)
  between operations  1.26 us (1%)
    all_to_all x1, starting transfers between devices, per_device(): lax.all_to_all(fields, 'theta', split_axis=3, concat_axis=2, tiled=True)  14.8 us
    all_to_all x1, waiting for transfers between devices, per_device(): lax.all_to_all(fields, 'theta', split_axis=3, concat_axis=2, tiled=True)  12.1 us
    ppermute x4, starting transfers between devices, extended_2(): lax.ppermute(head, axis, [((i + 1) % count, i) for i in range(ends)])  11.7 us
    ppermute x4, waiting for transfers between devices, extended_2(): lax.ppermute(head, axis, [((i + 1) % count, i) for i in range(ends)])  8.3 us
    unnamed x20, local copies, waits for them, and re-layouts  8.04 us
    ppermute x4, starting transfers between devices, extended_2(): lax.ppermute(tail, axis, [(i, (i + 1) % count) for i in range(ends)])  7.6 us
    ppermute x4, waiting for transfers between devices, extended_2(): lax.ppermute(tail, axis, [(i, (i + 1) % count) for i in range(ends)])  5.4 us
    dot_general x1, matrix products, per_device(): jnp.einsum('frsa,sc->arfc', lax.all_to_all(fields, 'theta', split_axis=3,...  3.54 us
  transfers between devices with their start and end apart: 9, of which 6 were waited for; matrix products, arithmetic and copies ran while one was open for 8% of the time, Pallas kernels for 0%

commit v1 on v0

v1 whole, which is shorter than its diff:
```python
import math

import jax
import jax.numpy as jnp
import numpy as np
from jax import lax
from jax.experimental import pallas as pl
from jax.experimental.pallas import tpu as pltpu
from jax.sharding import PartitionSpec as P

MODES = 64
GAMMA = 1.4
KAPPA = 2.0

BAND = 16
SECTOR = 8
AXIAL = 256
F32 = jnp.float32
ALL = range(5)


def primitives(q):
    inverse = 1.0 / q[0]
    ux, ur, ut = q[1] * inverse, q[2] * inverse, q[3] * inverse
    pressure = (GAMMA - 1.0) * (q[4] - 0.5 * (q[1] * ux + q[2] * ur + q[3] * ut))
    sound = jnp.sqrt(GAMMA * pressure * inverse)
    return ux, ur, ut, pressure, sound


def flux(q, prim, d):
    u, pressure = prim[d - 1], prim[3]
    f = [q[d], q[1] * u, q[2] * u, q[3] * u, (q[4] + pressure) * u]
    f[d] = f[d] + pressure
    return f, jnp.abs(u) + prim[4]


def face(left_q, left_flux, right_q, right_flux):
    (fl, sl), (fr, sr) = left_flux, right_flux
    fastest = jnp.maximum(sl, sr)
    return [(fl[v] + fr[v]) - fastest * (right_q[v] - left_q[v]) for v in ALL]


def roll(x, shift, axis):
    return pltpu.roll(x, shift % x.shape[axis], axis)


def axial_difference(q, prim, lane):
    f, speed = flux(q, prim, 1)
    axis = q[0].ndim - 1
    qn = [roll(x, -1, axis) for x in q]
    fn = [qn[1]] + [roll(f[v], -1, axis) for v in range(1, 5)]
    right = face(q, (f, speed), qn, (fn, roll(speed, -1, axis)))
    ends = [2.0 * x for x in f]
    right = [jnp.where(lane == AXIAL - 1, e, x) for e, x in zip(ends, right)]
    left = [jnp.where(lane == 0, e, roll(x, 1, axis)) for e, x in zip(ends, right)]
    return [a - b for a, b in zip(right, left)]


def advance(q, prim, half_source, axial, radial, swirl, inv_r, inv_h, spin_r, bladed, rotor):
    ux, ur, ut, pressure, sound = prim
    half_r = 0.5 * inv_r
    force = bladed * (q[0] * (ut - rotor * spin_r))
    gains = [
        None,
        None,
        half_r * (q[3] * ut + pressure),
        -force - half_r * (q[2] * ut),
        -ut * force,
    ]
    rate = jnp.abs(ux) + jnp.abs(ur) + jnp.abs(ut) * inv_h + sound * (2.0 + inv_h)
    weight = 1.0 / (rate + 7.5)
    out = []
    for v in ALL:
        total = half_source[v] - 0.25 * axial[v] - radial[v] - swirl[v]
        if gains[v] is not None:
            total = total + gains[v]
        out.append((rate * q[v] + total) * weight)
    return out


def geometry_table(rows, circle):
    mean = circle / (2.0 * math.pi)
    row = np.arange(-1, rows + 1, dtype=np.float64)
    radius = mean * (0.8 + 0.4 * (row + 0.5) / rows)
    inner = mean * (0.8 + 0.4 * row / rows)
    outer = mean * (0.8 + 0.4 * (row + 1.0) / rows)
    spacing = radius * (2.0 * math.pi / circle)
    spin = radius / (1.2 * mean)
    table = np.stack(
        [0.25 * outer / radius, 0.25 * inner / radius, 0.25 / spacing, 1.0 / radius, 1.0 / spacing, spin]
    )
    return table.astype(np.float32)


def pack_kernel(q_ref, qp_ref, rad_ref, other_ref, core_ref, odiag_ref, cdiag_ref):
    odd = lax.axis_index("theta") % 2 == 1
    band = lax.axis_index("rad")
    near = jnp.where(band == 0, BAND - 1, 0)
    far = jnp.where(band == 0, BAND - 2, 1)
    for v in ALL:
        rad_ref[v, 0] = q_ref[v, near]
        rad_ref[v, 1] = q_ref[v, far]
        rad_ref[v, 2] = qp_ref[v, near]
        first, second = q_ref[v, :, 0, :], q_ref[v, :, 1, :]
        last, before = q_ref[v, :, SECTOR - 1, :], q_ref[v, :, SECTOR - 2, :]
        pfirst, plast = qp_ref[v, :, 0, :], qp_ref[v, :, SECTOR - 1, :]
        for ref, flip in ((other_ref, odd), (core_ref, jnp.logical_not(odd))):
            ref[v, 0:16] = jnp.where(flip, last, first)
            ref[v, 16:32] = jnp.where(flip, before, second)
            ref[v, 32:48] = jnp.where(flip, plast, pfirst)
        edge = q_ref[v, near]
        head, tail = edge[0:1], edge[SECTOR - 1 : SECTOR]
        odiag_ref[v : v + 1] = jnp.where(odd, tail, head)
        cdiag_ref[v : v + 1] = jnp.where(odd, head, tail)
    odiag_ref[5:8] = jnp.zeros((3, AXIAL), F32)
    cdiag_ref[5:8] = jnp.zeros((3, AXIAL), F32)


def flow_kernel(
    total_rows,
    circle,
    table_ref,
    blade_ref,
    q_ref,
    qp_ref,
    rad_ref,
    other_ref,
    core_ref,
    odiag_ref,
    cdiag_ref,
    flow_ref,
    send_ref,
    p0,
    p1,
    hs,
    ce,
    h,
    h2,
    fields,
):
    odd = lax.axis_index("theta") % 2 == 1
    band = lax.axis_index("rad")
    first_row = band * BAND
    low = band == 0
    blade = blade_ref[...]
    bladed_row = (blade > 0).astype(F32)
    rotor_row = (blade == 1).astype(F32)
    bladed = jnp.broadcast_to(bladed_row, (SECTOR, AXIAL))
    rotor = jnp.broadcast_to(rotor_row, (SECTOR, AXIAL))
    lane = lax.broadcasted_iota(jnp.int32, (SECTOR, AXIAL), 1)
    sub = lax.broadcasted_iota(jnp.int32, (SECTOR, AXIAL), 0)
    mirror = (1.0, 1.0, -1.0, 1.0, 1.0)

    near_at = jnp.where(low, BAND + 2, 1)
    far_at = jnp.where(low, BAND + 3, 0)
    wall_at = jnp.where(low, 1, BAND + 2)
    wall_row = jnp.where(low, 0, BAND - 1)
    for v in ALL:
        p0[v, 2 : BAND + 2] = q_ref[v]
        hs[v, 1 : BAND + 1] = 10.0 * q_ref[v] - 2.5 * qp_ref[v]
        p0[v, near_at] = rad_ref[v, 0]
        p0[v, far_at] = rad_ref[v, 1]
        p0[v, wall_at] = mirror[v] * q_ref[v, wall_row]
        hs[v, near_at - 1] = 10.0 * rad_ref[v, 0] - 2.5 * rad_ref[v, 2]

    rows16 = lax.broadcasted_iota(jnp.int32, (BAND, AXIAL), 0) + first_row
    lane16 = lax.broadcasted_iota(jnp.int32, (BAND, AXIAL), 1)
    rowf = rows16.astype(F32)
    mean = circle / (2.0 * math.pi)
    radius = mean * (0.8 + 0.4 * (rowf + 0.5) / total_rows)
    inner = mean * (0.8 + 0.4 * rowf / total_rows)
    outer = mean * (0.8 + 0.4 * (rowf + 1.0) / total_rows)
    inv_r = 1.0 / radius
    inv_h = inv_r * mean
    spin_r = radius * (1.0 / (1.2 * mean))
    corner_at = jnp.where(low, BAND, -1) + 8
    bladed16 = jnp.broadcast_to(bladed_row, (BAND, AXIAL))
    rotor16 = jnp.broadcast_to(rotor_row, (BAND, AXIAL))
    columns = []
    for side in (0, 1):
        use_core = odd if side == 0 else jnp.logical_not(odd)
        edge = 0 if side == 0 else SECTOR - 1

        def pick(lo, hi):
            return [jnp.where(use_core, core_ref[v, lo:hi], other_ref[v, lo:hi]) for v in ALL]

        near, far, prev = pick(0, 16), pick(16, 32), pick(32, 48)
        corner = [jnp.where(use_core, cdiag_ref[v : v + 1], odiag_ref[v : v + 1]) for v in ALL]
        own = [q_ref[v, :, edge, :] for v in ALL]
        own_corner = [rad_ref[v, 0, edge : edge + 1, :] for v in ALL]

        def swirl_face(halo, own):
            a, b = flux(halo, primitives(halo), 3), flux(own, primitives(own), 3)
            return face(halo, a, own, b) if side == 0 else face(own, b, halo, a)

        near_prim = primitives(near)
        nf = flux(near, near_prim, 3)
        of = flux(own, primitives(own), 3)
        ff = flux(far, primitives(far), 3)
        if side == 0:
            inside, outside = face(near, nf, own, of), face(far, ff, near, nf)
            swirl = [a - b for a, b in zip(inside, outside)]
        else:
            inside, outside = face(own, of, near, nf), face(near, nf, far, ff)
            swirl = [a - b for a, b in zip(outside, inside)]
        corner_face = swirl_face(corner, own_corner)
        for v in ALL:
            h[v, side, 8:24] = inside[v]
            h[v, side, pl.ds(corner_at, 1)] = corner_face[v]
            ce[v, side, 8:24] = near[v]
            ce[v, side, 7:8] = jnp.where(low, mirror[v] * near[v][0:1], corner[v])
            ce[v, side, 24:25] = jnp.where(low, corner[v], mirror[v] * near[v][BAND - 1 : BAND])
        below = [ce[v, side, 7:23] for v in ALL]
        above = [ce[v, side, 9:25] for v in ALL]
        rf = flux(near, near_prim, 2)
        g_in = face(below, flux(below, primitives(below), 2), near, rf)
        g_out = face(near, rf, above, flux(above, primitives(above), 2))
        half_source = [10.0 * near[v] - 2.5 * prev[v] for v in ALL]
        radial = [(0.25 * inv_r) * (outer * g_out[v] - inner * g_in[v]) for v in ALL]
        columns.append(
            advance(
                near,
                near_prim,
                half_source,
                axial_difference(near, near_prim, lane16),
                radial,
                [(0.25 * inv_h) * x for x in swirl],
                inv_r,
                inv_h,
                spin_r,
                bladed16,
                rotor16,
            )
        )

    def row(j, q, prim, g_in, g_out, faces):
        f = flux(q, prim, 3)
        qn = [roll(x, -1, 0) for x in q]
        fn = [qn[3]] + [roll(f[0][v], -1, 0) for v in range(1, 5)]
        between = face(q, f, qn, (fn, roll(f[1], -1, 0)))
        swirl = []
        at = j + 8
        g = first_row + j + 1
        a_out, a_in, a_h = table_ref[0, g], table_ref[1, g], table_ref[2, g]
        for v in ALL:
            right = jnp.where(sub == SECTOR - 1, faces[v, 1, pl.ds(at, 1)], between[v])
            left = jnp.where(sub == 0, faces[v, 0, pl.ds(at, 1)], roll(between[v], 1, 0))
            swirl.append(a_h * (right - left))
        radial = [a_out * g_out[v] - a_in * g_in[v] for v in ALL]
        return advance(
            q,
            prim,
            [hs[v, j + 1] for v in ALL],
            axial_difference(q, prim, lane),
            radial,
            swirl,
            table_ref[3, g],
            table_ref[4, g],
            table_ref[5, g],
            bladed,
            rotor,
        )

    def sweep(source, offset, start, count, faces, store):
        def load(j):
            q = [source[v, j + offset] for v in ALL]
            return q, primitives(q)

        below, below_prim = load(start - 1)
        q, prim = load(start)
        g_in = face(below, flux(below, below_prim, 2), q, flux(q, prim, 2))

        def body(i, carry):
            q, prim, g_in = carry
            j = start + i
            above, above_prim = load(j + 1)
            g_out = face(q, flux(q, prim, 2), above, flux(above, above_prim, 2))
            store(j, row(j, q, prim, g_in, g_out, faces))
            return above, above_prim, g_out

        lax.fori_loop(0, count, body, (q, prim, g_in))

    def keep(j, q):
        for v in ALL:
            p1[v, j + 1] = q[v]

    sweep(p0, 2, jnp.where(low, 0, -1), BAND + 1, h, keep)
    for v in ALL:
        p1[v, wall_at - 1] = mirror[v] * p1[v, wall_row + 1]

    for side in (0, 1):
        edge = 0 if side == 0 else SECTOR - 1
        halo = columns[side]
        own = [p1[v, 1 : BAND + 1, edge, :] for v in ALL]
        a, b = flux(halo, primitives(halo), 3), flux(own, primitives(own), 3)
        faces = face(halo, a, own, b) if side == 0 else face(own, b, halo, a)
        for v in ALL:
            h2[v, side, 8:24] = faces[v]

    def finish(j, q):
        for v in ALL:
            flow_ref[v, j] = q[v]
        ux, _, _, pressure, _ = primitives(q)
        fields[0, j] = pressure
        fields[1, j] = ux

    sweep(p1, 1, 0, BAND, h2, finish)
    for f in (0, 1):
        turned = fields[f].reshape(BAND * SECTOR, AXIAL).T
        send_ref[pl.ds(f, AXIAL, stride=2), :] = turned


def mode_kernel(got_ref, basis_ref, out_ref, turned):
    sectors = got_ref.shape[0] // 4
    parts = []
    for e in (0, 1):
        for f in (0, 1):
            n = 2 * e + f
            turned[n] = got_ref[pl.ds(n, sectors, stride=4), :].T
            parts.append(
                jnp.concatenate([turned[n, pl.ds(m, BAND, stride=SECTOR), :] for m in range(SECTOR)], axis=1)
            )
    product = jnp.dot(
        jnp.concatenate(parts, axis=0), basis_ref[...], precision=lax.Precision.HIGHEST, preferred_element_type=F32
    )
    for e in (0, 1):
        for f in (0, 1):
            n = 2 * e + f
            out_ref[e, :, 2 * MODES * f : 2 * MODES * (f + 1)] = product[BAND * n : BAND * (n + 1)]


def mode_basis(sectors):
    circle = sectors * SECTOR
    cell = (np.arange(SECTOR)[:, None] + SECTOR * np.arange(sectors)[None, :]).reshape(-1)
    phase = (cell[:, None] * np.arange(1, MODES + 1)[None, :] % circle) * (2.0 * np.pi / circle)
    return (np.concatenate([np.cos(phase), -np.sin(phase)], axis=1) / np.sqrt(circle)).astype(np.float32)


def shaped(*shape):
    return jax.ShapeDtypeStruct(shape, F32)


def vmem():
    return pl.BlockSpec(memory_space=pltpu.VMEM)


def per_device(q_level, q_prev, blade_row):
    sectors = lax.axis_size("theta")
    bands = lax.axis_size("rad")
    circle = sectors * SECTOR
    core = [(t, t ^ 1) for t in range(sectors)]
    other = [(t, (((t + 1) ^ 1) - 1) % sectors) for t in range(sectors)]
    diagonal = lambda pairs: [(bands * a + b, bands * c + 1 - b) for a, c in pairs for b in range(bands)]

    rad_out, other_out, core_out, odiag_out, cdiag_out = pl.pallas_call(
        pack_kernel,
        out_shape=[
            shaped(5, 3, SECTOR, AXIAL),
            shaped(5, 48, AXIAL),
            shaped(5, 48, AXIAL),
            shaped(8, AXIAL),
            shaped(8, AXIAL),
        ],
        in_specs=[vmem()] * 2,
        out_specs=[vmem()] * 5,
    )(q_level, q_prev)
    other_in = lax.ppermute(other_out, "theta", other)
    odiag_in = lax.ppermute(odiag_out, ("theta", "rad"), diagonal(other))
    rad_in = lax.ppermute(rad_out, "rad", [(0, 1), (1, 0)])
    cdiag_in = lax.ppermute(cdiag_out, ("theta", "rad"), diagonal(core))
    core_in = lax.ppermute(core_out, "theta", core)

    def kernel(*refs):
        flow_kernel(bands * BAND, circle, *refs)

    flow_state, send = pl.pallas_call(
        kernel,
        out_shape=[shaped(5, BAND, SECTOR, AXIAL), shaped(2 * AXIAL, BAND * SECTOR)],
        in_specs=[pl.BlockSpec(memory_space=pltpu.SMEM)] + [vmem()] * 8,
        out_specs=[vmem()] * 2,
        scratch_shapes=[
            pltpu.VMEM((5, BAND + 4, SECTOR, AXIAL), F32),
            pltpu.VMEM((5, BAND + 2, SECTOR, AXIAL), F32),
            pltpu.VMEM((5, BAND + 2, SECTOR, AXIAL), F32),
            pltpu.VMEM((5, 2, 32, AXIAL), F32),
            pltpu.VMEM((5, 2, 32, AXIAL), F32),
            pltpu.VMEM((5, 2, 32, AXIAL), F32),
            pltpu.VMEM((2, BAND, SECTOR, AXIAL), F32),
        ],
    )(
        jnp.asarray(geometry_table(bands * BAND, circle)),
        blade_row.reshape(1, AXIAL),
        q_level,
        q_prev,
        rad_in,
        other_in,
        core_in,
        odiag_in,
        cdiag_in,
    )
    got = lax.all_to_all(send.reshape(sectors, 4, 128), "theta", split_axis=0, concat_axis=0, tiled=True)
    spectra = pl.pallas_call(
        mode_kernel,
        out_shape=shaped(2, BAND, 4 * MODES),
        in_specs=[vmem()] * 2,
        out_specs=vmem(),
        scratch_shapes=[pltpu.VMEM((4, BAND * SECTOR, sectors), F32)],
    )(got.reshape(4 * sectors, 128), jnp.asarray(mode_basis(sectors)))
    return flow_state, spectra


def solution(mesh):
    in_specs = (P(None, "rad", "theta", None), P(None, "rad", "theta", None), P())
    out_specs = (P(None, "rad", "theta", None), P("theta", "rad", None))
    return jax.shard_map(per_device, mesh=mesh, in_specs=in_specs, out_specs=out_specs, check_vma=False)
```

time: 92.8 us -> 59.1 us (0.64)
  blocking collectives: 0 us -> 26 us
  waiting for transfers between devices: 25.8 us -> 4.04 us
  starting transfers between devices: 34.2 us -> 13.3 us
  other arithmetic: 16.1 us -> 0 us
  Pallas kernels: 0 us -> 14.1 us
  local copies, waits for them, and re-layouts: 11.5 us -> 0.81 us
  matrix products: 3.54 us -> 0 us
    all_to_all x0 -> x1, blocking collectives: none -> 26 us  [per_device(): lax.all_to_all(send.reshape(sectors, 4, 128), 'theta', split_axis=0, conc...]
    all_to_all x1 -> x0, starting transfers between devices: 14.8 us -> none  [per_device(): lax.all_to_all(fields, 'theta', split_axis=3, concat_axis=2, tiled=True)]
    pallas_call x0 -> x3, Pallas kernels: none -> 14.1 us  [the longest x1 9.52 us: per_device(): pl.pallas_call(kernel, out_shape=[shaped(5, BAND, SECTOR, AXIAL), shaped(...]
    all_to_all x1 -> x0, waiting for transfers between devices: 12.1 us -> none  [per_device(): lax.all_to_all(fields, 'theta', split_axis=3, concat_axis=2, tiled=True)]
    ppermute x8 -> x5, waiting for transfers between devices: 13.7 us -> 4.04 us  [the longest x1 3 us: per_device(): odiag_in = lax.ppermute(odiag_out, ('theta', 'rad'), diagonal(other))]
    unnamed x20 -> x12, local copies, waits for them, and re-layouts: 8.04 us -> 0.81 us
    ppermute x8 -> x5, starting transfers between devices: 19.3 us -> 13.3 us  [the longest x1 8.6 us: per_device(): core_in = lax.ppermute(core_out, 'theta', core)]
    dot_general x1 -> x0, matrix products: 3.54 us -> none  [per_device(): jnp.einsum('frsa,sc->arfc', lax.all_to_all(fields, 'theta', split_axis=3,...]
  transfers between devices with their start and end apart: 9 -> 5, of which waited for: 6 -> 2; matrix products, arithmetic and copies ran while one was open for 8% -> 0% of each run, Pallas kernels for 0% -> 0%
where the time goes in v1:
time: 59.1 us; the launch traced here: 58.9 us
  blocking collectives  26 us (44%)
  Pallas kernels  14.1 us (24%)
  starting transfers between devices  13.3 us (23%)
  waiting for transfers between devices  4.04 us (7%)
  local copies, waits for them, and re-layouts  0.81 us (1%)
  between operations  0.67 us (1%)
    all_to_all x1, blocking collectives, per_device(): lax.all_to_all(send.reshape(sectors, 4, 128), 'theta', split_axis=0, conc...  26 us
    pallas_call x1, Pallas kernels, per_device(): pl.pallas_call(kernel, out_shape=[shaped(5, BAND, SECTOR, AXIAL), shaped(...  9.52 us
    ppermute x1, starting transfers between devices, per_device(): core_in = lax.ppermute(core_out, 'theta', core)  8.6 us
    ppermute x1, starting transfers between devices, per_device(): other_in = lax.ppermute(other_out, 'theta', other)  3.03 us
    ppermute x1, waiting for transfers between devices, per_device(): odiag_in = lax.ppermute(odiag_out, ('theta', 'rad'), diagonal(other))  3 us
    pallas_call x1, Pallas kernels, per_device(): pl.pallas_call(pack_kernel, out_shape=[shaped(5, 3, SECTOR, AXIAL), shape...  2.3 us
    pallas_call x1, Pallas kernels, per_device(): pl.pallas_call(mode_kernel, out_shape=shaped(2, BAND, 4 * MODES), in_spec...  2.26 us
    ppermute x1, starting transfers between devices, per_device(): cdiag_in = lax.ppermute(cdiag_out, ('theta', 'rad'), diagonal(core))  1.29 us
  transfers between devices with their start and end apart: 5, of which 2 were waited for; matrix products, arithmetic and copies ran while one was open for 0% of the time, Pallas kernels for 0%

profile of v1, /device:TPU:1, one launch (start us, length us, event | category | flops | bytes accessed | tf_op | source)
XLA Modules:
  0.0 58.9 jit_solution(3102614814499274705)
XLA Ops:
  0.6 2.3 %shard_map.68 = (f32[5,3,8,256]{3,2,1,0:T(8,128)}, f32[5,48,256]{2,1,0:T(8,128)}, f32[5,48,256]{2,1,0:T(8,128)}, f32[8,256]{1,0:T(8,128)}, f32[8,256]{1,0:T(8,128)}) custom-call(f32[5,16,8,256]{3,2,1,0:T(8,128)} %refs_2_.1, f32[5,16,8,256]{3,2,1,0:T(8,128)} %refs_3_.1), custom_call_target="tpu_custom_call" | custom-call | tf_op jit(solution)/shard_map/pallas_call | solution.py:355
  2.9 0.0 copy-start.5
  2.9 3.0 %collective-permute-start.1 = (f32[5,48,256]{2,1,0:T(8,128)}, f32[5,48,256]{2,1,0:T(8,128)S(1)}, u32[]{:S(2)}, u32[]{:S(2)}) collective-permute-start(f32[5,48,256]{2,1,0:T(8,128)} %get-tuple-element.10), channel_id=1, source_target_pairs={{0,254},{2,4},{4,2},{6,8},{8,6},{10,12},{12,10},{14,16},{16,14},{1... | collective-permute-start | bytes 737288 | tf_op jit(solution)/shard_map/ppermute | solution.py:367
  6.0 8.6 %collective-permute-start.2 = (f32[5,48,256]{2,1,0:T(8,128)}, f32[5,48,256]{2,1,0:T(8,128)S(1)}, u32[]{:S(2)}, u32[]{:S(2)}) collective-permute-start(f32[5,48,256]{2,1,0:T(8,128)} %get-tuple-element.11), channel_id=1, source_target_pairs={{0,2},{2,0},{4,6},{6,4},{8,10},{10,8},{12,14},{14,12},{16,18},{18,... | collective-permute-start | bytes 737288 | tf_op jit(solution)/shard_map/ppermute | solution.py:371
  14.6 0.4 collective-permute-start
  15.0 0.0 collective-permute-start.3
  15.0 0.0 copy-done.5
  15.0 1.3 %collective-permute-start.4 = (f32[8,256]{1,0:T(8,128)S(1)}, f32[8,256]{1,0:T(8,128)S(1)}, u32[]{:S(2)}, u32[]{:S(2)}) collective-permute-start(f32[8,256]{1,0:T(8,128)S(1)} %copy-done.5), channel_id=1, source_target_pairs={{0,3},{1,2},{2,1},{3,0},{4,7},{5,6},{6,5},{7,4},{8,11},{9,10},{10,... | collective-permute-start | bytes 24584 | tf_op jit(solution)/shard_map/ppermute | solution.py:370
  16.2 3.0 %collective-permute-done.3.refs_7_ = f32[8,256]{1,0:T(8,128)S(1)} collective-permute-done((f32[8,256]{1,0:T(8,128)}, f32[8,256]{1,0:T(8,128)S(1)}, u32[]{:S(2)}, u32[]{:S(2)}) %collective-permute-start.3) | collective-permute-done | bytes 8224 | tf_op jit(solution)/shard_map/ppermute | solution.py:368
  19.2 0.0 copy-start.3
  19.3 1.0 %collective-permute-done.4.refs_8_ = f32[8,256]{1,0:T(8,128)S(1)} collective-permute-done((f32[8,256]{1,0:T(8,128)S(1)}, f32[8,256]{1,0:T(8,128)S(1)}, u32[]{:S(2)}, u32[]{:S(2)}) %collective-permute-start.4) | collective-permute-done | bytes 8224 | tf_op jit(solution)/shard_map/ppermute | solution.py:370
  20.3 0.0 copy-start.4
  20.3 0.0 collective-permute-done.refs_4_
  20.3 0.0 copy-start.2
  20.3 0.0 collective-permute-done.1.refs_5_
  20.3 0.0 copy-start
  20.3 0.0 collective-permute-done.2.refs_6_
  20.3 0.0 copy-start.1
  20.3 0.0 copy-done.3
  20.3 0.5 copy-done.4
  20.9 0.1 copy-done.2
  20.9 0.1 copy-done
  21.0 0.1 copy-done.1
  21.1 9.5 %shard_map.69 = (f32[5,16,8,256]{3,2,1,0:T(8,128)}, f32[512,128]{1,0:T(8,128)}) custom-call(f32[6,34]{1,0:T(8,128)} %constant.4.clone.refs_0_, s32[1,256]{1,0:T(1,128)} %bitcast.5, f32[5,16,8,256]{3,2,1,0:T(8,128)} %refs_2_.1, f32[5,16,8,256]{3,2,1,0:T(8,128)} %refs_3_.1, f32[5,3,8,256]{3,2,1,0:T(8,128)} %copy-done.2, f32[5,48,256]{2,1,0:T(8,128)} %copy-done, ...), custom_call_target="tpu_custom_call" | custom-call | tf_op jit(solution)/shard_map/pallas_call | solution.py:376
  30.7 26.0 %all_to_all.5 = f32[128,4,128]{2,1,0:T(4,128)} all-to-all(f32[128,4,128]{2,1,0:T(4,128)} %bitcast.4), channel_id=1, replica_groups=mesh['theta'=128,'rad'=2] {'theta'}, dimensions={0} | all-to-all | bytes 524288 | tf_op jit(solution)/shard_map/all_to_all | solution.py:401
  56.6 2.3 %shard_map.70 = f32[2,16,256]{2,1,0:T(8,128)} custom-call(f32[512,128]{1,0:T(8,128)} %bitcast.3, f32[1024,128]{1,0:T(8,128)} %constant.5.clone.basis_ref), custom_call_target="tpu_custom_call" | custom-call | tf_op jit(solution)/shard_map/pallas_call | solution.py:402
Async XLA Ops:
  2.9 12.0 %copy-start.5 = (f32[8,256]{1,0:T(8,128)S(1)}, f32[8,256]{1,0:T(8,128)}, u32[]{:S(2)}) copy-start(f32[8,256]{1,0:T(8,128)} %get-tuple-element.13) | copy-start | bytes 24580
  2.9 17.4 %collective-permute-start.1 = (f32[5,48,256]{2,1,0:T(8,128)}, f32[5,48,256]{2,1,0:T(8,128)S(1)}, u32[]{:S(2)}, u32[]{:S(2)}) collective-permute-start(f32[5,48,256]{2,1,0:T(8,128)} %get-tuple-element.10), channel_id=1, source_target_pairs={{0,254},{2,4},{4,2},{6,8},{8,6},{10,12},{12,10},{14,16},{16,14},{1... | collective-permute-start | bytes 737288 | tf_op jit(solution)/shard_map/ppermute | solution.py:367
  6.0 14.4 %collective-permute-start.2 = (f32[5,48,256]{2,1,0:T(8,128)}, f32[5,48,256]{2,1,0:T(8,128)S(1)}, u32[]{:S(2)}, u32[]{:S(2)}) collective-permute-start(f32[5,48,256]{2,1,0:T(8,128)} %get-tuple-element.11), channel_id=1, source_target_pairs={{0,2},{2,0},{4,6},{6,4},{8,10},{10,8},{12,14},{14,12},{16,18},{18,... | collective-permute-start | bytes 737288 | tf_op jit(solution)/shard_map/ppermute | solution.py:371
  14.6 5.7 %collective-permute-start = (f32[5,3,8,256]{3,2,1,0:T(8,128)}, f32[5,3,8,256]{3,2,1,0:T(8,128)S(1)}, u32[]{:S(2)}, u32[]{:S(2)}) collective-permute-start(f32[5,3,8,256]{3,2,1,0:T(8,128)} %get-tuple-element.9), channel_id=1, source_target_pairs={{0,1},{1,0},{2,3},{3,2},{4,5},{5,4},{6,7},{7,6},{8,9},{9,8},{10,11... | collective-permute-start | bytes 368648 | tf_op jit(solution)/shard_map/ppermute | solution.py:369
  15.0 4.3 %collective-permute-start.3 = (f32[8,256]{1,0:T(8,128)}, f32[8,256]{1,0:T(8,128)S(1)}, u32[]{:S(2)}, u32[]{:S(2)}) collective-permute-start(f32[8,256]{1,0:T(8,128)} %get-tuple-element.12), channel_id=1, source_target_pairs={{0,255},{1,254},{2,5},{3,4},{4,3},{5,2},{6,9},{7,8},{8,7},{9,6},{1... | collective-permute-start | bytes 24584 | tf_op jit(solution)/shard_map/ppermute | solution.py:368
  15.0 5.3 %collective-permute-start.4 = (f32[8,256]{1,0:T(8,128)S(1)}, f32[8,256]{1,0:T(8,128)S(1)}, u32[]{:S(2)}, u32[]{:S(2)}) collective-permute-start(f32[8,256]{1,0:T(8,128)S(1)} %copy-done.5), channel_id=1, source_target_pairs={{0,3},{1,2},{2,1},{3,0},{4,7},{5,6},{6,5},{7,4},{8,11},{9,10},{10,... | collective-permute-start | bytes 24584 | tf_op jit(solution)/shard_map/ppermute | solution.py:370
  19.2 1.1 %copy-start.3 = (f32[8,256]{1,0:T(8,128)}, f32[8,256]{1,0:T(8,128)S(1)}, u32[]{:S(2)}) copy-start(f32[8,256]{1,0:T(8,128)S(1)} %collective-permute-done.3.refs_7_) | copy-start | bytes 24580
  20.3 0.6 %copy-start.4 = (f32[8,256]{1,0:T(8,128)}, f32[8,256]{1,0:T(8,128)S(1)}, u32[]{:S(2)}) copy-start(f32[8,256]{1,0:T(8,128)S(1)} %collective-permute-done.4.refs_8_) | copy-start | bytes 24580
  20.3 0.7 %copy-start.2 = (f32[5,3,8,256]{3,2,1,0:T(8,128)}, f32[5,3,8,256]{3,2,1,0:T(8,128)S(1)}, u32[]{:S(2)}) copy-start(f32[5,3,8,256]{3,2,1,0:T(8,128)S(1)} %collective-permute-done.refs_4_) | copy-start | bytes 368644
  20.3 0.7 %copy-start = (f32[5,48,256]{2,1,0:T(8,128)}, f32[5,48,256]{2,1,0:T(8,128)S(1)}, u32[]{:S(2)}) copy-start(f32[5,48,256]{2,1,0:T(8,128)S(1)} %collective-permute-done.1.refs_5_) | copy-start | bytes 737284
  20.3 0.8 %copy-start.1 = (f32[5,48,256]{2,1,0:T(8,128)}, f32[5,48,256]{2,1,0:T(8,128)S(1)}, u32[]{:S(2)}) copy-start(f32[5,48,256]{2,1,0:T(8,128)S(1)} %collective-permute-done.2.refs_6_) | copy-start | bytes 737284

commit v2 on v1

v2 whole, which is shorter than its diff:
```python
import math

import jax
import jax.numpy as jnp
import numpy as np
from jax import lax
from jax.experimental import pallas as pl
from jax.experimental.pallas import tpu as pltpu
from jax.sharding import PartitionSpec as P

MODES = 64
GAMMA = 1.4
KAPPA = 2.0

BAND = 16
SECTOR = 8
AXIAL = 256
F32 = jnp.float32
ALL = range(5)


def primitives(q):
    inverse = 1.0 / q[0]
    ux, ur, ut = q[1] * inverse, q[2] * inverse, q[3] * inverse
    pressure = (GAMMA - 1.0) * (q[4] - 0.5 * (q[1] * ux + q[2] * ur + q[3] * ut))
    sound = jnp.sqrt(GAMMA * pressure * inverse)
    return ux, ur, ut, pressure, sound


def flux(q, prim, d):
    u, pressure = prim[d - 1], prim[3]
    f = [q[d], q[1] * u, q[2] * u, q[3] * u, (q[4] + pressure) * u]
    f[d] = f[d] + pressure
    return f, jnp.abs(u) + prim[4]


def face(left_q, left_flux, right_q, right_flux):
    (fl, sl), (fr, sr) = left_flux, right_flux
    fastest = jnp.maximum(sl, sr)
    return [(fl[v] + fr[v]) - fastest * (right_q[v] - left_q[v]) for v in ALL]


def roll(x, shift, axis):
    return pltpu.roll(x, shift % x.shape[axis], axis)


def axial_difference(q, prim, lane):
    f, speed = flux(q, prim, 1)
    axis = q[0].ndim - 1
    qn = [roll(x, -1, axis) for x in q]
    fn = [qn[1]] + [roll(f[v], -1, axis) for v in range(1, 5)]
    right = face(q, (f, speed), qn, (fn, roll(speed, -1, axis)))
    ends = [2.0 * x for x in f]
    right = [jnp.where(lane == AXIAL - 1, e, x) for e, x in zip(ends, right)]
    left = [jnp.where(lane == 0, e, roll(x, 1, axis)) for e, x in zip(ends, right)]
    return [a - b for a, b in zip(right, left)]


def advance(q, prim, half_source, axial, radial, swirl, inv_r, inv_h, spin_r, bladed, rotor):
    ux, ur, ut, pressure, sound = prim
    half_r = 0.5 * inv_r
    force = bladed * (q[0] * (ut - rotor * spin_r))
    gains = [
        None,
        None,
        half_r * (q[3] * ut + pressure),
        -force - half_r * (q[2] * ut),
        -ut * force,
    ]
    rate = jnp.abs(ux) + jnp.abs(ur) + jnp.abs(ut) * inv_h + sound * (2.0 + inv_h)
    weight = 1.0 / (rate + 7.5)
    out = []
    for v in ALL:
        total = half_source[v] - 0.25 * axial[v] - radial[v] - swirl[v]
        if gains[v] is not None:
            total = total + gains[v]
        out.append((rate * q[v] + total) * weight)
    return out


def geometry_table(rows, circle):
    mean = circle / (2.0 * math.pi)
    row = np.arange(-1, rows + 1, dtype=np.float64)
    radius = mean * (0.8 + 0.4 * (row + 0.5) / rows)
    inner = mean * (0.8 + 0.4 * row / rows)
    outer = mean * (0.8 + 0.4 * (row + 1.0) / rows)
    spacing = radius * (2.0 * math.pi / circle)
    spin = radius / (1.2 * mean)
    table = np.stack(
        [0.25 * outer / radius, 0.25 * inner / radius, 0.25 / spacing, 1.0 / radius, 1.0 / spacing, spin]
    )
    return table.astype(np.float32)


def edge_row(band, at_low, at_high):
    return jnp.where(band == 0, at_low, at_high)


def rad_kernel(q_ref, qp_ref, rad_ref):
    band = lax.axis_index("rad")
    near = edge_row(band, BAND - 1, 0)
    far = edge_row(band, BAND - 2, 1)
    for v in ALL:
        rad_ref[v, 0] = q_ref[v, near]
        rad_ref[v, 1] = q_ref[v, far]
        rad_ref[v, 2] = qp_ref[v, near]


def pack_kernel(q_ref, qp_ref, rad_ref, other_ref, core_ref):
    odd = lax.axis_index("theta") % 2 == 1
    last = SECTOR - 1
    for v in ALL:
        low = [q_ref[v, :, 0, :], q_ref[v, :, 1, :], qp_ref[v, :, 0, :]]
        high = [q_ref[v, :, last, :], q_ref[v, :, last - 1, :], qp_ref[v, :, last, :]]
        corner = rad_ref[v, 0]
        low.append(jnp.broadcast_to(corner[0:1], (8, AXIAL)))
        high.append(jnp.broadcast_to(corner[last : last + 1], (8, AXIAL)))
        for n, (a, b) in enumerate(zip(low, high)):
            rows = slice(BAND * n, BAND * n + a.shape[0])
            other_ref[v, rows] = jnp.where(odd, b, a)
            core_ref[v, rows] = jnp.where(odd, a, b)


MIRROR = (1.0, 1.0, -1.0, 1.0, 1.0)


def blades(blade_ref, rows):
    blade = blade_ref[...]
    bladed = jnp.broadcast_to((blade > 0).astype(F32), (rows, AXIAL))
    rotor = jnp.broadcast_to((blade == 1).astype(F32), (rows, AXIAL))
    return bladed, rotor


def row_step(g, table_ref, q, prim, half_source, g_in, g_out, ends, masks, blade):
    lane, sub = masks
    f, speed = flux(q, prim, 3)
    qn = [roll(x, -1, 0) for x in q]
    fn = [qn[3]] + [roll(f[v], -1, 0) for v in range(1, 5)]
    between = face(q, (f, speed), qn, (fn, roll(speed, -1, 0)))
    a_out, a_in, a_h = table_ref[0, g], table_ref[1, g], table_ref[2, g]
    swirl = []
    for v in ALL:
        end = 0.0 if ends is None else ends[v]
        right = jnp.where(sub == SECTOR - 1, end, between[v])
        left = jnp.where(sub == 0, end, roll(between[v], 1, 0))
        swirl.append(a_h * (right - left))
    radial = [a_out * g_out[v] - a_in * g_in[v] for v in ALL]
    return advance(
        q,
        prim,
        half_source,
        axial_difference(q, prim, lane),
        radial,
        swirl,
        table_ref[3, g],
        table_ref[4, g],
        table_ref[5, g],
        *blade,
    )


def sweep(load, step, store):
    below = load(-1)
    below_prim = primitives(below)
    q = load(0)
    prim = primitives(q)
    g_in = face(below, flux(below, below_prim, 2), q, flux(q, prim, 2))

    def body(j, carry):
        q, prim, g_in = carry
        above = load(j + 1)
        above_prim = primitives(above)
        g_out = face(q, flux(q, prim, 2), above, flux(above, above_prim, 2))
        store(j, step(j, q, prim, g_in, g_out))
        return above, above_prim, g_out

    lax.fori_loop(0, BAND, body, (q, prim, g_in), unroll=4)


def early_kernel(table_ref, blade_ref, q_ref, qp_ref, rad_ref, p1_ref, hs_ref, p0):
    band = lax.axis_index("rad")
    first_row = band * BAND
    low = band == 0
    masks = (
        lax.broadcasted_iota(jnp.int32, (SECTOR, AXIAL), 1),
        lax.broadcasted_iota(jnp.int32, (SECTOR, AXIAL), 0),
    )
    blade = blades(blade_ref, SECTOR)
    near_at = edge_row(band, BAND + 1, 0)
    wall_at = edge_row(band, 0, BAND + 1)
    wall_row = edge_row(band, 0, BAND - 1)
    edge = edge_row(band, BAND - 1, 0)
    for v in ALL:
        p0[v, 1 : BAND + 1] = q_ref[v]
        p0[v, near_at] = rad_ref[v, 0]
        p0[v, wall_at] = MIRROR[v] * q_ref[v, wall_row]
        hs_ref[v] = 10.0 * q_ref[v] - 2.5 * qp_ref[v]

    def store(j, q):
        for v in ALL:
            p1_ref[v, j + 1] = q[v]

    sweep(
        lambda j: [p0[v, j + 1] for v in ALL],
        lambda j, q, prim, g_in, g_out: row_step(
            first_row + j + 1, table_ref, q, prim, [hs_ref[v, j] for v in ALL], g_in, g_out, None, masks, blade
        ),
        store,
    )
    near = [rad_ref[v, 0] for v in ALL]
    far = [rad_ref[v, 1] for v in ALL]
    own = [q_ref[v, edge] for v in ALL]
    below = [jnp.where(low, own[v], far[v]) for v in ALL]
    above = [jnp.where(low, far[v], own[v]) for v in ALL]
    prim = primitives(near)
    f = flux(near, prim, 2)
    g_in = face(below, flux(below, primitives(below), 2), near, f)
    g_out = face(near, f, above, flux(above, primitives(above), 2))
    half_source = [10.0 * near[v] - 2.5 * rad_ref[v, 2] for v in ALL]
    stepped = row_step(first_row + near_at, table_ref, near, prim, half_source, g_in, g_out, None, masks, blade)
    for v in ALL:
        p1_ref[v, near_at] = stepped[v]
        p1_ref[v, wall_at] = jnp.zeros((SECTOR, AXIAL), F32)


def final_kernel(
    total_rows,
    circle,
    table_ref,
    blade_ref,
    q_ref,
    rad_ref,
    p1_ref,
    hs_ref,
    other_ref,
    core_ref,
    flow_ref,
    send_ref,
    p1,
    ends,
    ce,
    fields,
):
    odd = lax.axis_index("theta") % 2 == 1
    band = lax.axis_index("rad")
    first_row = band * BAND
    low = band == 0
    near_at = edge_row(band, BAND + 1, 0)
    wall_at = edge_row(band, 0, BAND + 1)
    wall_row = edge_row(band, 0, BAND - 1)
    masks = (
        lax.broadcasted_iota(jnp.int32, (SECTOR, AXIAL), 1),
        lax.broadcasted_iota(jnp.int32, (SECTOR, AXIAL), 0),
    )
    for v in ALL:
        p1[v] = p1_ref[v]

    rows = (lax.broadcasted_iota(jnp.int32, (BAND, AXIAL), 0) + first_row).astype(F32)
    lane = lax.broadcasted_iota(jnp.int32, (BAND, AXIAL), 1)
    mean = circle / (2.0 * math.pi)
    radius = mean * (0.8 + 0.4 * (rows + 0.5) / total_rows)
    inner = mean * (0.8 + 0.4 * rows / total_rows)
    outer = mean * (0.8 + 0.4 * (rows + 1.0) / total_rows)
    inv_r = 1.0 / radius
    inv_h = inv_r * mean
    spin_r = radius * (1.0 / (1.2 * mean))
    a_h = 0.25 * inv_h
    blade16 = blades(blade_ref, BAND)
    g_near = first_row + near_at

    def speed_weight(prim, inv_h):
        ux, ur, ut, _, sound = prim
        return 1.0 / (jnp.abs(ux) + jnp.abs(ur) + jnp.abs(ut) * inv_h + sound * (2.0 + inv_h) + 7.5)

    for side in (0, 1):
        use_core = odd if side == 0 else jnp.logical_not(odd)
        at = 0 if side == 0 else SECTOR - 1
        sign = 1.0 if side == 0 else -1.0

        def pick(lo, hi):
            return [jnp.where(use_core, core_ref[v, lo:hi], other_ref[v, lo:hi]) for v in ALL]

        def ordered(halo, halo_flux, own, own_flux):
            if side == 0:
                return face(halo, halo_flux, own, own_flux)
            return face(own, own_flux, halo, halo_flux)

        near, far, prev, corner = pick(0, 16), pick(16, 32), pick(32, 48), pick(48, 49)
        own = [q_ref[v, :, at, :] for v in ALL]
        own_prim, near_prim = primitives(own), primitives(near)
        near_flux = flux(near, near_prim, 3)
        inside = ordered(near, near_flux, own, flux(own, own_prim, 3))
        outside = ordered(far, flux(far, primitives(far), 3), near, near_flux)
        scale = (sign * a_h) * speed_weight(own_prim, inv_h)
        own_next = [p1_ref[v, 1 : BAND + 1, at, :] + scale * inside[v] for v in ALL]

        edge = [rad_ref[v, 0, at : at + 1, :] for v in ALL]
        edge_prim = primitives(edge)
        corner_face = ordered(corner, flux(corner, primitives(corner), 3), edge, flux(edge, edge_prim, 3))
        corner_scale = (sign * table_ref[2, g_near]) * speed_weight(edge_prim, table_ref[4, g_near])

        for v in ALL:
            p1[v, 1 : BAND + 1, at, :] = own_next[v]
            p1[v, near_at, at : at + 1, :] = p1_ref[v, near_at, at : at + 1, :] + corner_scale * corner_face[v]
            ce[v, side, 8:24] = near[v]
            ce[v, side, 7:8] = jnp.where(low, MIRROR[v] * near[v][0:1], corner[v])
            ce[v, side, 24:25] = jnp.where(low, corner[v], MIRROR[v] * near[v][BAND - 1 : BAND])
        below = [ce[v, side, 7:23] for v in ALL]
        above = [ce[v, side, 9:25] for v in ALL]
        f = flux(near, near_prim, 2)
        g_in = face(below, flux(below, primitives(below), 2), near, f)
        g_out = face(near, f, above, flux(above, primitives(above), 2))
        near_next = advance(
            near,
            near_prim,
            [10.0 * near[v] - 2.5 * prev[v] for v in ALL],
            axial_difference(near, near_prim, lane),
            [(0.25 * inv_r) * (outer * g_out[v] - inner * g_in[v]) for v in ALL],
            [(sign * a_h) * (inside[v] - outside[v]) for v in ALL],
            inv_r,
            inv_h,
            spin_r,
            *blade16,
        )
        faces = ordered(
            near_next, flux(near_next, primitives(near_next), 3), own_next, flux(own_next, primitives(own_next), 3)
        )
        for v in ALL:
            ends[v, :, at, :] = faces[v]

    for v in ALL:
        p1[v, wall_at] = MIRROR[v] * p1[v, wall_row + 1]

    def store(j, q):
        for v in ALL:
            flow_ref[v, j] = q[v]
        ux, _, _, pressure, _ = primitives(q)
        fields[0, j] = pressure
        fields[1, j] = ux

    blade = blades(blade_ref, SECTOR)
    sweep(
        lambda j: [p1[v, j + 1] for v in ALL],
        lambda j, q, prim, g_in, g_out: row_step(
            first_row + j + 1,
            table_ref,
            q,
            prim,
            [hs_ref[v, j] for v in ALL],
            g_in,
            g_out,
            [ends[v, j] for v in ALL],
            masks,
            blade,
        ),
        store,
    )
    for f in (0, 1):
        turned = fields[f].reshape(BAND * SECTOR, AXIAL).T
        send_ref[pl.ds(f, AXIAL, stride=2), :] = turned


def mode_kernel(got_ref, basis_ref, out_ref, turned):
    sectors = got_ref.shape[0] // 4
    parts = []
    for e in (0, 1):
        for f in (0, 1):
            n = 2 * e + f
            turned[n] = got_ref[pl.ds(n, sectors, stride=4), :].T
            parts.append(
                jnp.concatenate([turned[n, pl.ds(m, BAND, stride=SECTOR), :] for m in range(SECTOR)], axis=1)
            )
    product = jnp.dot(
        jnp.concatenate(parts, axis=0), basis_ref[...], precision=lax.Precision.HIGHEST, preferred_element_type=F32
    )
    for e in (0, 1):
        for f in (0, 1):
            n = 2 * e + f
            out_ref[e, :, 2 * MODES * f : 2 * MODES * (f + 1)] = product[BAND * n : BAND * (n + 1)]


def mode_basis(sectors):
    circle = sectors * SECTOR
    cell = (np.arange(SECTOR)[:, None] + SECTOR * np.arange(sectors)[None, :]).reshape(-1)
    phase = (cell[:, None] * np.arange(1, MODES + 1)[None, :] % circle) * (2.0 * np.pi / circle)
    return (np.concatenate([np.cos(phase), -np.sin(phase)], axis=1) / np.sqrt(circle)).astype(np.float32)


def shaped(*shape):
    return jax.ShapeDtypeStruct(shape, F32)


def vmem():
    return pl.BlockSpec(memory_space=pltpu.VMEM)


def limit(mib):
    return pltpu.CompilerParams(vmem_limit_bytes=mib << 20)


def per_device(q_level, q_prev, blade_row):
    sectors = lax.axis_size("theta")
    bands = lax.axis_size("rad")
    circle = sectors * SECTOR
    core = [(t, t ^ 1) for t in range(sectors)]
    other = [(t, (((t + 1) ^ 1) - 1) % sectors) for t in range(sectors)]
    table = jnp.asarray(geometry_table(bands * BAND, circle))
    blade = blade_row.reshape(1, AXIAL)
    smem = pl.BlockSpec(memory_space=pltpu.SMEM)

    rad_out = pl.pallas_call(
        rad_kernel,
        out_shape=shaped(5, 3, SECTOR, AXIAL),
        in_specs=[vmem()] * 2,
        out_specs=vmem(),
        compiler_params=limit(4),
    )(q_level, q_prev)
    rad_in = lax.ppermute(rad_out, "rad", [(0, 1), (1, 0)])
    other_out, core_out = pl.pallas_call(
        pack_kernel,
        out_shape=[shaped(5, 56, AXIAL)] * 2,
        in_specs=[vmem()] * 3,
        out_specs=[vmem()] * 2,
        compiler_params=limit(4),
    )(q_level, q_prev, rad_in)
    other_in = lax.ppermute(other_out, "theta", other)
    core_in = lax.ppermute(core_out, "theta", core)
    part, half_source = pl.pallas_call(
        early_kernel,
        out_shape=[shaped(5, BAND + 2, SECTOR, AXIAL), shaped(5, BAND, SECTOR, AXIAL)],
        in_specs=[smem] + [vmem()] * 4,
        out_specs=[vmem()] * 2,
        scratch_shapes=[pltpu.VMEM((5, BAND + 2, SECTOR, AXIAL), F32)],
        compiler_params=limit(8),
        cost_estimate=pl.CostEstimate(flops=10_000_000, bytes_accessed=3_500_000, transcendentals=100_000),
    )(table, blade, q_level, q_prev, rad_in)

    def kernel(*refs):
        final_kernel(bands * BAND, circle, *refs)

    flow_state, send = pl.pallas_call(
        kernel,
        out_shape=[shaped(5, BAND, SECTOR, AXIAL), shaped(2 * AXIAL, BAND * SECTOR)],
        in_specs=[smem] + [vmem()] * 7,
        out_specs=[vmem()] * 2,
        scratch_shapes=[
            pltpu.VMEM((5, BAND + 2, SECTOR, AXIAL), F32),
            pltpu.VMEM((5, BAND, SECTOR, AXIAL), F32),
            pltpu.VMEM((5, 2, 32, AXIAL), F32),
            pltpu.VMEM((2, BAND, SECTOR, AXIAL), F32),
        ],
        compiler_params=limit(8),
    )(table, blade, q_level, rad_in, part, half_source, other_in, core_in)
    got = lax.all_to_all(send.reshape(sectors, 4, 128), "theta", split_axis=0, concat_axis=0, tiled=True)
    spectra = pl.pallas_call(
        mode_kernel,
        out_shape=shaped(2, BAND, 4 * MODES),
        in_specs=[vmem()] * 2,
        out_specs=vmem(),
        scratch_shapes=[pltpu.VMEM((4, BAND * SECTOR, sectors), F32)],
        compiler_params=limit(4),
    )(got.reshape(4 * sectors, 128), jnp.asarray(mode_basis(sectors)))
    return flow_state, spectra


def solution(mesh):
    in_specs = (P(None, "rad", "theta", None), P(None, "rad", "theta", None), P())
    out_specs = (P(None, "rad", "theta", None), P("theta", "rad", None))
    return jax.shard_map(per_device, mesh=mesh, in_specs=in_specs, out_specs=out_specs, check_vma=False)
```

time: 59.1 us -> 55 us (0.931)
  Pallas kernels: 14.1 us -> 7.6 us
  blocking collectives: 26 us -> 28.3 us
  waiting for transfers between devices: 4.04 us -> 2.28 us
  local copies, waits for them, and re-layouts: 0.81 us -> 2.2 us
    pallas_call x1, Pallas kernels: 9.52 us -> 4.06 us  [per_device(): pl.pallas_call(kernel, out_shape=[shaped(5, BAND, SECTOR, AXIAL), shaped(...]
    ppermute x2 -> x0, waiting for transfers between devices: 4.04 us -> none  [the longest x1 3 us: per_device(): odiag_in = lax.ppermute(odiag_out, ('theta', 'rad'), diagonal(other))]
    all_to_all x1, blocking collectives: 26 us -> 28.3 us  [per_device(): lax.all_to_all(send.reshape(sectors, 4, 128), 'theta', split_axis=0, conc...]
    ppermute x1, waiting for transfers between devices: 0.01 us -> 2.27 us  [per_device(): rad_in = lax.ppermute(rad_out, 'rad', [(0, 1), (1, 0)])]
    ppermute x1, starting transfers between devices: 0.39 us -> 2.21 us  [per_device(): rad_in = lax.ppermute(rad_out, 'rad', [(0, 1), (1, 0)])]
    unnamed x12 -> x14, local copies, waits for them, and re-layouts: 0.81 us -> 2.2 us
    ppermute x2 -> x0, starting transfers between devices: 1.29 us -> none  [the longest x1 1.29 us: per_device(): cdiag_in = lax.ppermute(cdiag_out, ('theta', 'rad'), diagonal(core))]
    pallas_call x1, Pallas kernels: 2.26 us -> 1.14 us  [per_device(): pl.pallas_call(mode_kernel, out_shape=shaped(2, BAND, 4 * MODES), in_spec...]
  transfers between devices with their start and end apart: 5 -> 3, of which waited for: 2 -> 1; matrix products, arithmetic and copies ran while one was open for 0% -> 0% of each run, Pallas kernels for 0% -> 4%
where the time goes in v2:
time: 55 us; the launch traced here: 54.8 us
  blocking collectives  28.3 us (51%)
  starting transfers between devices  13.7 us (25%)
  Pallas kernels  7.6 us (14%)
  waiting for transfers between devices  2.28 us (4%)
  local copies, waits for them, and re-layouts  2.2 us (4%)
  between operations  0.7 us (1%)
    all_to_all x1, blocking collectives, per_device(): lax.all_to_all(send.reshape(sectors, 4, 128), 'theta', split_axis=0, conc...  28.3 us
    ppermute x1, starting transfers between devices, per_device(): core_in = lax.ppermute(core_out, 'theta', core)  7.73 us
    pallas_call x1, Pallas kernels, per_device(): pl.pallas_call(kernel, out_shape=[shaped(5, BAND, SECTOR, AXIAL), shaped(...  4.06 us
    ppermute x1, starting transfers between devices, per_device(): other_in = lax.ppermute(other_out, 'theta', other)  3.78 us
    ppermute x1, waiting for transfers between devices, per_device(): rad_in = lax.ppermute(rad_out, 'rad', [(0, 1), (1, 0)])  2.27 us
    ppermute x1, starting transfers between devices, per_device(): rad_in = lax.ppermute(rad_out, 'rad', [(0, 1), (1, 0)])  2.21 us
    unnamed x14, local copies, waits for them, and re-layouts  2.2 us
    pallas_call x1, Pallas kernels, per_device(): pl.pallas_call(early_kernel, out_shape=[shaped(5, BAND + 2, SECTOR, AXIAL...  2.17 us
  transfers between devices with their start and end apart: 3, of which 1 were waited for; matrix products, arithmetic and copies ran while one was open for 0% of the time, Pallas kernels for 4%

profile of v2, /device:TPU:1, one launch (start us, length us, event | category | flops | bytes accessed | tf_op | source)
XLA Modules:
  0.0 54.8 jit_solution(14424153863380105213)
XLA Ops:
  0.6 0.0 copy-start
  0.6 1.1 %copy-done = f32[5,16,8,256]{3,2,1,0:T(8,128)S(1)} copy-done((f32[5,16,8,256]{3,2,1,0:T(8,128)S(1)}, f32[5,16,8,256]{3,2,1,0:T(8,128)}, u32[]{:S(2)}) %copy-start) | copy-done | bytes 655384
  1.7 0.0 copy-start.2
  1.7 1.1 %copy-done.2 = f32[5,16,8,256]{3,2,1,0:T(8,128)S(1)} copy-done((f32[5,16,8,256]{3,2,1,0:T(8,128)S(1)}, f32[5,16,8,256]{3,2,1,0:T(8,128)}, u32[]{:S(2)}) %copy-start.2) | copy-done | bytes 655384
  2.8 0.0 copy-start.1
  2.8 0.0 copy-start.3
  2.8 2.2 %collective-permute-start = (f32[5,3,8,256]{3,2,1,0:T(8,128)S(1)}, f32[5,3,8,256]{3,2,1,0:T(8,128)S(1)}, u32[]{:S(2)}, u32[]{:S(2)}) collective-permute-start(f32[5,3,8,256]{3,2,1,0:T(8,128)S(1)} %shard_map.68), channel_id=1, source_target_pairs={{0,1},{1,0},{2,3},{3,2},{4,5},{5,4},{6,7},{7,6},{8,9},{9,8},{10,11... | collective-permute-start | bytes 368648 | tf_op jit(solution)/shard_map/ppermute | solution.py:418
  5.1 2.3 %collective-permute-done.rad_ref.refs_3_ = f32[5,3,8,256]{3,2,1,0:T(8,128)S(1)} collective-permute-done((f32[5,3,8,256]{3,2,1,0:T(8,128)S(1)}, f32[5,3,8,256]{3,2,1,0:T(8,128)S(1)}, u32[]{:S(2)}, u32[]{:S(2)}) %collective-permute-start) | collective-permute-done | bytes 122912 | tf_op jit(solution)/shard_map/ppermute | solution.py:418
  7.3 0.2 shard_map.70
  7.6 0.0 copy-start.5
  7.6 3.8 %collective-permute-start.1 = (f32[5,56,256]{2,1,0:T(8,128)S(1)}, f32[5,56,256]{2,1,0:T(8,128)S(1)}, u32[]{:S(2)}, u32[]{:S(2)}) collective-permute-start(f32[5,56,256]{2,1,0:T(8,128)S(1)} %get-tuple-element.10), channel_id=1, source_target_pairs={{0,254},{2,4},{4,2},{6,8},{8,6},{10,12},{12,10},{14,16},{16,14},{1... | collective-permute-start | bytes 860168 | tf_op jit(solution)/shard_map/ppermute | solution.py:426
  11.4 0.0 copy-start.6
  11.4 7.7 %collective-permute-start.2 = (f32[5,56,256]{2,1,0:T(8,128)S(1)}, f32[5,56,256]{2,1,0:T(8,128)S(1)}, u32[]{:S(2)}, u32[]{:S(2)}) collective-permute-start(f32[5,56,256]{2,1,0:T(8,128)S(1)} %get-tuple-element.11), channel_id=1, source_target_pairs={{0,2},{2,0},{4,6},{6,4},{8,10},{10,8},{12,14},{14,12},{16,18},{18,... | collective-permute-start | bytes 860168 | tf_op jit(solution)/shard_map/ppermute | solution.py:427
  19.1 0.0 copy-done.1
  19.1 0.0 copy-done.3
  19.1 0.0 copy-done.5
  19.1 0.0 copy-done.6
  19.1 2.2 %shard_map.69 = (f32[5,18,8,256]{3,2,1,0:T(8,128)S(1)}, f32[5,16,8,256]{3,2,1,0:T(8,128)S(1)}) custom-call(f32[6,34]{1,0:T(8,128)S(1)} %copy-done.5, s32[1,256]{1,0:T(1,128)S(1)} %bitcast.5, f32[5,16,8,256]{3,2,1,0:T(8,128)S(1)} %copy-done.1, f32[5,16,8,256]{3,2,1,0:T(8,128)S(1)} %copy-done.3, f32[5,3,8,256]{3,2,1,0:T(8,128)S(1)} %collective-permute-done.rad_ref.refs_3_), custom_call_target="tpu_custom_call" | custom-call | flops 10000000 | bytes 3500000 | tf_op jit(solution)/shard_map/pallas_call | solution.py:428
  21.3 0.0 collective-permute-done.1.refs_6_
  21.3 0.0 collective-permute-done.2.refs_7_
  21.3 4.1 %shard_map.71 = (f32[5,16,8,256]{3,2,1,0:T(8,128)}, f32[512,128]{1,0:T(8,128)S(1)}) custom-call(f32[6,34]{1,0:T(8,128)S(1)} %copy-done.5, s32[1,256]{1,0:T(1,128)S(1)} %bitcast.6, f32[5,16,8,256]{3,2,1,0:T(8,128)S(1)} %copy-done.1, f32[5,3,8,256]{3,2,1,0:T(8,128)S(1)} %collective-permute-done.rad_ref.refs_3_, ...), custom_call_target="tpu_custom_call" | custom-call | tf_op jit(solution)/shard_map/pallas_call | solution.py:441
  25.4 0.0 copy-start.4
  25.4 28.3 %all_to_all.5 = f32[128,4,128]{2,1,0:T(4,128)S(1)} all-to-all(f32[128,4,128]{2,1,0:T(4,128)S(1)} %bitcast.4), channel_id=1, replica_groups=mesh['theta'=128,'rad'=2] {'theta'}, dimensions={0} | all-to-all | bytes 524288 | tf_op jit(solution)/shard_map/all_to_all | solution.py:454
  53.6 0.0 copy-done.4
  53.6 1.1 %shard_map.72 = f32[2,16,256]{2,1,0:T(8,128)} custom-call(f32[512,128]{1,0:T(8,128)S(1)} %bitcast.3, f32[1024,128]{1,0:T(8,128)S(1)} %copy-done.4), custom_call_target="tpu_custom_call" | custom-call | tf_op jit(solution)/shard_map/pallas_call | solution.py:455
  (1 shorter events, 0.0 us)
Async XLA Ops:
  0.6 1.1 %copy-start = (f32[5,16,8,256]{3,2,1,0:T(8,128)S(1)}, f32[5,16,8,256]{3,2,1,0:T(8,128)}, u32[]{:S(2)}) copy-start(f32[5,16,8,256]{3,2,1,0:T(8,128)} %refs_2_.1) | copy-start | bytes 1966084
  1.7 1.1 %copy-start.2 = (f32[5,16,8,256]{3,2,1,0:T(8,128)S(1)}, f32[5,16,8,256]{3,2,1,0:T(8,128)}, u32[]{:S(2)}) copy-start(f32[5,16,8,256]{3,2,1,0:T(8,128)} %qp_ref.5) | copy-start | bytes 1966084
  2.8 16.3 %copy-start.1 = (f32[5,16,8,256]{3,2,1,0:T(8,128)S(1)}, f32[5,16,8,256]{3,2,1,0:T(8,128)}, u32[]{:S(2)}) copy-start(f32[5,16,8,256]{3,2,1,0:T(8,128)} %refs_2_.1) | copy-start | bytes 1966084
  2.8 16.3 %copy-start.3 = (f32[5,16,8,256]{3,2,1,0:T(8,128)S(1)}, f32[5,16,8,256]{3,2,1,0:T(8,128)}, u32[]{:S(2)}) copy-start(f32[5,16,8,256]{3,2,1,0:T(8,128)} %qp_ref.5) | copy-start | bytes 1966084
  2.8 4.5 %collective-permute-start = (f32[5,3,8,256]{3,2,1,0:T(8,128)S(1)}, f32[5,3,8,256]{3,2,1,0:T(8,128)S(1)}, u32[]{:S(2)}, u32[]{:S(2)}) collective-permute-start(f32[5,3,8,256]{3,2,1,0:T(8,128)S(1)} %shard_map.68), channel_id=1, source_target_pairs={{0,1},{1,0},{2,3},{3,2},{4,5},{5,4},{6,7},{7,6},{8,9},{9,8},{10,11... | collective-permute-start | bytes 368648 | tf_op jit(solution)/shard_map/ppermute | solution.py:418
  7.6 11.5 %copy-start.5 = (f32[6,34]{1,0:T(8,128)S(1)}, f32[6,34]{1,0:T(8,128)}, u32[]{:S(2)}) copy-start(f32[6,34]{1,0:T(8,128)} %constant.4.clone.table_ref.refs_0_) | copy-start | bytes 2452
  7.6 13.7 %collective-permute-start.1 = (f32[5,56,256]{2,1,0:T(8,128)S(1)}, f32[5,56,256]{2,1,0:T(8,128)S(1)}, u32[]{:S(2)}, u32[]{:S(2)}) collective-permute-start(f32[5,56,256]{2,1,0:T(8,128)S(1)} %get-tuple-element.10), channel_id=1, source_target_pairs={{0,254},{2,4},{4,2},{6,8},{8,6},{10,12},{12,10},{14,16},{16,14},{1... | collective-permute-start | bytes 860168 | tf_op jit(solution)/shard_map/ppermute | solution.py:426
  11.4 7.7 %copy-start.6 = (s32[256]{0:T(256)S(1)}, s32[256]{0:T(256)}, u32[]{:S(2)}) copy-start(s32[256]{0:T(256)} %param.7) | copy-start | bytes 3076
  11.4 9.9 %collective-permute-start.2 = (f32[5,56,256]{2,1,0:T(8,128)S(1)}, f32[5,56,256]{2,1,0:T(8,128)S(1)}, u32[]{:S(2)}, u32[]{:S(2)}) collective-permute-start(f32[5,56,256]{2,1,0:T(8,128)S(1)} %get-tuple-element.11), channel_id=1, source_target_pairs={{0,2},{2,0},{4,6},{6,4},{8,10},{10,8},{12,14},{14,12},{16,18},{18,... | collective-permute-start | bytes 860168 | tf_op jit(solution)/shard_map/ppermute | solution.py:427
  25.4 28.3 %copy-start.4 = (f32[1024,128]{1,0:T(8,128)S(1)}, f32[1024,128]{1,0:T(8,128)}, u32[]{:S(2)}) copy-start(f32[1024,128]{1,0:T(8,128)} %constant.5.clone.basis_ref) | copy-start | bytes 1572868

commit v3 on v2

--- a/solution.py
+++ b/solution.py
@@ -96,29 +96,11 @@
     return jnp.where(band == 0, at_low, at_high)
 
 
-def rad_kernel(q_ref, qp_ref, rad_ref):
-    band = lax.axis_index("rad")
-    near = edge_row(band, BAND - 1, 0)
-    far = edge_row(band, BAND - 2, 1)
-    for v in ALL:
-        rad_ref[v, 0] = q_ref[v, near]
-        rad_ref[v, 1] = q_ref[v, far]
-        rad_ref[v, 2] = qp_ref[v, near]
-
-
-def pack_kernel(q_ref, qp_ref, rad_ref, other_ref, core_ref):
-    odd = lax.axis_index("theta") % 2 == 1
-    last = SECTOR - 1
-    for v in ALL:
-        low = [q_ref[v, :, 0, :], q_ref[v, :, 1, :], qp_ref[v, :, 0, :]]
-        high = [q_ref[v, :, last, :], q_ref[v, :, last - 1, :], qp_ref[v, :, last, :]]
-        corner = rad_ref[v, 0]
-        low.append(jnp.broadcast_to(corner[0:1], (8, AXIAL)))
-        high.append(jnp.broadcast_to(corner[last : last + 1], (8, AXIAL)))
-        for n, (a, b) in enumerate(zip(low, high)):
-            rows = slice(BAND * n, BAND * n + a.shape[0])
-            other_ref[v, rows] = jnp.where(odd, b, a)
-            core_ref[v, rows] = jnp.where(odd, a, b)
+def rad_kernel(q_ref, rad_ref, sem):
+    near = edge_row(lax.axis_index("rad"), BAND - 1, 0)
+    copy = pltpu.make_async_copy(q_ref.at[:, near], rad_ref, sem)
+    copy.start()
+    copy.wait()
 
 
 MIRROR = (1.0, 1.0, -1.0, 1.0, 1.0)
@@ -129,6 +111,80 @@
     bladed = jnp.broadcast_to((blade > 0).astype(F32), (rows, AXIAL))
     rotor = jnp.broadcast_to((blade == 1).astype(F32), (rows, AXIAL))
     return bladed, rotor
+
+
+class Columns:
+    def __init__(self, first_row, total_rows, circle):
+        rows = (lax.broadcasted_iota(jnp.int32, (BAND, AXIAL), 0) + first_row).astype(F32)
+        mean = circle / (2.0 * math.pi)
+        radius = mean * (0.8 + 0.4 * (rows + 0.5) / total_rows)
+        self.inner = mean * (0.8 + 0.4 * rows / total_rows)
+        self.outer = mean * (0.8 + 0.4 * (rows + 1.0) / total_rows)
+        self.inv_r = 1.0 / radius
+        self.inv_h = self.inv_r * mean
+        self.spin_r = radius * (1.0 / (1.2 * mean))
+        self.a_h = 0.25 * self.inv_h
+
+
+def load_kernel(q_ref, qp_ref, q_out_ref, qp_out_ref, sems):
+    copies = [
+        pltpu.make_async_copy(q_ref, q_out_ref, sems.at[0]),
+        pltpu.make_async_copy(qp_ref, qp_out_ref, sems.at[1]),
+    ]
+    for copy in copies:
+        copy.start()
+    for copy in copies:
+        copy.wait()
+
+
+def pack_kernel(total_rows, circle, blade_ref, q_ref, qp_ref, rad_ref, other_ref, core_ref, ce):
+    odd = lax.axis_index("theta") % 2 == 1
+    band = lax.axis_index("rad")
+    low = band == 0
+    geo = Columns(band * BAND, total_rows, circle)
+    blade = blades(blade_ref, BAND)
+    lane = lax.broadcasted_iota(jnp.int32, (BAND, AXIAL), 1)
+    sides = []
+    for side in (0, 1):
+        at, inner = (0, 1) if side == 0 else (SECTOR - 1, SECTOR - 2)
+        edge = [q_ref[v, :, at, :] for v in ALL]
+        second = [q_ref[v, :, inner, :] for v in ALL]
+        half_source = [10.0 * edge[v] - 2.5 * qp_ref[v, :, at, :] for v in ALL]
+        corner = [rad_ref[v, at : at + 1, :] for v in ALL]
+        for v in ALL:
+            ce[v, side, 8:24] = edge[v]
+            ce[v, side, 7:8] = jnp.where(low, MIRROR[v] * edge[v][0:1], corner[v])
+            ce[v, side, 24:25] = jnp.where(low, corner[v], MIRROR[v] * edge[v][BAND - 1 : BAND])
+        below = [ce[v, side, 7:23] for v in ALL]
+        above = [ce[v, side, 9:25] for v in ALL]
+        prim = primitives(edge)
+        f = flux(edge, prim, 2)
+        g_in = face(below, flux(below, primitives(below), 2), edge, f)
+        g_out = face(edge, f, above, flux(above, primitives(above), 2))
+        f = flux(edge, prim, 3)
+        second_flux = flux(second, primitives(second), 3)
+        if side == 0:
+            swirl = [geo.a_h * x for x in face(edge, f, second, second_flux)]
+        else:
+            swirl = [-geo.a_h * x for x in face(second, second_flux, edge, f)]
+        part = advance(
+            edge,
+            prim,
+            half_source,
+            axial_difference(edge, prim, lane),
+            [(0.25 * geo.inv_r) * (geo.outer * g_out[v] - geo.inner * g_in[v]) for v in ALL],
+            swirl,
+            geo.inv_r,
+            geo.inv_h,
+            geo.spin_r,
+            *blade,
+        )
+        sides.append((edge, part, [jnp.broadcast_to(x, (8, AXIAL)) for x in corner]))
+    for n, (a, b) in enumerate(zip(*sides)):
+        for v in ALL:
+            rows = slice(BAND * n, BAND * n + a[v].shape[0])
+            other_ref[v, rows] = jnp.where(odd, b[v], a[v])
+            core_ref[v, rows] = jnp.where(odd, a[v], b[v])
 
 
 def row_step(g, table_ref, q, prim, half_source, g_in, g_out, ends, masks, blade):
@@ -177,10 +233,9 @@
     lax.fori_loop(0, BAND, body, (q, prim, g_in), unroll=4)
 
 
-def early_kernel(table_ref, blade_ref, q_ref, qp_ref, rad_ref, p1_ref, hs_ref, p0):
+def early_kernel(table_ref, blade_ref, q_ref, qp_ref, rad_ref, p1_ref, edge_ref, hs_ref, p0):
     band = lax.axis_index("rad")
     first_row = band * BAND
-    low = band == 0
     masks = (
         lax.broadcasted_iota(jnp.int32, (SECTOR, AXIAL), 1),
         lax.broadcasted_iota(jnp.int32, (SECTOR, AXIAL), 0),
@@ -189,16 +244,15 @@
     near_at = edge_row(band, BAND + 1, 0)
     wall_at = edge_row(band, 0, BAND + 1)
     wall_row = edge_row(band, 0, BAND - 1)
-    edge = edge_row(band, BAND - 1, 0)
     for v in ALL:
         p0[v, 1 : BAND + 1] = q_ref[v]
-        p0[v, near_at] = rad_ref[v, 0]
+        p0[v, near_at] = rad_ref[v]
         p0[v, wall_at] = MIRROR[v] * q_ref[v, wall_row]
         hs_ref[v] = 10.0 * q_ref[v] - 2.5 * qp_ref[v]
 
     def store(j, q):
         for v in ALL:
-            p1_ref[v, j + 1] = q[v]
+            p1_ref[v, j] = q[v]
 
     sweep(
         lambda j: [p0[v, j + 1] for v in ALL],
@@ -207,20 +261,8 @@
         ),
         store,
     )
-    near = [rad_ref[v, 0] for v in ALL]
-    far = [rad_ref[v, 1] for v in ALL]
-    own = [q_ref[v, edge] for v in ALL]
-    below = [jnp.where(low, own[v], far[v]) for v in ALL]
-    above = [jnp.where(low, far[v], own[v]) for v in ALL]
-    prim = primitives(near)
-    f = flux(near, prim, 2)
-    g_in = face(below, flux(below, primitives(below), 2), near, f)
-    g_out = face(near, f, above, flux(above, primitives(above), 2))
-    half_source = [10.0 * near[v] - 2.5 * rad_ref[v, 2] for v in ALL]
-    stepped = row_step(first_row + near_at, table_ref, near, prim, half_source, g_in, g_out, None, masks, blade)
-    for v in ALL:
-        p1_ref[v, near_at] = stepped[v]
-        p1_ref[v, wall_at] = jnp.zeros((SECTOR, AXIAL), F32)
+    for v in ALL:
+        edge_ref[v] = p1_ref[v, edge_row(band, BAND - 1, 0)]
 
 
 def final_kernel(
@@ -232,19 +274,18 @@
     rad_ref,
     p1_ref,
     hs_ref,
+    next_ref,
     other_ref,
     core_ref,
     flow_ref,
     send_ref,
     p1,
     ends,
-    ce,
     fields,
 ):
     odd = lax.axis_index("theta") % 2 == 1
     band = lax.axis_index("rad")
     first_row = band * BAND
-    low = band == 0
     near_at = edge_row(band, BAND + 1, 0)
     wall_at = edge_row(band, 0, BAND + 1)
     wall_row = edge_row(band, 0, BAND - 1)
@@ -253,22 +294,13 @@
         lax.broadcasted_iota(jnp.int32, (SECTOR, AXIAL), 0),
     )
     for v in ALL:
-        p1[v] = p1_ref[v]
-
-    rows = (lax.broadcasted_iota(jnp.int32, (BAND, AXIAL), 0) + first_row).astype(F32)
-    lane = lax.broadcasted_iota(jnp.int32, (BAND, AXIAL), 1)
-    mean = circle / (2.0 * math.pi)
-    radius = mean * (0.8 + 0.4 * (rows + 0.5) / total_rows)
-    inner = mean * (0.8 + 0.4 * rows / total_rows)
-    outer = mean * (0.8 + 0.4 * (rows + 1.0) / total_rows)
-    inv_r = 1.0 / radius
-    inv_h = inv_r * mean
-    spin_r = radius * (1.0 / (1.2 * mean))
-    a_h = 0.25 * inv_h
-    blade16 = blades(blade_ref, BAND)
+        p1[v, 1 : BAND + 1] = p1_ref[v]
+        p1[v, near_at] = next_ref[v]
+
+    geo = Columns(first_row, total_rows, circle)
     g_near = first_row + near_at
 
-    def speed_weight(prim, inv_h):
+    def weight(prim, inv_h):
         ux, ur, ut, _, sound = prim
         return 1.0 / (jnp.abs(ux) + jnp.abs(ur) + jnp.abs(ut) * inv_h + sound * (2.0 + inv_h) + 7.5)
 
@@ -280,52 +312,28 @@
         def pick(lo, hi):
             return [jnp.where(use_core, core_ref[v, lo:hi], other_ref[v, lo:hi]) for v in ALL]
 
-        def ordered(halo, halo_flux, own, own_flux):
-            if side == 0:
-                return face(halo, halo_flux, own, own_flux)
-            return face(own, own_flux, halo, halo_flux)
-
-        near, far, prev, corner = pick(0, 16), pick(16, 32), pick(32, 48), pick(48, 49)
+        def ordered(halo, halo_prim, own, own_prim):
+            a, b = flux(halo, halo_prim, 3), flux(own, own_prim, 3)
+            return face(halo, a, own, b) if side == 0 else face(own, b, halo, a)
+
+        near, near_part, corner = pick(0, 16), pick(16, 32), pick(32, 33)
         own = [q_ref[v, :, at, :] for v in ALL]
         own_prim, near_prim = primitives(own), primitives(near)
-        near_flux = flux(near, near_prim, 3)
-        inside = ordered(near, near_flux, own, flux(own, own_prim, 3))
-        outside = ordered(far, flux(far, primitives(far), 3), near, near_flux)
-        scale = (sign * a_h) * speed_weight(own_prim, inv_h)
-        own_next = [p1_ref[v, 1 : BAND + 1, at, :] + scale * inside[v] for v in ALL]
-
-        edge = [rad_ref[v, 0, at : at + 1, :] for v in ALL]
+        shared = ordered(near, near_prim, own, own_prim)
+        own_scale = (sign * geo.a_h) * weight(own_prim, geo.inv_h)
+        near_scale = (-sign * geo.a_h) * weight(near_prim, geo.inv_h)
+        own_next = [p1_ref[v, :, at, :] + own_scale * shared[v] for v in ALL]
+        near_next = [near_part[v] + near_scale * shared[v] for v in ALL]
+
+        edge = [rad_ref[v, at : at + 1, :] for v in ALL]
         edge_prim = primitives(edge)
-        corner_face = ordered(corner, flux(corner, primitives(corner), 3), edge, flux(edge, edge_prim, 3))
-        corner_scale = (sign * table_ref[2, g_near]) * speed_weight(edge_prim, table_ref[4, g_near])
-
+        corner_face = ordered(corner, primitives(corner), edge, edge_prim)
+        corner_scale = (sign * table_ref[2, g_near]) * weight(edge_prim, table_ref[4, g_near])
+
+        faces = ordered(near_next, primitives(near_next), own_next, primitives(own_next))
         for v in ALL:
             p1[v, 1 : BAND + 1, at, :] = own_next[v]
-            p1[v, near_at, at : at + 1, :] = p1_ref[v, near_at, at : at + 1, :] + corner_scale * corner_face[v]
-            ce[v, side, 8:24] = near[v]
-            ce[v, side, 7:8] = jnp.where(low, MIRROR[v] * near[v][0:1], corner[v])
-            ce[v, side, 24:25] = jnp.where(low, corner[v], MIRROR[v] * near[v][BAND - 1 : BAND])
-        below = [ce[v, side, 7:23] for v in ALL]
-        above = [ce[v, side, 9:25] for v in ALL]
-        f = flux(near, near_prim, 2)
-        g_in = face(below, flux(below, primitives(below), 2), near, f)
-        g_out = face(near, f, above, flux(above, primitives(above), 2))
-        near_next = advance(
-            near,
-            near_prim,
-            [10.0 * near[v] - 2.5 * prev[v] for v in ALL],
-            axial_difference(near, near_prim, lane),
-            [(0.25 * inv_r) * (outer * g_out[v] - inner * g_in[v]) for v in ALL],
-            [(sign * a_h) * (inside[v] - outside[v]) for v in ALL],
-            inv_r,
-            inv_h,
-            spin_r,
-            *blade16,
-        )
-        faces = ordered(
-            near_next, flux(near_next, primitives(near_next), 3), own_next, flux(own_next, primitives(own_next), 3)
-        )
-        for v in ALL:
+            p1[v, near_at, at : at + 1, :] = next_ref[v, at : at + 1, :] + corner_scale * corner_face[v]
             ends[v, :, at, :] = faces[v]
 
     for v in ALL:
@@ -360,7 +368,9 @@
         send_ref[pl.ds(f, AXIAL, stride=2), :] = turned
 
 
-def mode_kernel(got_ref, basis_ref, out_ref, turned):
+def mode_kernel(got_ref, basis_ref, flow_ref, out_ref, flow_out_ref, turned, sem):
+    copy = pltpu.make_async_copy(flow_ref, flow_out_ref, sem)
+    copy.start()
     sectors = got_ref.shape[0] // 4
     parts = []
     for e in (0, 1):
@@ -377,6 +387,7 @@
         for f in (0, 1):
             n = 2 * e + f
             out_ref[e, :, 2 * MODES * f : 2 * MODES * (f + 1)] = product[BAND * n : BAND * (n + 1)]
+    copy.wait()
 
 
 def mode_basis(sectors):
@@ -395,7 +406,7 @@
 
 
 def limit(mib):
-    return pltpu.CompilerParams(vmem_limit_bytes=mib << 20)
+    return pltpu.CompilerParams(vmem_limit_bytes=int(mib * 2**20))
 
 
 def per_device(q_level, q_prev, blade_row):
@@ -408,58 +419,77 @@
     blade = blade_row.reshape(1, AXIAL)
     smem = pl.BlockSpec(memory_space=pltpu.SMEM)
 
-    rad_out = pl.pallas_call(
-        rad_kernel,
-        out_shape=shaped(5, 3, SECTOR, AXIAL),
-        in_specs=[vmem()] * 2,
-        out_specs=vmem(),
+    hbm = pl.BlockSpec(memory_space=pltpu.HBM)
+    swap = [(0, 1), (1, 0)]
+
+    def pack(*refs):
+        pack_kernel(bands * BAND, circle, *refs)
+
+    def final(*refs):
+        final_kernel(bands * BAND, circle, *refs)
+
+    rad_in = lax.ppermute(
+        pl.pallas_call(
+            rad_kernel,
+            out_shape=shaped(5, SECTOR, AXIAL),
+            in_specs=[hbm],
+            out_specs=vmem(),
+            scratch_shapes=[pltpu.SemaphoreType.DMA],
+            compiler_params=limit(63.5),
+        )(q_level),
+        "rad",
+        swap,
+    )
+    q_level, q_prev = pl.pallas_call(
+        load_kernel,
+        out_shape=[shaped(5, BAND, SECTOR, AXIAL)] * 2,
+        in_specs=[hbm] * 2,
+        out_specs=[vmem()] * 2,
+        scratch_shapes=[pltpu.SemaphoreType.DMA((2,))],
+        compiler_params=limit(2),
+        cost_estimate=pl.CostEstimate(flops=0, bytes_accessed=3_000_000, transcendentals=0),
+    )(q_level, q_prev)
+    other_out, core_out = pl.pallas_call(
+        pack,
+        out_shape=[shaped(5, 40, AXIAL)] * 2,
+        in_specs=[vmem()] * 4,
+        out_specs=[vmem()] * 2,
+        scratch_shapes=[pltpu.VMEM((5, 2, 32, AXIAL), F32)],
         compiler_params=limit(4),
-    )(q_level, q_prev)
-    rad_in = lax.ppermute(rad_out, "rad", [(0, 1), (1, 0)])
-    other_out, core_out = pl.pallas_call(
-        pack_kernel,
-        out_shape=[shaped(5, 56, AXIAL)] * 2,
-        in_specs=[vmem()] * 3,
-        out_specs=[vmem()] * 2,
-        compiler_params=limit(4),
-    )(q_level, q_prev, rad_in)
+    )(blade, q_level, q_prev, rad_in)
+    core_in = lax.ppermute(core_out, "theta", core)
     other_in = lax.ppermute(other_out, "theta", other)
-    core_in = lax.ppermute(core_out, "theta", core)
-    part, half_source = pl.pallas_call(
+    part, edge, half_source = pl.pallas_call(
         early_kernel,
-        out_shape=[shaped(5, BAND + 2, SECTOR, AXIAL), shaped(5, BAND, SECTOR, AXIAL)],
+        out_shape=[shaped(5, BAND, SECTOR, AXIAL), shaped(5, SECTOR, AXIAL), shaped(5, BAND, SECTOR, AXIAL)],
         in_specs=[smem] + [vmem()] * 4,
-        out_specs=[vmem()] * 2,
+        out_specs=[vmem()] * 3,
         scratch_shapes=[pltpu.VMEM((5, BAND + 2, SECTOR, AXIAL), F32)],
         compiler_params=limit(8),
         cost_estimate=pl.CostEstimate(flops=10_000_000, bytes_accessed=3_500_000, transcendentals=100_000),
     )(table, blade, q_level, q_prev, rad_in)
-
-    def kernel(*refs):
-        final_kernel(bands * BAND, circle, *refs)
-
+    next_in = lax.ppermute(edge, "rad", swap)
     flow_state, send = pl.pallas_call(
-        kernel,
+        final,
         out_shape=[shaped(5, BAND, SECTOR, AXIAL), shaped(2 * AXIAL, BAND * SECTOR)],
-        in_specs=[smem] + [vmem()] * 7,
+        in_specs=[smem] + [vmem()] * 8,
         out_specs=[vmem()] * 2,
         scratch_shapes=[
             pltpu.VMEM((5, BAND + 2, SECTOR, AXIAL), F32),
             pltpu.VMEM((5, BAND, SECTOR, AXIAL), F32),
-            pltpu.VMEM((5, 2, 32, AXIAL), F32),
             pltpu.VMEM((2, BAND, SECTOR, AXIAL), F32),
         ],
         compiler_params=limit(8),
-    )(table, blade, q_level, rad_in, part, half_source, other_in, core_in)
+    )(table, blade, q_level, rad_in, part, half_source, next_in, other_in, core_in)
     got = lax.all_to_all(send.reshape(sectors, 4, 128), "theta", split_axis=0, concat_axis=0, tiled=True)
-    spectra = pl.pallas_call(
+    spectra, flow_state = pl.pallas_call(
         mode_kernel,
-        out_shape=shaped(2, BAND, 4 * MODES),
-        in_specs=[vmem()] * 2,
-        out_specs=vmem(),
-        scratch_shapes=[pltpu.VMEM((4, BAND * SECTOR, sectors), F32)],
+        out_shape=[shaped(2, BAND, 4 * MODES), shaped(5, BAND, SECTOR, AXIAL)],
+        in_specs=[vmem()] * 3,
+        out_specs=[vmem(), hbm],
+        scratch_shapes=[pltpu.VMEM((4, BAND * SECTOR, sectors), F32), pltpu.SemaphoreType.DMA],
         compiler_params=limit(4),
-    )(got.reshape(4 * sectors, 128), jnp.asarray(mode_basis(sectors)))
+    )(got.reshape(4 * sectors, 128), jnp.asarray(mode_basis(sectors)), flow_state)
     return flow_state, spectra
 
 

time: 55 us -> 54.1 us (0.984)
  blocking collectives: 28.3 us -> 24.7 us
  Pallas kernels: 7.6 us -> 9.84 us
  starting transfers between devices: 13.7 us -> 12.9 us
  local copies, waits for them, and re-layouts: 2.2 us -> 2.86 us
  waiting for transfers between devices: 2.28 us -> 2.85 us
    all_to_all x1, blocking collectives: 28.3 us -> 24.7 us  [per_device(): lax.all_to_all(send.reshape(sectors, 4, 128), 'theta', split_axis=0, conc...]
    pallas_call x5 -> x6, Pallas kernels: 7.6 us -> 9.84 us  [the longest x1 2.87 us: per_device(): pl.pallas_call(final, out_shape=[shaped(5, BAND, SECTOR, AXIAL), shaped(2...]
    ppermute x1, starting transfers between devices: 3.78 us -> 2.58 us  [per_device(): other_in = lax.ppermute(other_out, 'theta', other)]
    unnamed x14 -> x10, local copies, waits for them, and re-layouts: 2.2 us -> 2.86 us
    ppermute x1 -> x2, waiting for transfers between devices: 2.27 us -> 2.84 us  [the longest x1 2.84 us: per_device(): next_in = lax.ppermute(edge, 'rad', swap)]
    ppermute x1 -> x2, starting transfers between devices: 2.21 us -> 2.31 us  [the longest x1 2.21 us: per_device(): lax.ppermute(pl.pallas_call(rad_kernel, out_shape=shaped(5, SECTOR, AXIAL...]
  transfers between devices with their start and end apart: 3 -> 4, of which waited for: 1 -> 1; matrix products, arithmetic and copies ran while one was open for 0% -> 0% of each run, Pallas kernels for 4% -> 4%
where the time goes in v3:
time: 54.1 us; the launch traced here: 53.8 us
  blocking collectives  24.7 us (46%)
  starting transfers between devices  12.9 us (24%)
  Pallas kernels  9.84 us (18%)
  local copies, waits for them, and re-layouts  2.86 us (5%)
  waiting for transfers between devices  2.85 us (5%)
  between operations  0.7 us (1%)
    all_to_all x1, blocking collectives, per_device(): lax.all_to_all(send.reshape(sectors, 4, 128), 'theta', split_axis=0, conc...  24.7 us
    ppermute x1, starting transfers between devices, per_device(): core_in = lax.ppermute(core_out, 'theta', core)  8.01 us
    pallas_call x1, Pallas kernels, per_device(): pl.pallas_call(final, out_shape=[shaped(5, BAND, SECTOR, AXIAL), shaped(2...  2.87 us
    unnamed x10, local copies, waits for them, and re-layouts  2.86 us
    ppermute x1, waiting for transfers between devices, per_device(): next_in = lax.ppermute(edge, 'rad', swap)  2.84 us
    ppermute x1, starting transfers between devices, per_device(): other_in = lax.ppermute(other_out, 'theta', other)  2.58 us
    ppermute x1, starting transfers between devices, per_device(): lax.ppermute(pl.pallas_call(rad_kernel, out_shape=shaped(5, SECTOR, AXIAL...  2.21 us
    pallas_call x1, Pallas kernels, per_device(): pl.pallas_call(early_kernel, out_shape=[shaped(5, BAND, SECTOR, AXIAL), s...  1.96 us
  transfers between devices with their start and end apart: 4, of which 1 were waited for; matrix products, arithmetic and copies ran while one was open for 0% of the time, Pallas kernels for 4%

profile of v3, /device:TPU:1, one launch (start us, length us, event | category | flops | bytes accessed | tf_op | source)
XLA Modules:
  0.0 53.8 jit_solution(13412057502977395533)
XLA Ops:
  0.6 1.4 %shard_map.69 = f32[5,8,256]{2,1,0:T(8,128)} custom-call(f32[5,16,8,256]{3,2,1,0:T(8,128)} %q_ref.3), custom_call_target="tpu_custom_call" | custom-call | tf_op jit(solution)/shard_map/pallas_call | solution.py:432
  2.0 2.2 %collective-permute-start = (f32[5,8,256]{2,1,0:T(8,128)}, f32[5,8,256]{2,1,0:T(8,128)S(1)}, u32[]{:S(2)}, u32[]{:S(2)}) collective-permute-start(f32[5,8,256]{2,1,0:T(8,128)} %shard_map.69), channel_id=1, source_target_pairs={{0,1},{1,0},{2,3},{3,2},{4,5},{5,4},{6,7},{7,6},{8,9},{9,8},{10,11... | collective-permute-start | bytes 122888 | tf_op jit(solution)/shard_map/ppermute | solution.py:431
  4.3 0.0 copy-start
  4.3 1.1 %copy-done = f32[5,16,8,256]{3,2,1,0:T(8,128)S(1)} copy-done((f32[5,16,8,256]{3,2,1,0:T(8,128)S(1)}, f32[5,16,8,256]{3,2,1,0:T(8,128)}, u32[]{:S(2)}) %copy-start) | copy-done | bytes 655384
  5.3 0.0 copy-start.1
  5.4 1.1 %copy-done.1 = f32[5,16,8,256]{3,2,1,0:T(8,128)S(1)} copy-done((f32[5,16,8,256]{3,2,1,0:T(8,128)S(1)}, f32[5,16,8,256]{3,2,1,0:T(8,128)}, u32[]{:S(2)}) %copy-start.1) | copy-done | bytes 655384
  6.4 0.4 shard_map.68
  6.9 0.0 collective-permute-done.rad_ref.refs_3_
  6.9 0.0 copy-start.4
  6.9 0.7 %copy-done.4 = s32[256]{0:T(256)S(1)} copy-done((s32[256]{0:T(256)S(1)}, s32[256]{0:T(256)}, u32[]{:S(2)}) %copy-start.4) | copy-done | bytes 1048
  7.6 0.0 copy-start.3
  7.6 1.7 %shard_map.71 = (f32[5,40,256]{2,1,0:T(8,128)S(1)}, f32[5,40,256]{2,1,0:T(8,128)S(1)}) custom-call(s32[1,256]{1,0:T(1,128)S(1)} %bitcast.5, f32[5,16,8,256]{3,2,1,0:T(8,128)S(1)} %get-tuple-element.13.q_ref.refs_1_.refs_2_, f32[5,16,8,256]{3,2,1,0:T(8,128)S(1)} %get-tuple-element.14.qp_ref.refs_2_, f32[5,8,256]{2,1,0:T(8,128)S(1)} %collective-permute-done.rad_ref.refs_3_), custom_call_target="tpu_custom_call" | custom-call | tf_op jit(solution)/shard_map/pallas_call | solution.py:452
  9.3 2.6 %collective-permute-start.2 = (f32[5,40,256]{2,1,0:T(8,128)S(1)}, f32[5,40,256]{2,1,0:T(8,128)S(1)}, u32[]{:S(2)}, u32[]{:S(2)}) collective-permute-start(f32[5,40,256]{2,1,0:T(8,128)S(1)} %get-tuple-element.18), channel_id=1, source_target_pairs={{0,254},{2,4},{4,2},{6,8},{8,6},{10,12},{12,10},{14,16},{16,14},{1... | collective-permute-start | bytes 614408 | tf_op jit(solution)/shard_map/ppermute | solution.py:461
  11.8 8.0 %collective-permute-start.3 = (f32[5,40,256]{2,1,0:T(8,128)S(1)}, f32[5,40,256]{2,1,0:T(8,128)S(1)}, u32[]{:S(2)}, u32[]{:S(2)}) collective-permute-start(f32[5,40,256]{2,1,0:T(8,128)S(1)} %get-tuple-element.19), channel_id=1, source_target_pairs={{0,2},{2,0},{4,6},{6,4},{8,10},{10,8},{12,14},{14,12},{16,18},{18,... | collective-permute-start | bytes 614408 | tf_op jit(solution)/shard_map/ppermute | solution.py:460
  19.9 0.0 copy-done.3
  19.9 2.0 %shard_map.70 = (f32[5,16,8,256]{3,2,1,0:T(8,128)S(1)}, f32[5,8,256]{2,1,0:T(8,128)S(1)}, f32[5,16,8,256]{3,2,1,0:T(8,128)S(1)}) custom-call(f32[6,34]{1,0:T(8,128)S(1)} %copy-done.3, s32[1,256]{1,0:T(1,128)S(1)} %bitcast.6, f32[5,16,8,256]{3,2,1,0:T(8,128)S(1)} %get-tuple-element.13.q_ref.refs_1_.refs_2_, ...), custom_call_target="tpu_custom_call" | custom-call | flops 10000000 | bytes 3500000 | tf_op jit(solution)/shard_map/pallas_call | solution.py:462
  21.8 0.1 collective-permute-start.1
  21.9 2.8 %collective-permute-done.1.refs_6_ = f32[5,8,256]{2,1,0:T(8,128)S(1)} collective-permute-done((f32[5,8,256]{2,1,0:T(8,128)S(1)}, f32[5,8,256]{2,1,0:T(8,128)S(1)}, u32[]{:S(2)}, u32[]{:S(2)}) %collective-permute-start.1) | collective-permute-done | bytes 40992 | tf_op jit(solution)/shard_map/ppermute | solution.py:471
  24.8 0.0 collective-permute-done.2.refs_7_
  24.8 0.0 collective-permute-done.3.refs_8_
  24.8 2.9 %shard_map.72 = (f32[5,16,8,256]{3,2,1,0:T(8,128)S(1)}, f32[512,128]{1,0:T(8,128)S(1)}) custom-call(f32[6,34]{1,0:T(8,128)S(1)} %copy-done.3, s32[1,256]{1,0:T(1,128)S(1)} %bitcast.7, f32[5,16,8,256]{3,2,1,0:T(8,128)S(1)} %get-tuple-element.13.q_ref.refs_1_.refs_2_, f32[5,8,256]{2,1,0:T(8,128)S(1)} %collective-permute-done.rad_ref.refs_3_, ...), custom_call_target="tpu_custom_call" | custom-call | tf_op jit(solution)/shard_map/pallas_call | solution.py:472
  27.6 0.0 copy-start.2
  27.7 24.7 %all_to_all.5 = f32[128,4,128]{2,1,0:T(4,128)S(1)} all-to-all(f32[128,4,128]{2,1,0:T(4,128)S(1)} %bitcast.4), channel_id=1, replica_groups=mesh['theta'=128,'rad'=2] {'theta'}, dimensions={0} | all-to-all | bytes 524288 | tf_op jit(solution)/shard_map/all_to_all | solution.py:484
  52.4 0.0 copy-done.2
  52.4 1.5 %shard_map.73 = (f32[2,16,256]{2,1,0:T(8,128)}, f32[5,16,8,256]{3,2,1,0:T(8,128)}) custom-call(f32[512,128]{1,0:T(8,128)S(1)} %bitcast.3, f32[1024,128]{1,0:T(8,128)S(1)} %copy-done.2, f32[5,16,8,256]{3,2,1,0:T(8,128)S(1)} %get-tuple-element.21.flow_ref), custom_call_target="tpu_custom_call" | custom-call | tf_op jit(solution)/shard_map/pallas_call | solution.py:485
Async XLA Ops:
  2.0 4.8 %collective-permute-start = (f32[5,8,256]{2,1,0:T(8,128)}, f32[5,8,256]{2,1,0:T(8,128)S(1)}, u32[]{:S(2)}, u32[]{:S(2)}) collective-permute-start(f32[5,8,256]{2,1,0:T(8,128)} %shard_map.69), channel_id=1, source_target_pairs={{0,1},{1,0},{2,3},{3,2},{4,5},{5,4},{6,7},{7,6},{8,9},{9,8},{10,11... | collective-permute-start | bytes 122888 | tf_op jit(solution)/shard_map/ppermute | solution.py:431
  4.3 1.1 %copy-start = (f32[5,16,8,256]{3,2,1,0:T(8,128)S(1)}, f32[5,16,8,256]{3,2,1,0:T(8,128)}, u32[]{:S(2)}) copy-start(f32[5,16,8,256]{3,2,1,0:T(8,128)} %q_ref.3) | copy-start | bytes 1966084
  5.3 1.1 %copy-start.1 = (f32[5,16,8,256]{3,2,1,0:T(8,128)S(1)}, f32[5,16,8,256]{3,2,1,0:T(8,128)}, u32[]{:S(2)}) copy-start(f32[5,16,8,256]{3,2,1,0:T(8,128)} %qp_ref.1) | copy-start | bytes 1966084
  6.9 0.7 %copy-start.4 = (s32[256]{0:T(256)S(1)}, s32[256]{0:T(256)}, u32[]{:S(2)}) copy-start(s32[256]{0:T(256)} %param.7) | copy-start | bytes 3076
  7.6 12.3 %copy-start.3 = (f32[6,34]{1,0:T(8,128)S(1)}, f32[6,34]{1,0:T(8,128)}, u32[]{:S(2)}) copy-start(f32[6,34]{1,0:T(8,128)} %constant.4.clone.table_ref.refs_0_) | copy-start | bytes 2452
  9.3 15.5 %collective-permute-start.2 = (f32[5,40,256]{2,1,0:T(8,128)S(1)}, f32[5,40,256]{2,1,0:T(8,128)S(1)}, u32[]{:S(2)}, u32[]{:S(2)}) collective-permute-start(f32[5,40,256]{2,1,0:T(8,128)S(1)} %get-tuple-element.18), channel_id=1, source_target_pairs={{0,254},{2,4},{4,2},{6,8},{8,6},{10,12},{12,10},{14,16},{16,14},{1... | collective-permute-start | bytes 614408 | tf_op jit(solution)/shard_map/ppermute | solution.py:461
  11.8 12.9 %collective-permute-start.3 = (f32[5,40,256]{2,1,0:T(8,128)S(1)}, f32[5,40,256]{2,1,0:T(8,128)S(1)}, u32[]{:S(2)}, u32[]{:S(2)}) collective-permute-start(f32[5,40,256]{2,1,0:T(8,128)S(1)} %get-tuple-element.19), channel_id=1, source_target_pairs={{0,2},{2,0},{4,6},{6,4},{8,10},{10,8},{12,14},{14,12},{16,18},{18,... | collective-permute-start | bytes 614408 | tf_op jit(solution)/shard_map/ppermute | solution.py:460
  21.8 2.9 %collective-permute-start.1 = (f32[5,8,256]{2,1,0:T(8,128)S(1)}, f32[5,8,256]{2,1,0:T(8,128)S(1)}, u32[]{:S(2)}, u32[]{:S(2)}) collective-permute-start(f32[5,8,256]{2,1,0:T(8,128)S(1)} %get-tuple-element.17), channel_id=1, source_target_pairs={{0,1},{1,0},{2,3},{3,2},{4,5},{5,4},{6,7},{7,6},{8,9},{9,8},{10,11... | collective-permute-start | bytes 122888 | tf_op jit(solution)/shard_map/ppermute | solution.py:471
  27.6 24.7 %copy-start.2 = (f32[1024,128]{1,0:T(8,128)S(1)}, f32[1024,128]{1,0:T(8,128)}, u32[]{:S(2)}) copy-start(f32[1024,128]{1,0:T(8,128)} %constant.5.clone.basis_ref) | copy-start | bytes 1572868

commit v4 on v3

--- a/solution.py
+++ b/solution.py
@@ -15,6 +15,7 @@
 BAND = 16
 SECTOR = 8
 AXIAL = 256
+LOAD_VMEM = 55_000_000
 F32 = jnp.float32
 ALL = range(5)
 
@@ -96,13 +97,6 @@
     return jnp.where(band == 0, at_low, at_high)
 
 
-def rad_kernel(q_ref, rad_ref, sem):
-    near = edge_row(lax.axis_index("rad"), BAND - 1, 0)
-    copy = pltpu.make_async_copy(q_ref.at[:, near], rad_ref, sem)
-    copy.start()
-    copy.wait()
-
-
 MIRROR = (1.0, 1.0, -1.0, 1.0, 1.0)
 
 
@@ -126,10 +120,12 @@
         self.a_h = 0.25 * self.inv_h
 
 
-def load_kernel(q_ref, qp_ref, q_out_ref, qp_out_ref, sems):
+def load_kernel(q_ref, qp_ref, near_ref, q_out_ref, qp_out_ref, sems):
+    edge = edge_row(lax.axis_index("rad"), BAND - 1, 0)
     copies = [
-        pltpu.make_async_copy(q_ref, q_out_ref, sems.at[0]),
-        pltpu.make_async_copy(qp_ref, qp_out_ref, sems.at[1]),
+        pltpu.make_async_copy(q_ref.at[:, edge], near_ref, sems.at[0]),
+        pltpu.make_async_copy(q_ref, q_out_ref, sems.at[1]),
+        pltpu.make_async_copy(qp_ref, qp_out_ref, sems.at[2]),
     ]
     for copy in copies:
         copy.start()
@@ -137,24 +133,24 @@
         copy.wait()
 
 
-def pack_kernel(total_rows, circle, blade_ref, q_ref, qp_ref, rad_ref, other_ref, core_ref, ce):
-    odd = lax.axis_index("theta") % 2 == 1
+def edge_kernel(total_rows, circle, blade_ref, q_ref, qp_ref, edges_ref, ce):
     band = lax.axis_index("rad")
     low = band == 0
     geo = Columns(band * BAND, total_rows, circle)
     blade = blades(blade_ref, BAND)
     lane = lax.broadcasted_iota(jnp.int32, (BAND, AXIAL), 1)
-    sides = []
+    row = lax.broadcasted_iota(jnp.int32, (BAND, AXIAL), 0)
+    below_scale = jnp.where((row == 0) & jnp.logical_not(low), 0.0, 0.25 * geo.inv_r * geo.inner)
+    above_scale = jnp.where((row == BAND - 1) & low, 0.0, 0.25 * geo.inv_r * geo.outer)
     for side in (0, 1):
         at, inner = (0, 1) if side == 0 else (SECTOR - 1, SECTOR - 2)
         edge = [q_ref[v, :, at, :] for v in ALL]
         second = [q_ref[v, :, inner, :] for v in ALL]
         half_source = [10.0 * edge[v] - 2.5 * qp_ref[v, :, at, :] for v in ALL]
-        corner = [rad_ref[v, at : at + 1, :] for v in ALL]
         for v in ALL:
             ce[v, side, 8:24] = edge[v]
-            ce[v, side, 7:8] = jnp.where(low, MIRROR[v] * edge[v][0:1], corner[v])
-            ce[v, side, 24:25] = jnp.where(low, corner[v], MIRROR[v] * edge[v][BAND - 1 : BAND])
+            ce[v, side, 7:8] = MIRROR[v] * edge[v][0:1]
+            ce[v, side, 24:25] = MIRROR[v] * edge[v][BAND - 1 : BAND]
         below = [ce[v, side, 7:23] for v in ALL]
         above = [ce[v, side, 9:25] for v in ALL]
         prim = primitives(edge)
@@ -172,19 +168,49 @@
             prim,
             half_source,
             axial_difference(edge, prim, lane),
-            [(0.25 * geo.inv_r) * (geo.outer * g_out[v] - geo.inner * g_in[v]) for v in ALL],
+            [above_scale * g_out[v] - below_scale * g_in[v] for v in ALL],
             swirl,
             geo.inv_r,
             geo.inv_h,
             geo.spin_r,
             *blade,
         )
-        sides.append((edge, part, [jnp.broadcast_to(x, (8, AXIAL)) for x in corner]))
-    for n, (a, b) in enumerate(zip(*sides)):
         for v in ALL:
-            rows = slice(BAND * n, BAND * n + a[v].shape[0])
-            other_ref[v, rows] = jnp.where(odd, b[v], a[v])
-            core_ref[v, rows] = jnp.where(odd, a[v], b[v])
+            edges_ref[v, side, 0:16] = edge[v]
+            edges_ref[v, side, 16:32] = part[v]
+
+
+def step_weight(prim, inv_h):
+    ux, ur, ut, _, sound = prim
+    return 1.0 / (jnp.abs(ux) + jnp.abs(ur) + jnp.abs(ut) * inv_h + sound * (2.0 + inv_h) + 7.5)
+
+
+def pack_kernel(table_ref, edges_ref, rad_ref, core_ref, other_ref):
+    odd = lax.axis_index("theta") % 2 == 1
+    band = lax.axis_index("rad")
+    low = band == 0
+    edge_at = edge_row(band, BAND - 1, 0)
+    g = band * BAND + edge_at + 1
+    scale = jnp.where(low, -table_ref[0, g], table_ref[1, g])
+    sides = []
+    for side in (0, 1):
+        at = 0 if side == 0 else SECTOR - 1
+        edge = [edges_ref[v, side, pl.ds(edge_at, 1), :] for v in ALL]
+        corner = [rad_ref[v, at : at + 1, :] for v in ALL]
+        prim = primitives(edge)
+        a, b = flux(edge, prim, 2), flux(corner, primitives(corner), 2)
+        below = [jnp.where(low, edge[v], corner[v]) for v in ALL]
+        above = [jnp.where(low, corner[v], edge[v]) for v in ALL]
+        pick = lambda x, y: ([jnp.where(low, p, r) for p, r in zip(x[0], y[0])], jnp.where(low, x[1], y[1]))
+        g_face = face(below, pick(a, b), above, pick(b, a))
+        weight = scale * step_weight(prim, table_ref[4, g])
+        sides.append((corner, [weight * x for x in g_face]))
+    for v in ALL:
+        for ref, flip in ((core_ref, jnp.logical_not(odd)), (other_ref, odd)):
+            ref[v, 0:32] = jnp.where(flip, edges_ref[v, 1], edges_ref[v, 0])
+            at = 16 + edge_at
+            ref[v, pl.ds(at, 1), :] = ref[v, pl.ds(at, 1), :] + jnp.where(flip, sides[1][1][v], sides[0][1][v])
+            ref[v, 32:40] = jnp.broadcast_to(jnp.where(flip, sides[1][0][v], sides[0][0][v]), (8, AXIAL))
 
 
 def row_step(g, table_ref, q, prim, half_source, g_in, g_out, ends, masks, blade):
@@ -300,10 +326,6 @@
     geo = Columns(first_row, total_rows, circle)
     g_near = first_row + near_at
 
-    def weight(prim, inv_h):
-        ux, ur, ut, _, sound = prim
-        return 1.0 / (jnp.abs(ux) + jnp.abs(ur) + jnp.abs(ut) * inv_h + sound * (2.0 + inv_h) + 7.5)
-
     for side in (0, 1):
         use_core = odd if side == 0 else jnp.logical_not(odd)
         at = 0 if side == 0 else SECTOR - 1
@@ -320,15 +342,15 @@
         own = [q_ref[v, :, at, :] for v in ALL]
         own_prim, near_prim = primitives(own), primitives(near)
         shared = ordered(near, near_prim, own, own_prim)
-        own_scale = (sign * geo.a_h) * weight(own_prim, geo.inv_h)
-        near_scale = (-sign * geo.a_h) * weight(near_prim, geo.inv_h)
+        own_scale = (sign * geo.a_h) * step_weight(own_prim, geo.inv_h)
+        near_scale = (-sign * geo.a_h) * step_weight(near_prim, geo.inv_h)
         own_next = [p1_ref[v, :, at, :] + own_scale * shared[v] for v in ALL]
         near_next = [near_part[v] + near_scale * shared[v] for v in ALL]
 
         edge = [rad_ref[v, at : at + 1, :] for v in ALL]
         edge_prim = primitives(edge)
         corner_face = ordered(corner, primitives(corner), edge, edge_prim)
-        corner_scale = (sign * table_ref[2, g_near]) * weight(edge_prim, table_ref[4, g_near])
+        corner_scale = (sign * table_ref[2, g_near]) * step_weight(edge_prim, table_ref[4, g_near])
 
         faces = ordered(near_next, primitives(near_next), own_next, primitives(own_next))
         for v in ALL:
@@ -422,41 +444,41 @@
     hbm = pl.BlockSpec(memory_space=pltpu.HBM)
     swap = [(0, 1), (1, 0)]
 
-    def pack(*refs):
-        pack_kernel(bands * BAND, circle, *refs)
+    def edges(*refs):
+        edge_kernel(bands * BAND, circle, *refs)
 
     def final(*refs):
         final_kernel(bands * BAND, circle, *refs)
 
-    rad_in = lax.ppermute(
-        pl.pallas_call(
-            rad_kernel,
-            out_shape=shaped(5, SECTOR, AXIAL),
-            in_specs=[hbm],
-            out_specs=vmem(),
-            scratch_shapes=[pltpu.SemaphoreType.DMA],
-            compiler_params=limit(63.5),
-        )(q_level),
-        "rad",
-        swap,
-    )
-    q_level, q_prev = pl.pallas_call(
+    near, q_level, q_prev = pl.pallas_call(
         load_kernel,
-        out_shape=[shaped(5, BAND, SECTOR, AXIAL)] * 2,
+        out_shape=[
+            shaped(5, SECTOR, AXIAL),
+            shaped(5, BAND, SECTOR, AXIAL),
+            shaped(5, BAND, SECTOR, AXIAL),
+        ],
         in_specs=[hbm] * 2,
-        out_specs=[vmem()] * 2,
-        scratch_shapes=[pltpu.SemaphoreType.DMA((2,))],
-        compiler_params=limit(2),
-        cost_estimate=pl.CostEstimate(flops=0, bytes_accessed=3_000_000, transcendentals=0),
+        out_specs=[vmem()] * 3,
+        scratch_shapes=[pltpu.SemaphoreType.DMA((3,))],
+        compiler_params=pltpu.CompilerParams(vmem_limit_bytes=LOAD_VMEM),
     )(q_level, q_prev)
-    other_out, core_out = pl.pallas_call(
-        pack,
-        out_shape=[shaped(5, 40, AXIAL)] * 2,
-        in_specs=[vmem()] * 4,
-        out_specs=[vmem()] * 2,
+    rad_in = lax.ppermute(near, "rad", swap)
+    edge_columns = pl.pallas_call(
+        edges,
+        out_shape=shaped(5, 2, 32, AXIAL),
+        in_specs=[vmem()] * 3,
+        out_specs=vmem(),
         scratch_shapes=[pltpu.VMEM((5, 2, 32, AXIAL), F32)],
         compiler_params=limit(4),
-    )(blade, q_level, q_prev, rad_in)
+        cost_estimate=pl.CostEstimate(flops=5_000_000, bytes_accessed=2_000_000, transcendentals=50_000),
+    )(blade, q_level, q_prev)
+    core_out, other_out = pl.pallas_call(
+        pack_kernel,
+        out_shape=[shaped(5, 40, AXIAL)] * 2,
+        in_specs=[smem] + [vmem()] * 2,
+        out_specs=[vmem()] * 2,
+        compiler_params=limit(4),
+    )(table, edge_columns, rad_in)
     core_in = lax.ppermute(core_out, "theta", core)
     other_in = lax.ppermute(other_out, "theta", other)
     part, edge, half_source = pl.pallas_call(

time: 54.1 us -> 51.9 us (0.959)
  local copies, waits for them, and re-layouts: 2.86 us -> 0.69 us
    unnamed x10 -> x6, local copies, waits for them, and re-layouts: 2.86 us -> 0.69 us
  transfers between devices with their start and end apart: 4 -> 4, of which waited for: 1 -> 1; matrix products, arithmetic and copies ran while one was open for 0% -> 0% of each run, Pallas kernels for 4% -> 7%
where the time goes in v4:
time: 51.9 us; the launch traced here: 51.7 us
  blocking collectives  24.7 us (48%)
  starting transfers between devices  12.9 us (25%)
  Pallas kernels  9.92 us (19%)
  waiting for transfers between devices  2.85 us (5%)
  local copies, waits for them, and re-layouts  0.69 us (1%)
  between operations  0.69 us (1%)
    all_to_all x1, blocking collectives, per_device(): lax.all_to_all(send.reshape(sectors, 4, 128), 'theta', split_axis=0, conc...  24.7 us
    ppermute x1, starting transfers between devices, per_device(): core_in = lax.ppermute(core_out, 'theta', core)  7.89 us
    pallas_call x1, Pallas kernels, per_device(): pl.pallas_call(final, out_shape=[shaped(5, BAND, SECTOR, AXIAL), shaped(2...  2.87 us
    ppermute x1, waiting for transfers between devices, per_device(): next_in = lax.ppermute(edge, 'rad', swap)  2.84 us
    ppermute x1, starting transfers between devices, per_device(): other_in = lax.ppermute(other_out, 'theta', other)  2.7 us
    ppermute x1, starting transfers between devices, per_device(): rad_in = lax.ppermute(near, 'rad', swap)  2.21 us
    pallas_call x1, Pallas kernels, per_device(): pl.pallas_call(early_kernel, out_shape=[shaped(5, BAND, SECTOR, AXIAL), s...  1.96 us
    pallas_call x1, Pallas kernels, per_device(): pl.pallas_call(edges, out_shape=shaped(5, 2, 32, AXIAL), in_specs=[vmem()...  1.59 us
  transfers between devices with their start and end apart: 4, of which 1 were waited for; matrix products, arithmetic and copies ran while one was open for 0% of the time, Pallas kernels for 7%

profile of v4, /device:TPU:1, one launch (start us, length us, event | category | flops | bytes accessed | tf_op | source)
XLA Modules:
  0.0 51.7 jit_solution(5704783366480399612)
XLA Ops:
  0.6 1.3 %shard_map.68 = (f32[5,8,256]{2,1,0:T(8,128)S(1)}, f32[5,16,8,256]{3,2,1,0:T(8,128)S(1)}, f32[5,16,8,256]{3,2,1,0:T(8,128)S(1)}) custom-call(f32[5,16,8,256]{3,2,1,0:T(8,128)} %q_ref.1, f32[5,16,8,256]{3,2,1,0:T(8,128)} %qp_ref.1), custom_call_target="tpu_custom_call" | custom-call | tf_op jit(solution)/shard_map/pallas_call | solution.py:453
  2.0 2.2 %collective-permute-start = (f32[5,8,256]{2,1,0:T(8,128)S(1)}, f32[5,8,256]{2,1,0:T(8,128)S(1)}, u32[]{:S(2)}, u32[]{:S(2)}) collective-permute-start(f32[5,8,256]{2,1,0:T(8,128)S(1)} %get-tuple-element.15), channel_id=1, source_target_pairs={{0,1},{1,0},{2,3},{3,2},{4,5},{5,4},{6,7},{7,6},{8,9},{9,8},{10,11... | collective-permute-start | bytes 122888 | tf_op jit(solution)/shard_map/ppermute | solution.py:465
  4.2 0.0 copy-start.2
  4.2 0.7 %copy-done.2 = s32[256]{0:T(256)S(1)} copy-done((s32[256]{0:T(256)S(1)}, s32[256]{0:T(256)}, u32[]{:S(2)}) %copy-start.2) | copy-done | bytes 1048
  4.9 0.0 copy-start.1
  4.9 1.6 %shard_map.70.edges_ref = f32[5,2,32,256]{3,2,1,0:T(8,128)S(1)} custom-call(s32[1,256]{1,0:T(1,128)S(1)} %bitcast.5, f32[5,16,8,256]{3,2,1,0:T(8,128)S(1)} %get-tuple-element.14.q_ref.refs_1_.refs_2_, f32[5,16,8,256]{3,2,1,0:T(8,128)S(1)} %get-tuple-element.16.qp_ref.refs_2_), custom_call_target="tpu_custom_call" | custom-call | flops 5000000 | bytes 2000000 | tf_op jit(solution)/shard_map/pallas_call | solution.py:466
  6.5 0.0 collective-permute-done.rad_ref.refs_3_
  6.5 0.0 copy-done.1
  6.5 0.7 %shard_map.71 = (f32[5,40,256]{2,1,0:T(8,128)S(1)}, f32[5,40,256]{2,1,0:T(8,128)S(1)}) custom-call(f32[6,34]{1,0:T(8,128)S(1)} %copy-done.1, f32[5,2,32,256]{3,2,1,0:T(8,128)S(1)} %shard_map.70.edges_ref, f32[5,8,256]{2,1,0:T(8,128)S(1)} %collective-permute-done.rad_ref.refs_3_), custom_call_target="tpu_custom_call" | custom-call | tf_op jit(solution)/shard_map/pallas_call | solution.py:475
  7.2 2.7 %collective-permute-start.2 = (f32[5,40,256]{2,1,0:T(8,128)S(1)}, f32[5,40,256]{2,1,0:T(8,128)S(1)}, u32[]{:S(2)}, u32[]{:S(2)}) collective-permute-start(f32[5,40,256]{2,1,0:T(8,128)S(1)} %get-tuple-element.20), channel_id=1, source_target_pairs={{0,254},{2,4},{4,2},{6,8},{8,6},{10,12},{12,10},{14,16},{16,14},{1... | collective-permute-start | bytes 614408 | tf_op jit(solution)/shard_map/ppermute | solution.py:483
  9.9 7.9 %collective-permute-start.3 = (f32[5,40,256]{2,1,0:T(8,128)S(1)}, f32[5,40,256]{2,1,0:T(8,128)S(1)}, u32[]{:S(2)}, u32[]{:S(2)}) collective-permute-start(f32[5,40,256]{2,1,0:T(8,128)S(1)} %get-tuple-element.21), channel_id=1, source_target_pairs={{0,2},{2,0},{4,6},{6,4},{8,10},{10,8},{12,14},{14,12},{16,18},{18,... | collective-permute-start | bytes 614408 | tf_op jit(solution)/shard_map/ppermute | solution.py:482
  17.8 2.0 %shard_map.69 = (f32[5,16,8,256]{3,2,1,0:T(8,128)S(1)}, f32[5,8,256]{2,1,0:T(8,128)S(1)}, f32[5,16,8,256]{3,2,1,0:T(8,128)S(1)}) custom-call(f32[6,34]{1,0:T(8,128)S(1)} %copy-done.1, s32[1,256]{1,0:T(1,128)S(1)} %bitcast.6, f32[5,16,8,256]{3,2,1,0:T(8,128)S(1)} %get-tuple-element.14.q_ref.refs_1_.refs_2_, ...), custom_call_target="tpu_custom_call" | custom-call | flops 10000000 | bytes 3500000 | tf_op jit(solution)/shard_map/pallas_call | solution.py:484
  19.7 0.1 collective-permute-start.1
  19.8 2.8 %collective-permute-done.1.refs_6_ = f32[5,8,256]{2,1,0:T(8,128)S(1)} collective-permute-done((f32[5,8,256]{2,1,0:T(8,128)S(1)}, f32[5,8,256]{2,1,0:T(8,128)S(1)}, u32[]{:S(2)}, u32[]{:S(2)}) %collective-permute-start.1) | collective-permute-done | bytes 40992 | tf_op jit(solution)/shard_map/ppermute | solution.py:493
  22.7 0.0 collective-permute-done.2.refs_7_
  22.7 0.0 collective-permute-done.3.refs_8_
  22.7 2.9 %shard_map.72 = (f32[5,16,8,256]{3,2,1,0:T(8,128)S(1)}, f32[512,128]{1,0:T(8,128)S(1)}) custom-call(f32[6,34]{1,0:T(8,128)S(1)} %copy-done.1, s32[1,256]{1,0:T(1,128)S(1)} %bitcast.7, f32[5,16,8,256]{3,2,1,0:T(8,128)S(1)} %get-tuple-element.14.q_ref.refs_1_.refs_2_, f32[5,8,256]{2,1,0:T(8,128)S(1)} %collective-permute-done.rad_ref.refs_3_, ...), custom_call_target="tpu_custom_call" | custom-call | tf_op jit(solution)/shard_map/pallas_call | solution.py:494
  25.6 0.0 copy-start
  25.6 24.7 %all_to_all.5 = f32[128,4,128]{2,1,0:T(4,128)S(1)} all-to-all(f32[128,4,128]{2,1,0:T(4,128)S(1)} %bitcast.4), channel_id=1, replica_groups=mesh['theta'=128,'rad'=2] {'theta'}, dimensions={0} | all-to-all | bytes 524288 | tf_op jit(solution)/shard_map/all_to_all | solution.py:506
  50.3 0.0 copy-done
  50.3 1.5 %shard_map.73 = (f32[2,16,256]{2,1,0:T(8,128)}, f32[5,16,8,256]{3,2,1,0:T(8,128)}) custom-call(f32[512,128]{1,0:T(8,128)S(1)} %bitcast.3, f32[1024,128]{1,0:T(8,128)S(1)} %copy-done, f32[5,16,8,256]{3,2,1,0:T(8,128)S(1)} %get-tuple-element.23.flow_ref), custom_call_target="tpu_custom_call" | custom-call | tf_op jit(solution)/shard_map/pallas_call | solution.py:507
Async XLA Ops:
  2.0 4.5 %collective-permute-start = (f32[5,8,256]{2,1,0:T(8,128)S(1)}, f32[5,8,256]{2,1,0:T(8,128)S(1)}, u32[]{:S(2)}, u32[]{:S(2)}) collective-permute-start(f32[5,8,256]{2,1,0:T(8,128)S(1)} %get-tuple-element.15), channel_id=1, source_target_pairs={{0,1},{1,0},{2,3},{3,2},{4,5},{5,4},{6,7},{7,6},{8,9},{9,8},{10,11... | collective-permute-start | bytes 122888 | tf_op jit(solution)/shard_map/ppermute | solution.py:465
  4.2 0.7 %copy-start.2 = (s32[256]{0:T(256)S(1)}, s32[256]{0:T(256)}, u32[]{:S(2)}) copy-start(s32[256]{0:T(256)} %param.7) | copy-start | bytes 3076
  4.9 1.6 %copy-start.1 = (f32[6,34]{1,0:T(8,128)S(1)}, f32[6,34]{1,0:T(8,128)}, u32[]{:S(2)}) copy-start(f32[6,34]{1,0:T(8,128)} %constant.4.clone.table_ref.refs_0_) | copy-start | bytes 2452
  7.2 15.5 %collective-permute-start.2 = (f32[5,40,256]{2,1,0:T(8,128)S(1)}, f32[5,40,256]{2,1,0:T(8,128)S(1)}, u32[]{:S(2)}, u32[]{:S(2)}) collective-permute-start(f32[5,40,256]{2,1,0:T(8,128)S(1)} %get-tuple-element.20), channel_id=1, source_target_pairs={{0,254},{2,4},{4,2},{6,8},{8,6},{10,12},{12,10},{14,16},{16,14},{1... | collective-permute-start | bytes 614408 | tf_op jit(solution)/shard_map/ppermute | solution.py:483
  9.9 12.8 %collective-permute-start.3 = (f32[5,40,256]{2,1,0:T(8,128)S(1)}, f32[5,40,256]{2,1,0:T(8,128)S(1)}, u32[]{:S(2)}, u32[]{:S(2)}) collective-permute-start(f32[5,40,256]{2,1,0:T(8,128)S(1)} %get-tuple-element.21), channel_id=1, source_target_pairs={{0,2},{2,0},{4,6},{6,4},{8,10},{10,8},{12,14},{14,12},{16,18},{18,... | collective-permute-start | bytes 614408 | tf_op jit(solution)/shard_map/ppermute | solution.py:482
  19.7 2.9 %collective-permute-start.1 = (f32[5,8,256]{2,1,0:T(8,128)S(1)}, f32[5,8,256]{2,1,0:T(8,128)S(1)}, u32[]{:S(2)}, u32[]{:S(2)}) collective-permute-start(f32[5,8,256]{2,1,0:T(8,128)S(1)} %get-tuple-element.19), channel_id=1, source_target_pairs={{0,1},{1,0},{2,3},{3,2},{4,5},{5,4},{6,7},{7,6},{8,9},{9,8},{10,11... | collective-permute-start | bytes 122888 | tf_op jit(solution)/shard_map/ppermute | solution.py:493
  25.6 24.7 %copy-start = (f32[1024,128]{1,0:T(8,128)S(1)}, f32[1024,128]{1,0:T(8,128)}, u32[]{:S(2)}) copy-start(f32[1024,128]{1,0:T(8,128)} %constant.5.clone.basis_ref) | copy-start | bytes 1572868

commit v5 on v4

--- a/solution.py
+++ b/solution.py
@@ -15,6 +15,7 @@
 BAND = 16
 SECTOR = 8
 AXIAL = 256
+RAD_VMEM = 56_200_000
 LOAD_VMEM = 55_000_000
 F32 = jnp.float32
 ALL = range(5)
@@ -120,12 +121,16 @@
         self.a_h = 0.25 * self.inv_h
 
 
-def load_kernel(q_ref, qp_ref, near_ref, q_out_ref, qp_out_ref, sems):
-    edge = edge_row(lax.axis_index("rad"), BAND - 1, 0)
+def rad_kernel(q_ref, near_ref, sem):
+    copy = pltpu.make_async_copy(q_ref.at[:, edge_row(lax.axis_index("rad"), BAND - 1, 0)], near_ref, sem)
+    copy.start()
+    copy.wait()
+
+
+def load_kernel(q_ref, qp_ref, q_out_ref, qp_out_ref, sems):
     copies = [
-        pltpu.make_async_copy(q_ref.at[:, edge], near_ref, sems.at[0]),
-        pltpu.make_async_copy(q_ref, q_out_ref, sems.at[1]),
-        pltpu.make_async_copy(qp_ref, qp_out_ref, sems.at[2]),
+        pltpu.make_async_copy(q_ref, q_out_ref, sems.at[0]),
+        pltpu.make_async_copy(qp_ref, qp_out_ref, sems.at[1]),
     ]
     for copy in copies:
         copy.start()
@@ -133,7 +138,7 @@
         copy.wait()
 
 
-def edge_kernel(total_rows, circle, blade_ref, q_ref, qp_ref, edges_ref, ce):
+def edge_kernel(total_rows, circle, blade_ref, q_ref, qp_ref, edges_ref, ce, taken):
     band = lax.axis_index("rad")
     low = band == 0
     geo = Columns(band * BAND, total_rows, circle)
@@ -144,11 +149,15 @@
     above_scale = jnp.where((row == BAND - 1) & low, 0.0, 0.25 * geo.inv_r * geo.outer)
     for side in (0, 1):
         at, inner = (0, 1) if side == 0 else (SECTOR - 1, SECTOR - 2)
-        edge = [q_ref[v, :, at, :] for v in ALL]
-        second = [q_ref[v, :, inner, :] for v in ALL]
-        half_source = [10.0 * edge[v] - 2.5 * qp_ref[v, :, at, :] for v in ALL]
         for v in ALL:
-            ce[v, side, 8:24] = edge[v]
+            ce[v, side, 8:24] = q_ref[v, :, at, :]
+            taken[v, side, 0] = q_ref[v, :, inner, :]
+            taken[v, side, 1] = qp_ref[v, :, at, :]
+    for side in (0, 1):
+        edge = [ce[v, side, 8:24] for v in ALL]
+        second = [taken[v, side, 0] for v in ALL]
+        half_source = [10.0 * edge[v] - 2.5 * taken[v, side, 1] for v in ALL]
+        for v in ALL:
             ce[v, side, 7:8] = MIRROR[v] * edge[v][0:1]
             ce[v, side, 24:25] = MIRROR[v] * edge[v][BAND - 1 : BAND]
         below = [ce[v, side, 7:23] for v in ALL]
@@ -185,7 +194,7 @@
     return 1.0 / (jnp.abs(ux) + jnp.abs(ur) + jnp.abs(ut) * inv_h + sound * (2.0 + inv_h) + 7.5)
 
 
-def pack_kernel(table_ref, edges_ref, rad_ref, core_ref, other_ref):
+def pack_kernel(table_ref, edges_ref, rad_ref, own_ref, core_ref, other_ref):
     odd = lax.axis_index("theta") % 2 == 1
     band = lax.axis_index("rad")
     low = band == 0
@@ -206,11 +215,14 @@
         weight = scale * step_weight(prim, table_ref[4, g])
         sides.append((corner, [weight * x for x in g_face]))
     for v in ALL:
+        for side in (0, 1):
+            own_ref[v, side] = edges_ref[v, side, 16:32]
+            own_ref[v, side, pl.ds(edge_at, 1), :] = edges_ref[v, side, pl.ds(16 + edge_at, 1), :] + sides[side][1][v]
         for ref, flip in ((core_ref, jnp.logical_not(odd)), (other_ref, odd)):
-            ref[v, 0:32] = jnp.where(flip, edges_ref[v, 1], edges_ref[v, 0])
-            at = 16 + edge_at
-            ref[v, pl.ds(at, 1), :] = ref[v, pl.ds(at, 1), :] + jnp.where(flip, sides[1][1][v], sides[0][1][v])
-            ref[v, 32:40] = jnp.broadcast_to(jnp.where(flip, sides[1][0][v], sides[0][0][v]), (8, AXIAL))
+            at = 32 * v
+            ref[at : at + 16] = jnp.where(flip, edges_ref[v, 1, 0:16], edges_ref[v, 0, 0:16])
+            ref[at + 16 : at + 32] = jnp.where(flip, own_ref[v, 1], own_ref[v, 0])
+            ref[160 + v : 161 + v] = jnp.where(flip, sides[1][0][v], sides[0][0][v])
 
 
 def row_step(g, table_ref, q, prim, half_source, g_in, g_out, ends, masks, blade):
@@ -296,7 +308,8 @@
     circle,
     table_ref,
     blade_ref,
-    q_ref,
+    edges_ref,
+    own_ref,
     rad_ref,
     p1_ref,
     hs_ref,
@@ -331,20 +344,21 @@
         at = 0 if side == 0 else SECTOR - 1
         sign = 1.0 if side == 0 else -1.0
 
-        def pick(lo, hi):
-            return [jnp.where(use_core, core_ref[v, lo:hi], other_ref[v, lo:hi]) for v in ALL]
+        def pick(first, step, count):
+            spans = [slice(first + step * v, first + step * v + count) for v in ALL]
+            return [jnp.where(use_core, core_ref[span], other_ref[span]) for span in spans]
 
         def ordered(halo, halo_prim, own, own_prim):
             a, b = flux(halo, halo_prim, 3), flux(own, own_prim, 3)
             return face(halo, a, own, b) if side == 0 else face(own, b, halo, a)
 
-        near, near_part, corner = pick(0, 16), pick(16, 32), pick(32, 33)
-        own = [q_ref[v, :, at, :] for v in ALL]
+        near, near_part, corner = pick(0, 32, 16), pick(16, 32, 16), pick(160, 1, 1)
+        own = [edges_ref[v, side, 0:16] for v in ALL]
         own_prim, near_prim = primitives(own), primitives(near)
         shared = ordered(near, near_prim, own, own_prim)
         own_scale = (sign * geo.a_h) * step_weight(own_prim, geo.inv_h)
         near_scale = (-sign * geo.a_h) * step_weight(near_prim, geo.inv_h)
-        own_next = [p1_ref[v, :, at, :] + own_scale * shared[v] for v in ALL]
+        own_next = [own_ref[v, side] + own_scale * shared[v] for v in ALL]
         near_next = [near_part[v] + near_scale * shared[v] for v in ALL]
 
         edge = [rad_ref[v, at : at + 1, :] for v in ALL]
@@ -450,33 +464,38 @@
     def final(*refs):
         final_kernel(bands * BAND, circle, *refs)
 
-    near, q_level, q_prev = pl.pallas_call(
+    near = pl.pallas_call(
+        rad_kernel,
+        out_shape=shaped(5, SECTOR, AXIAL),
+        in_specs=[hbm],
+        out_specs=vmem(),
+        scratch_shapes=[pltpu.SemaphoreType.DMA],
+        compiler_params=pltpu.CompilerParams(vmem_limit_bytes=RAD_VMEM),
+    )(q_level)
+    rad_in = lax.ppermute(near, "rad", swap)
+    q_level, q_prev = pl.pallas_call(
         load_kernel,
-        out_shape=[
-            shaped(5, SECTOR, AXIAL),
-            shaped(5, BAND, SECTOR, AXIAL),
-            shaped(5, BAND, SECTOR, AXIAL),
-        ],
+        out_shape=[shaped(5, BAND, SECTOR, AXIAL)] * 2,
         in_specs=[hbm] * 2,
-        out_specs=[vmem()] * 3,
-        scratch_shapes=[pltpu.SemaphoreType.DMA((3,))],
+        out_specs=[vmem()] * 2,
+        scratch_shapes=[pltpu.SemaphoreType.DMA((2,))],
         compiler_params=pltpu.CompilerParams(vmem_limit_bytes=LOAD_VMEM),
+        cost_estimate=pl.CostEstimate(flops=0, bytes_accessed=3_000_000, transcendentals=0),
     )(q_level, q_prev)
-    rad_in = lax.ppermute(near, "rad", swap)
     edge_columns = pl.pallas_call(
         edges,
         out_shape=shaped(5, 2, 32, AXIAL),
         in_specs=[vmem()] * 3,
         out_specs=vmem(),
-        scratch_shapes=[pltpu.VMEM((5, 2, 32, AXIAL), F32)],
+        scratch_shapes=[pltpu.VMEM((5, 2, 32, AXIAL), F32), pltpu.VMEM((5, 2, 2, BAND, AXIAL), F32)],
         compiler_params=limit(4),
         cost_estimate=pl.CostEstimate(flops=5_000_000, bytes_accessed=2_000_000, transcendentals=50_000),
     )(blade, q_level, q_prev)
-    core_out, other_out = pl.pallas_call(
+    own_columns, core_out, other_out = pl.pallas_call(
         pack_kernel,
-        out_shape=[shaped(5, 40, AXIAL)] * 2,
+        out_shape=[shaped(5, 2, BAND, AXIAL)] + [shaped(168, AXIAL)] * 2,
         in_specs=[smem] + [vmem()] * 2,
-        out_specs=[vmem()] * 2,
+        out_specs=[vmem()] * 3,
         compiler_params=limit(4),
     )(table, edge_columns, rad_in)
     core_in = lax.ppermute(core_out, "theta", core)
@@ -494,7 +513,7 @@
     flow_state, send = pl.pallas_call(
         final,
         out_shape=[shaped(5, BAND, SECTOR, AXIAL), shaped(2 * AXIAL, BAND * SECTOR)],
-        in_specs=[smem] + [vmem()] * 8,
+        in_specs=[smem] + [vmem()] * 9,
         out_specs=[vmem()] * 2,
         scratch_shapes=[
             pltpu.VMEM((5, BAND + 2, SECTOR, AXIAL), F32),
@@ -502,7 +521,7 @@
             pltpu.VMEM((2, BAND, SECTOR, AXIAL), F32),
         ],
         compiler_params=limit(8),
-    )(table, blade, q_level, rad_in, part, half_source, next_in, other_in, core_in)
+    )(table, blade, edge_columns, own_columns, rad_in, part, half_source, next_in, other_in, core_in)
     got = lax.all_to_all(send.reshape(sectors, 4, 128), "theta", split_axis=0, concat_axis=0, tiled=True)
     spectra, flow_state = pl.pallas_call(
         mode_kernel,

time: 51.9 us -> 51.1 us (0.985)
    pallas_call x1, Pallas kernels: 1.59 us -> 0.69 us  [per_device(): pl.pallas_call(edges, out_shape=shaped(5, 2, 32, AXIAL), in_specs=[vmem()...]
    pallas_call x2 -> x3, Pallas kernels: 2.03 us -> 2.78 us  [the longest x1 1.3 us: per_device(): pl.pallas_call(load_kernel, out_shape=[shaped(5, BAND, SECTOR, AXIAL)] *...]
  transfers between devices with their start and end apart: 4 -> 4, of which waited for: 1 -> 1; matrix products, arithmetic and copies ran while one was open for 0% -> 0% of each run, Pallas kernels for 7% -> 8%
where the time goes in v5:
time: 51.1 us; the launch traced here: 50.9 us
  blocking collectives  24.3 us (48%)
  starting transfers between devices  12.9 us (25%)
  Pallas kernels  9.45 us (18%)
  waiting for transfers between devices  2.85 us (6%)
  between operations  0.71 us (1%)
  local copies, waits for them, and re-layouts  0.68 us (1%)
    all_to_all x1, blocking collectives, per_device(): lax.all_to_all(send.reshape(sectors, 4, 128), 'theta', split_axis=0, conc...  24.3 us
    ppermute x1, starting transfers between devices, per_device(): core_in = lax.ppermute(core_out, 'theta', core)  8.02 us
    ppermute x1, waiting for transfers between devices, per_device(): next_in = lax.ppermute(edge, 'rad', swap)  2.84 us
    ppermute x1, starting transfers between devices, per_device(): other_in = lax.ppermute(other_out, 'theta', other)  2.56 us
    pallas_call x1, Pallas kernels, per_device(): pl.pallas_call(final, out_shape=[shaped(5, BAND, SECTOR, AXIAL), shaped(2...  2.53 us
    ppermute x1, starting transfers between devices, per_device(): rad_in = lax.ppermute(near, 'rad', swap)  2.21 us
    pallas_call x1, Pallas kernels, per_device(): pl.pallas_call(early_kernel, out_shape=[shaped(5, BAND, SECTOR, AXIAL), s...  1.98 us
    pallas_call x1, Pallas kernels, per_device(): pl.pallas_call(mode_kernel, out_shape=[shaped(2, BAND, 4 * MODES), shaped...  1.47 us
  transfers between devices with their start and end apart: 4, of which 1 were waited for; matrix products, arithmetic and copies ran while one was open for 0% of the time, Pallas kernels for 8%

profile of v5, /device:TPU:1, one launch (start us, length us, event | category | flops | bytes accessed | tf_op | source)
XLA Modules:
  0.0 50.9 jit_solution(14534367166716057686)
XLA Ops:
  0.6 0.8 %shard_map.70 = f32[5,8,256]{2,1,0:T(8,128)S(1)} custom-call(f32[5,16,8,256]{3,2,1,0:T(8,128)} %q_ref.3), custom_call_target="tpu_custom_call" | custom-call | tf_op jit(solution)/shard_map/pallas_call | solution.py:467
  1.4 2.2 %collective-permute-start = (f32[5,8,256]{2,1,0:T(8,128)S(1)}, f32[5,8,256]{2,1,0:T(8,128)S(1)}, u32[]{:S(2)}, u32[]{:S(2)}) collective-permute-start(f32[5,8,256]{2,1,0:T(8,128)S(1)} %shard_map.70), channel_id=1, source_target_pairs={{0,1},{1,0},{2,3},{3,2},{4,5},{5,4},{6,7},{7,6},{8,9},{9,8},{10,11... | collective-permute-start | bytes 122888 | tf_op jit(solution)/shard_map/ppermute | solution.py:475
  3.6 1.3 %shard_map.68 = (f32[5,16,8,256]{3,2,1,0:T(8,128)S(1)}, f32[5,16,8,256]{3,2,1,0:T(8,128)S(1)}) custom-call(f32[5,16,8,256]{3,2,1,0:T(8,128)} %q_ref.3, f32[5,16,8,256]{3,2,1,0:T(8,128)} %qp_ref.1), custom_call_target="tpu_custom_call" | custom-call | bytes 3000000 | tf_op jit(solution)/shard_map/pallas_call | solution.py:476
  5.0 0.0 copy-start.2
  5.0 0.7 %copy-done.2 = s32[256]{0:T(256)S(1)} copy-done((s32[256]{0:T(256)S(1)}, s32[256]{0:T(256)}, u32[]{:S(2)}) %copy-start.2) | copy-done | bytes 1048
  5.6 0.0 copy-start.1
  5.6 0.7 %shard_map.69.edges_ref.refs_2_ = f32[5,2,32,256]{3,2,1,0:T(8,128)S(1)} custom-call(s32[1,256]{1,0:T(1,128)S(1)} %bitcast.5, f32[5,16,8,256]{3,2,1,0:T(8,128)S(1)} %get-tuple-element.14.refs_1_.q_ref, f32[5,16,8,256]{3,2,1,0:T(8,128)S(1)} %get-tuple-element.15.refs_2_.qp_ref), custom_call_target="tpu_custom_call" | custom-call | flops 5000000 | bytes 2000000 | tf_op jit(solution)/shard_map/pallas_call | solution.py:485
  6.3 0.0 collective-permute-done.rad_ref.refs_4_
  6.3 0.0 copy-done.1
  6.4 0.7 %shard_map.71 = (f32[5,2,16,256]{3,2,1,0:T(8,128)S(1)}, f32[168,256]{1,0:T(8,128)S(1)}, f32[168,256]{1,0:T(8,128)S(1)}) custom-call(f32[6,34]{1,0:T(8,128)S(1)} %copy-done.1, f32[5,2,32,256]{3,2,1,0:T(8,128)S(1)} %shard_map.69.edges_ref.refs_2_, f32[5,8,256]{2,1,0:T(8,128)S(1)} %collective-permute-done.rad_ref.refs_4_), custom_call_target="tpu_custom_call" | custom-call | tf_op jit(solution)/shard_map/pallas_call | solution.py:494
  7.0 2.6 %collective-permute-start.2 = (f32[168,256]{1,0:T(8,128)S(1)}, f32[168,256]{1,0:T(8,128)S(1)}, u32[]{:S(2)}, u32[]{:S(2)}) collective-permute-start(f32[168,256]{1,0:T(8,128)S(1)} %get-tuple-element.20), channel_id=1, source_target_pairs={{0,254},{2,4},{4,2},{6,8},{8,6},{10,12},{12,10},{14,16},{16,14},{1... | collective-permute-start | bytes 516104 | tf_op jit(solution)/shard_map/ppermute | solution.py:502
  9.6 8.0 %collective-permute-start.3 = (f32[168,256]{1,0:T(8,128)S(1)}, f32[168,256]{1,0:T(8,128)S(1)}, u32[]{:S(2)}, u32[]{:S(2)}) collective-permute-start(f32[168,256]{1,0:T(8,128)S(1)} %get-tuple-element.21), channel_id=1, source_target_pairs={{0,2},{2,0},{4,6},{6,4},{8,10},{10,8},{12,14},{14,12},{16,18},{18,... | collective-permute-start | bytes 516104 | tf_op jit(solution)/shard_map/ppermute | solution.py:501
  17.6 2.0 %shard_map.72 = (f32[5,16,8,256]{3,2,1,0:T(8,128)S(1)}, f32[5,8,256]{2,1,0:T(8,128)S(1)}, f32[5,16,8,256]{3,2,1,0:T(8,128)S(1)}) custom-call(f32[6,34]{1,0:T(8,128)S(1)} %copy-done.1, s32[1,256]{1,0:T(1,128)S(1)} %bitcast.6, f32[5,16,8,256]{3,2,1,0:T(8,128)S(1)} %get-tuple-element.14.refs_1_.q_ref, f32[5,16,8,256]{3,2,1,0:T(8,128)S(1)} %get-tuple-element.15.refs_2_.qp_ref, ...), custom_call_target="tpu_custom_call" | custom-call | flops 10000000 | bytes 3500000 | tf_op jit(solution)/shard_map/pallas_call | solution.py:503
  19.6 0.1 collective-permute-start.1
  19.7 2.8 %collective-permute-done.1.refs_7_ = f32[5,8,256]{2,1,0:T(8,128)S(1)} collective-permute-done((f32[5,8,256]{2,1,0:T(8,128)S(1)}, f32[5,8,256]{2,1,0:T(8,128)S(1)}, u32[]{:S(2)}, u32[]{:S(2)}) %collective-permute-start.1) | collective-permute-done | bytes 40992 | tf_op jit(solution)/shard_map/ppermute | solution.py:512
  22.6 0.0 collective-permute-done.2.refs_8_
  22.6 0.0 collective-permute-done.3.refs_9_
  22.6 2.5 %shard_map.73 = (f32[5,16,8,256]{3,2,1,0:T(8,128)S(1)}, f32[512,128]{1,0:T(8,128)S(1)}) custom-call(f32[6,34]{1,0:T(8,128)S(1)} %copy-done.1, s32[1,256]{1,0:T(1,128)S(1)} %bitcast.7, f32[5,2,32,256]{3,2,1,0:T(8,128)S(1)} %shard_map.69.edges_ref.refs_2_, f32[5,2,16,256]{3,2,1,0:T(8,128)S(1)} %get-tuple-element.16.refs_3_, ...), custom_call_target="tpu_custom_call" | custom-call | tf_op jit(solution)/shard_map/pallas_call | solution.py:513
  25.1 0.0 copy-start
  25.1 24.3 %all_to_all.5 = f32[128,4,128]{2,1,0:T(4,128)S(1)} all-to-all(f32[128,4,128]{2,1,0:T(4,128)S(1)} %bitcast.4), channel_id=1, replica_groups=mesh['theta'=128,'rad'=2] {'theta'}, dimensions={0} | all-to-all | bytes 524288 | tf_op jit(solution)/shard_map/all_to_all | solution.py:525
  49.4 0.0 copy-done
  49.4 1.5 %shard_map.74 = (f32[2,16,256]{2,1,0:T(8,128)}, f32[5,16,8,256]{3,2,1,0:T(8,128)}) custom-call(f32[512,128]{1,0:T(8,128)S(1)} %bitcast.3, f32[1024,128]{1,0:T(8,128)S(1)} %copy-done, f32[5,16,8,256]{3,2,1,0:T(8,128)S(1)} %get-tuple-element.23.flow_ref), custom_call_target="tpu_custom_call" | custom-call | tf_op jit(solution)/shard_map/pallas_call | solution.py:526
Async XLA Ops:
  1.4 4.9 %collective-permute-start = (f32[5,8,256]{2,1,0:T(8,128)S(1)}, f32[5,8,256]{2,1,0:T(8,128)S(1)}, u32[]{:S(2)}, u32[]{:S(2)}) collective-permute-start(f32[5,8,256]{2,1,0:T(8,128)S(1)} %shard_map.70), channel_id=1, source_target_pairs={{0,1},{1,0},{2,3},{3,2},{4,5},{5,4},{6,7},{7,6},{8,9},{9,8},{10,11... | collective-permute-start | bytes 122888 | tf_op jit(solution)/shard_map/ppermute | solution.py:475
  5.0 0.7 %copy-start.2 = (s32[256]{0:T(256)S(1)}, s32[256]{0:T(256)}, u32[]{:S(2)}) copy-start(s32[256]{0:T(256)} %param.7) | copy-start | bytes 3076
  5.6 0.7 %copy-start.1 = (f32[6,34]{1,0:T(8,128)S(1)}, f32[6,34]{1,0:T(8,128)}, u32[]{:S(2)}) copy-start(f32[6,34]{1,0:T(8,128)} %constant.4.clone.table_ref.refs_0_) | copy-start | bytes 2452
  7.0 15.5 %collective-permute-start.2 = (f32[168,256]{1,0:T(8,128)S(1)}, f32[168,256]{1,0:T(8,128)S(1)}, u32[]{:S(2)}, u32[]{:S(2)}) collective-permute-start(f32[168,256]{1,0:T(8,128)S(1)} %get-tuple-element.20), channel_id=1, source_target_pairs={{0,254},{2,4},{4,2},{6,8},{8,6},{10,12},{12,10},{14,16},{16,14},{1... | collective-permute-start | bytes 516104 | tf_op jit(solution)/shard_map/ppermute | solution.py:502
  9.6 13.0 %collective-permute-start.3 = (f32[168,256]{1,0:T(8,128)S(1)}, f32[168,256]{1,0:T(8,128)S(1)}, u32[]{:S(2)}, u32[]{:S(2)}) collective-permute-start(f32[168,256]{1,0:T(8,128)S(1)} %get-tuple-element.21), channel_id=1, source_target_pairs={{0,2},{2,0},{4,6},{6,4},{8,10},{10,8},{12,14},{14,12},{16,18},{18,... | collective-permute-start | bytes 516104 | tf_op jit(solution)/shard_map/ppermute | solution.py:501
  19.6 2.9 %collective-permute-start.1 = (f32[5,8,256]{2,1,0:T(8,128)S(1)}, f32[5,8,256]{2,1,0:T(8,128)S(1)}, u32[]{:S(2)}, u32[]{:S(2)}) collective-permute-start(f32[5,8,256]{2,1,0:T(8,128)S(1)} %get-tuple-element.19), channel_id=1, source_target_pairs={{0,1},{1,0},{2,3},{3,2},{4,5},{5,4},{6,7},{7,6},{8,9},{9,8},{10,11... | collective-permute-start | bytes 122888 | tf_op jit(solution)/shard_map/ppermute | solution.py:512
  25.1 24.3 %copy-start = (f32[1024,128]{1,0:T(8,128)S(1)}, f32[1024,128]{1,0:T(8,128)}, u32[]{:S(2)}) copy-start(f32[1024,128]{1,0:T(8,128)} %constant.5.clone.basis_ref) | copy-start | bytes 1572868

commit v6 on v5

v6 whole, which is shorter than its diff:
```python
import math

import jax
import jax.numpy as jnp
import numpy as np
from jax import lax
from jax.experimental import pallas as pl
from jax.experimental.pallas import tpu as pltpu
from jax.sharding import PartitionSpec as P

MODES = 64
GAMMA = 1.4
KAPPA = 2.0

BAND = 16
SECTOR = 8
AXIAL = 256
RAD_VMEM = 56_200_000
LOAD_VMEM = 55_000_000
F32 = jnp.float32
ALL = range(5)


def primitives(q):
    inverse = 1.0 / q[0]
    ux, ur, ut = q[1] * inverse, q[2] * inverse, q[3] * inverse
    pressure = (GAMMA - 1.0) * (q[4] - 0.5 * (q[1] * ux + q[2] * ur + q[3] * ut))
    sound = jnp.sqrt(GAMMA * pressure * inverse)
    return ux, ur, ut, pressure, sound


def flux(q, prim, d):
    u, pressure = prim[d - 1], prim[3]
    f = [q[d], q[1] * u, q[2] * u, q[3] * u, (q[4] + pressure) * u]
    f[d] = f[d] + pressure
    return f, jnp.abs(u) + prim[4]


def face(left_q, left_flux, right_q, right_flux):
    (fl, sl), (fr, sr) = left_flux, right_flux
    fastest = jnp.maximum(sl, sr)
    return [(fl[v] + fr[v]) - fastest * (right_q[v] - left_q[v]) for v in ALL]


HALF = AXIAL // 2


def axial_neighbour(x, lane, step, end):
    low, high = x[:, :HALF], x[:, HALF:]
    turned_low, turned_high = pltpu.roll(low, -step % HALF, 1), pltpu.roll(high, -step % HALF, 1)
    if step == 1:
        seam = lane == HALF - 1
        parts = [jnp.where(seam, turned_high, turned_low), jnp.where(seam, end, turned_high)]
    else:
        seam = lane == 0
        parts = [jnp.where(seam, end, turned_low), jnp.where(seam, turned_low, turned_high)]
    return jnp.concatenate(parts, axis=1)


def axial_difference(q, prim, lane):
    f, speed = flux(q, prim, 1)

    def following(x):
        return axial_neighbour(x, lane, 1, x[:, HALF:])

    qn = [following(x) for x in q]
    fn = [qn[1]] + [following(f[v]) for v in range(1, 5)]
    right = face(q, (f, speed), qn, (fn, following(speed)))
    return [x - axial_neighbour(x, lane, -1, 2.0 * f[v][:, :HALF]) for v, x in enumerate(right)]


def step_weight(prim, inv_h):
    ux, ur, ut, _, sound = prim
    rate = 4.0 * (jnp.abs(ux) + jnp.abs(ur)) + jnp.abs(ut) * (4.0 * inv_h) + sound * (8.0 + 4.0 * inv_h)
    return rate, 1.0 / (rate + 30.0)


def advance(q, prim, source, axial, radial, swirl, inv_r, inv_h, spin_r, blade):
    ux, ur, ut, pressure, sound = prim
    twice_r = 2.0 * inv_r
    rate, weight = step_weight(prim, inv_h)
    bladed, rotor = blade
    force = bladed * (q[3] - (rotor * spin_r) * q[0])
    gains = [None, None, twice_r * (q[3] * ut + pressure), -twice_r * (q[2] * ut) - force, -ut * force]
    out = []
    for v in ALL:
        total = source[v] - axial[v] - radial[v] - swirl[v]
        if gains[v] is not None:
            total = total + gains[v]
        out.append((rate * q[v] + total) * weight)
    return out


def geometry_table(rows, circle):
    mean = circle / (2.0 * math.pi)
    row = np.arange(rows, dtype=np.float64)
    radius = mean * (0.8 + 0.4 * (row + 0.5) / rows)
    inner = mean * (0.8 + 0.4 * row / rows)
    outer = mean * (0.8 + 0.4 * (row + 1.0) / rows)
    spacing = radius * (2.0 * math.pi / circle)
    return np.stack([outer / radius, inner / radius, 1.0 / spacing, 1.0 / radius, radius / (1.2 * mean)])


def coefficients(low, table, j):
    last = table.shape[1] - 1
    at = [min(max(j + first, 0), last) for first in (0, BAND)]
    return [jnp.where(low, np.float32(row[at[0]]), np.float32(row[at[1]])) for row in table]


def edge_row(band, at_low, at_high):
    return jnp.where(band == 0, at_low, at_high)


MIRROR = (1.0, 1.0, -1.0, 1.0, 1.0)


def blades(blade_ref, rows):
    blade = blade_ref[...]
    bladed = jnp.broadcast_to(4.0 * (blade > 0).astype(F32), (rows, AXIAL))
    rotor = jnp.broadcast_to((blade == 1).astype(F32), (rows, AXIAL))
    return bladed, rotor


def rad_kernel(q_ref, near_ref, sem):
    copy = pltpu.make_async_copy(q_ref.at[:, edge_row(lax.axis_index("rad"), BAND - 1, 0)], near_ref, sem)
    copy.start()
    copy.wait()


def load_kernel(q_ref, qp_ref, q_out_ref, qp_out_ref, sems):
    copies = [
        pltpu.make_async_copy(q_ref, q_out_ref, sems.at[0]),
        pltpu.make_async_copy(qp_ref, qp_out_ref, sems.at[1]),
    ]
    for copy in copies:
        copy.start()
    for copy in copies:
        copy.wait()


class Columns:
    def __init__(self, first_row, total_rows, circle):
        rows = (lax.broadcasted_iota(jnp.int32, (BAND, AXIAL), 0) + first_row).astype(F32)
        mean = circle / (2.0 * math.pi)
        radius = mean * (0.8 + 0.4 * (rows + 0.5) / total_rows)
        self.inner = mean * (0.8 + 0.4 * rows / total_rows)
        self.outer = mean * (0.8 + 0.4 * (rows + 1.0) / total_rows)
        self.inv_r = 1.0 / radius
        self.inv_h = self.inv_r * mean
        self.spin_r = radius * (1.0 / (1.2 * mean))
        self.a_h = 0.25 * self.inv_h


def edge_kernel(total_rows, circle, blade_ref, q_ref, qp_ref, edges_ref, ce, taken):
    band = lax.axis_index("rad")
    low = band == 0
    geo = Columns(band * BAND, total_rows, circle)
    blade = blades(blade_ref, BAND)
    lane = lax.broadcasted_iota(jnp.int32, (BAND, HALF), 1)
    row = lax.broadcasted_iota(jnp.int32, (BAND, AXIAL), 0)
    below_scale = jnp.where((row == 0) & jnp.logical_not(low), 0.0, geo.inv_r * geo.inner)
    above_scale = jnp.where((row == BAND - 1) & low, 0.0, geo.inv_r * geo.outer)
    for side in (0, 1):
        at, inner = (0, 1) if side == 0 else (SECTOR - 1, SECTOR - 2)
        for v in ALL:
            ce[v, side, 8:24] = q_ref[v, :, at, :]
            taken[v, side, 0] = q_ref[v, :, inner, :]
            taken[v, side, 1] = qp_ref[v, :, at, :]
    for side in (0, 1):
        edge = [ce[v, side, 8:24] for v in ALL]
        second = [taken[v, side, 0] for v in ALL]
        source = [40.0 * edge[v] - 10.0 * taken[v, side, 1] for v in ALL]
        for v in ALL:
            ce[v, side, 7:8] = MIRROR[v] * edge[v][0:1]
            ce[v, side, 24:25] = MIRROR[v] * edge[v][BAND - 1 : BAND]
        below = [ce[v, side, 7:23] for v in ALL]
        above = [ce[v, side, 9:25] for v in ALL]
        prim = primitives(edge)
        f = flux(edge, prim, 2)
        g_in = face(below, flux(below, primitives(below), 2), edge, f)
        g_out = face(edge, f, above, flux(above, primitives(above), 2))
        f = flux(edge, prim, 3)
        second_flux = flux(second, primitives(second), 3)
        if side == 0:
            swirl = [geo.inv_h * x for x in face(edge, f, second, second_flux)]
        else:
            swirl = [-geo.inv_h * x for x in face(second, second_flux, edge, f)]
        part = advance(
            edge,
            prim,
            source,
            axial_difference(edge, prim, lane),
            [above_scale * g_out[v] - below_scale * g_in[v] for v in ALL],
            swirl,
            geo.inv_r,
            geo.inv_h,
            geo.spin_r,
            blade,
        )
        for v in ALL:
            edges_ref[v, side, 0:16] = edge[v]
            edges_ref[v, side, 16:32] = part[v]


def pack_kernel(table, q_ref, edges_ref, rad_ref, own_ref, core_ref, other_ref):
    odd = lax.axis_index("theta") % 2 == 1
    band = lax.axis_index("rad")
    low = band == 0
    edge_at = edge_row(band, BAND - 1, 0)
    below_coefs, above_coefs = coefficients(low, table, 0), coefficients(low, table, BAND - 1)
    edge = [q_ref[v, edge_at] for v in ALL]
    near = [rad_ref[v] for v in ALL]
    edge_prim, near_prim = primitives(edge), primitives(near)
    (fe, se), (fn, sn) = flux(edge, edge_prim, 2), flux(near, near_prim, 2)
    fastest = jnp.where(low, np.float32(1.0), np.float32(-1.0)) * jnp.maximum(se, sn)
    _, weight = step_weight(edge_prim, jnp.where(low, above_coefs[2], below_coefs[2]))
    scale = jnp.where(low, -above_coefs[0], below_coefs[1]) * weight
    change = [scale * ((fe[v] + fn[v]) - fastest * (near[v] - edge[v])) for v in ALL]
    here = lax.broadcasted_iota(jnp.int32, (BAND, AXIAL), 0) == edge_at
    for v in ALL:
        for side in (0, 1):
            at = 0 if side == 0 else SECTOR - 1
            own_ref[v, side] = edges_ref[v, side, 16:32] + jnp.where(here, change[v][at : at + 1], 0.0)
        for ref, flip in ((core_ref, jnp.logical_not(odd)), (other_ref, odd)):
            at = 32 * v
            ref[at : at + 16] = jnp.where(flip, edges_ref[v, 1, 0:16], edges_ref[v, 0, 0:16])
            ref[at + 16 : at + 32] = jnp.where(flip, own_ref[v, 1], own_ref[v, 0])
            ref[160 + v : 161 + v] = jnp.where(flip, near[v][SECTOR - 1 : SECTOR], near[v][0:1])


def masks():
    return (
        lax.broadcasted_iota(jnp.int32, (SECTOR, HALF), 1),
        lax.broadcasted_iota(jnp.int32, (SECTOR, AXIAL), 0),
    )


def row_step(coefs, q, prim, source, g_in, g_out, ends, masks, blade):
    lane, sub = masks
    a_out, a_in, inv_h, inv_r, spin_r = coefs
    f, speed = flux(q, prim, 3)
    ahead = lambda x: pltpu.roll(x, SECTOR - 1, 0)
    qn = [ahead(x) for x in q]
    fn = [qn[3]] + [ahead(f[v]) for v in range(1, 5)]
    between = face(q, (f, speed), qn, (fn, ahead(speed)))
    swirl = []
    for v in ALL:
        end = 0.0 if ends is None else ends[v]
        right = jnp.where(sub == SECTOR - 1, end, between[v])
        left = jnp.where(sub == 0, end, pltpu.roll(between[v], 1, 0))
        swirl.append(inv_h * (right - left))
    radial = [a_out * g_out[v] - a_in * g_in[v] for v in ALL]
    return advance(q, prim, source, axial_difference(q, prim, lane), radial, swirl, inv_r, inv_h, spin_r, blade)


def sweep(load, step, store):
    below, q = load(-1), load(0)
    prim = primitives(q)
    g_in = face(below, flux(below, primitives(below), 2), q, flux(q, prim, 2))
    for j in range(BAND):
        above = load(j + 1)
        above_prim = primitives(above)
        g_out = face(q, flux(q, prim, 2), above, flux(above, above_prim, 2))
        store(j, step(j, q, prim, g_in, g_out))
        q, prim, g_in = above, above_prim, g_out


def early_kernel(table, blade_ref, q_ref, qp_ref, rad_ref, p1_ref, edge_ref, source_ref):
    band = lax.axis_index("rad")
    low = band == 0
    mask = masks()
    blade = blades(blade_ref, SECTOR)

    def load(j):
        if j < 0:
            return [jnp.where(low, MIRROR[v] * q_ref[v, 0], rad_ref[v]) for v in ALL]
        if j == BAND:
            return [jnp.where(low, rad_ref[v], MIRROR[v] * q_ref[v, BAND - 1]) for v in ALL]
        return [q_ref[v, j] for v in ALL]

    def step(j, q, prim, g_in, g_out):
        source = [40.0 * q[v] - 10.0 * qp_ref[v, j] for v in ALL]
        for v in ALL:
            source_ref[v, j] = source[v]
        return row_step(coefficients(low, table, j), q, prim, source, g_in, g_out, None, mask, blade)

    def store(j, q):
        for v in ALL:
            p1_ref[v, j] = q[v]

    sweep(load, step, store)
    for v in ALL:
        edge_ref[v] = p1_ref[v, edge_row(band, BAND - 1, 0)]


def final_kernel(
    total_rows,
    circle,
    table,
    blade_ref,
    edges_ref,
    own_ref,
    rad_ref,
    p1_ref,
    source_ref,
    next_ref,
    other_ref,
    core_ref,
    flow_ref,
    send_ref,
    p1,
    nearby,
    ends,
    fields,
):
    odd = lax.axis_index("theta") % 2 == 1
    band = lax.axis_index("rad")
    low = band == 0
    mask = masks()
    blade = blades(blade_ref, SECTOR)
    for v in ALL:
        p1[v] = p1_ref[v]
        nearby[v] = next_ref[v]

    geo = Columns(band * BAND, total_rows, circle)
    near_inv_h = jnp.where(low, coefficients(low, table, BAND)[2], coefficients(low, table, -1)[2])

    for side in (0, 1):
        use_core = odd if side == 0 else jnp.logical_not(odd)
        at = 0 if side == 0 else SECTOR - 1
        sign = 1.0 if side == 0 else -1.0

        def pick(first, step, count):
            spans = [slice(first + step * v, first + step * v + count) for v in ALL]
            return [jnp.where(use_core, core_ref[span], other_ref[span]) for span in spans]

        def ordered(halo, halo_prim, own, own_prim):
            a, b = flux(halo, halo_prim, 3), flux(own, own_prim, 3)
            return face(halo, a, own, b) if side == 0 else face(own, b, halo, a)

        near, near_part, corner = pick(0, 32, 16), pick(16, 32, 16), pick(160, 1, 1)
        own = [edges_ref[v, side, 0:16] for v in ALL]
        own_prim, near_prim = primitives(own), primitives(near)
        shared = ordered(near, near_prim, own, own_prim)
        own_scale = (sign * geo.inv_h) * step_weight(own_prim, geo.inv_h)[1]
        near_scale = (-sign * geo.inv_h) * step_weight(near_prim, geo.inv_h)[1]
        own_next = [own_ref[v, side] + own_scale * shared[v] for v in ALL]
        near_next = [near_part[v] + near_scale * shared[v] for v in ALL]

        edge = [rad_ref[v, at : at + 1, :] for v in ALL]
        edge_prim = primitives(edge)
        corner_face = ordered(corner, primitives(corner), edge, edge_prim)
        corner_scale = (sign * near_inv_h) * step_weight(edge_prim, near_inv_h)[1]

        faces = ordered(near_next, primitives(near_next), own_next, primitives(own_next))
        for v in ALL:
            p1[v, :, at, :] = own_next[v]
            nearby[v, at : at + 1, :] = next_ref[v, at : at + 1, :] + corner_scale * corner_face[v]
            ends[v, :, at, :] = faces[v]

    def load(j):
        if j < 0:
            return [jnp.where(low, MIRROR[v] * p1[v, 0], nearby[v]) for v in ALL]
        if j == BAND:
            return [jnp.where(low, nearby[v], MIRROR[v] * p1[v, BAND - 1]) for v in ALL]
        return [p1[v, j] for v in ALL]

    def step(j, q, prim, g_in, g_out):
        source, end = [source_ref[v, j] for v in ALL], [ends[v, j] for v in ALL]
        return row_step(coefficients(low, table, j), q, prim, source, g_in, g_out, end, mask, blade)

    def store(j, q):
        for v in ALL:
            flow_ref[v, j] = q[v]
        ux, _, _, pressure, _ = primitives(q)
        fields[0, j] = pressure
        fields[1, j] = ux

    sweep(load, step, store)
    for f in (0, 1):
        turned = fields[f].reshape(BAND * SECTOR, AXIAL).T
        send_ref[pl.ds(f, AXIAL, stride=2), :] = turned


def mode_kernel(got_ref, basis_ref, flow_ref, out_ref, flow_out_ref, turned, sem):
    copy = pltpu.make_async_copy(flow_ref, flow_out_ref, sem)
    copy.start()
    sectors = got_ref.shape[0] // 4
    parts = []
    for e in (0, 1):
        for f in (0, 1):
            n = 2 * e + f
            turned[n] = got_ref[pl.ds(n, sectors, stride=4), :].T
            parts.append(
                jnp.concatenate([turned[n, pl.ds(m, BAND, stride=SECTOR), :] for m in range(SECTOR)], axis=1)
            )
    product = jnp.dot(
        jnp.concatenate(parts, axis=0), basis_ref[...], precision=lax.Precision.HIGHEST, preferred_element_type=F32
    )
    for e in (0, 1):
        for f in (0, 1):
            n = 2 * e + f
            out_ref[e, :, 2 * MODES * f : 2 * MODES * (f + 1)] = product[BAND * n : BAND * (n + 1)]
    copy.wait()


def mode_basis(sectors):
    circle = sectors * SECTOR
    cell = (np.arange(SECTOR)[:, None] + SECTOR * np.arange(sectors)[None, :]).reshape(-1)
    phase = (cell[:, None] * np.arange(1, MODES + 1)[None, :] % circle) * (2.0 * np.pi / circle)
    return (np.concatenate([np.cos(phase), -np.sin(phase)], axis=1) / np.sqrt(circle)).astype(np.float32)


def shaped(*shape):
    return jax.ShapeDtypeStruct(shape, F32)


def vmem():
    return pl.BlockSpec(memory_space=pltpu.VMEM)


def limit(mib):
    return pltpu.CompilerParams(vmem_limit_bytes=int(mib * 2**20))


def per_device(q_level, q_prev, blade_row):
    sectors = lax.axis_size("theta")
    bands = lax.axis_size("rad")
    circle = sectors * SECTOR
    core = [(t, t ^ 1) for t in range(sectors)]
    other = [(t, (((t + 1) ^ 1) - 1) % sectors) for t in range(sectors)]
    table = geometry_table(bands * BAND, circle)
    blade = blade_row.reshape(1, AXIAL)

    hbm = pl.BlockSpec(memory_space=pltpu.HBM)
    swap = [(0, 1), (1, 0)]

    def edges(*refs):
        edge_kernel(bands * BAND, circle, *refs)

    def pack(*refs):
        pack_kernel(table, *refs)

    def early(*refs):
        early_kernel(table, *refs)

    def final(*refs):
        final_kernel(bands * BAND, circle, table, *refs)

    near = pl.pallas_call(
        rad_kernel,
        out_shape=shaped(5, SECTOR, AXIAL),
        in_specs=[hbm],
        out_specs=vmem(),
        scratch_shapes=[pltpu.SemaphoreType.DMA],
        compiler_params=pltpu.CompilerParams(vmem_limit_bytes=RAD_VMEM),
    )(q_level)
    rad_in = lax.ppermute(near, "rad", swap)
    q_level, q_prev = pl.pallas_call(
        load_kernel,
        out_shape=[shaped(5, BAND, SECTOR, AXIAL)] * 2,
        in_specs=[hbm] * 2,
        out_specs=[vmem()] * 2,
        scratch_shapes=[pltpu.SemaphoreType.DMA((2,))],
        compiler_params=pltpu.CompilerParams(vmem_limit_bytes=LOAD_VMEM),
        cost_estimate=pl.CostEstimate(flops=0, bytes_accessed=3_000_000, transcendentals=0),
    )(q_level, q_prev)
    edge_columns = pl.pallas_call(
        edges,
        out_shape=shaped(5, 2, 32, AXIAL),
        in_specs=[vmem()] * 3,
        out_specs=vmem(),
        scratch_shapes=[pltpu.VMEM((5, 2, 32, AXIAL), F32), pltpu.VMEM((5, 2, 2, BAND, AXIAL), F32)],
        compiler_params=limit(4),
        cost_estimate=pl.CostEstimate(flops=5_000_000, bytes_accessed=2_000_000, transcendentals=50_000),
    )(blade, q_level, q_prev)
    own_columns, core_out, other_out = pl.pallas_call(
        pack,
        out_shape=[shaped(5, 2, BAND, AXIAL)] + [shaped(168, AXIAL)] * 2,
        in_specs=[vmem()] * 3,
        out_specs=[vmem()] * 3,
        compiler_params=limit(4),
    )(q_level, edge_columns, rad_in)
    core_in = lax.ppermute(core_out, "theta", core)
    other_in = lax.ppermute(other_out, "theta", other)
    part, edge, source = pl.pallas_call(
        early,
        out_shape=[shaped(5, BAND, SECTOR, AXIAL), shaped(5, SECTOR, AXIAL), shaped(5, BAND, SECTOR, AXIAL)],
        in_specs=[vmem()] * 4,
        out_specs=[vmem()] * 3,
        compiler_params=limit(8),
        cost_estimate=pl.CostEstimate(flops=10_000_000, bytes_accessed=3_500_000, transcendentals=100_000),
    )(blade, q_level, q_prev, rad_in)
    next_in = lax.ppermute(edge, "rad", swap)
    flow_state, send = pl.pallas_call(
        final,
        out_shape=[shaped(5, BAND, SECTOR, AXIAL), shaped(2 * AXIAL, BAND * SECTOR)],
        in_specs=[vmem()] * 9,
        out_specs=[vmem()] * 2,
        scratch_shapes=[
            pltpu.VMEM((5, BAND, SECTOR, AXIAL), F32),
            pltpu.VMEM((5, SECTOR, AXIAL), F32),
            pltpu.VMEM((5, BAND, SECTOR, AXIAL), F32),
            pltpu.VMEM((2, BAND, SECTOR, AXIAL), F32),
        ],
        compiler_params=limit(8),
    )(blade, edge_columns, own_columns, rad_in, part, source, next_in, other_in, core_in)
    got = lax.all_to_all(send.reshape(sectors, 4, 128), "theta", split_axis=0, concat_axis=0, tiled=True)
    spectra, flow_state = pl.pallas_call(
        mode_kernel,
        out_shape=[shaped(2, BAND, 4 * MODES), shaped(5, BAND, SECTOR, AXIAL)],
        in_specs=[vmem()] * 3,
        out_specs=[vmem(), hbm],
        scratch_shapes=[pltpu.VMEM((4, BAND * SECTOR, sectors), F32), pltpu.SemaphoreType.DMA],
        compiler_params=limit(4),
    )(got.reshape(4 * sectors, 128), jnp.asarray(mode_basis(sectors)), flow_state)
    return flow_state, spectra


def solution(mesh):
    in_specs = (P(None, "rad", "theta", None), P(None, "rad", "theta", None), P())
    out_specs = (P(None, "rad", "theta", None), P("theta", "rad", None))
    return jax.shard_map(per_device, mesh=mesh, in_specs=in_specs, out_specs=out_specs, check_vma=False)
```

time: 51.1 us -> 49.9 us (0.977)
  Pallas kernels: 9.45 us -> 7.69 us
    pallas_call x2, Pallas kernels: 2.66 us -> 1.54 us  [the longest x1 1.46 us: per_device(): pl.pallas_call(early, out_shape=[shaped(5, BAND, SECTOR, AXIAL), shaped(5...]
    pallas_call x1, Pallas kernels: 2.53 us -> 1.92 us  [per_device(): pl.pallas_call(final, out_shape=[shaped(5, BAND, SECTOR, AXIAL), shaped(2...]
    all_to_all x1, blocking collectives: 24.3 us -> 24.8 us  [per_device(): lax.all_to_all(send.reshape(sectors, 4, 128), 'theta', split_axis=0, conc...]
  transfers between devices with their start and end apart: 4 -> 4, of which waited for: 1 -> 1; matrix products, arithmetic and copies ran while one was open for 0% -> 0% of each run, Pallas kernels for 8% -> 7%
where the time goes in v6:
time: 49.9 us; the launch traced here: 49.7 us
  blocking collectives  24.8 us (50%)
  starting transfers between devices  12.9 us (26%)
  Pallas kernels  7.69 us (15%)
  waiting for transfers between devices  2.85 us (6%)
  between operations  0.7 us (1%)
  local copies, waits for them, and re-layouts  0.68 us (1%)
    all_to_all x1, blocking collectives, per_device(): lax.all_to_all(send.reshape(sectors, 4, 128), 'theta', split_axis=0, conc...  24.8 us
    ppermute x1, starting transfers between devices, per_device(): core_in = lax.ppermute(core_out, 'theta', core)  8.02 us
    ppermute x1, waiting for transfers between devices, per_device(): next_in = lax.ppermute(edge, 'rad', swap)  2.84 us
    ppermute x1, starting transfers between devices, per_device(): other_in = lax.ppermute(other_out, 'theta', other)  2.56 us
    ppermute x1, starting transfers between devices, per_device(): rad_in = lax.ppermute(near, 'rad', swap)  2.21 us
    pallas_call x1, Pallas kernels, per_device(): pl.pallas_call(final, out_shape=[shaped(5, BAND, SECTOR, AXIAL), shaped(2...  1.92 us
    pallas_call x1, Pallas kernels, per_device(): pl.pallas_call(mode_kernel, out_shape=[shaped(2, BAND, 4 * MODES), shaped...  1.47 us
    pallas_call x1, Pallas kernels, per_device(): pl.pallas_call(early, out_shape=[shaped(5, BAND, SECTOR, AXIAL), shaped(5...  1.46 us
  transfers between devices with their start and end apart: 4, of which 1 were waited for; matrix products, arithmetic and copies ran while one was open for 0% of the time, Pallas kernels for 7%

profile of v6, /device:TPU:1, one launch (start us, length us, event | category | flops | bytes accessed | tf_op | source)
XLA Modules:
  0.0 49.7 jit_solution(1677957048439373237)
XLA Ops:
  0.6 0.8 %shard_map.61 = f32[5,8,256]{2,1,0:T(8,128)S(1)} custom-call(f32[5,16,8,256]{3,2,1,0:T(8,128)} %q_ref.3), custom_call_target="tpu_custom_call" | custom-call | tf_op jit(solution)/shard_map/pallas_call | solution.py:450
  1.4 2.2 %collective-permute-start = (f32[5,8,256]{2,1,0:T(8,128)S(1)}, f32[5,8,256]{2,1,0:T(8,128)S(1)}, u32[]{:S(2)}, u32[]{:S(2)}) collective-permute-start(f32[5,8,256]{2,1,0:T(8,128)S(1)} %shard_map.61), channel_id=1, source_target_pairs={{0,1},{1,0},{2,3},{3,2},{4,5},{5,4},{6,7},{7,6},{8,9},{9,8},{10,11... | collective-permute-start | bytes 122888 | tf_op jit(solution)/shard_map/ppermute | solution.py:458
  3.6 1.3 %shard_map.59 = (f32[5,16,8,256]{3,2,1,0:T(8,128)S(1)}, f32[5,16,8,256]{3,2,1,0:T(8,128)S(1)}) custom-call(f32[5,16,8,256]{3,2,1,0:T(8,128)} %q_ref.3, f32[5,16,8,256]{3,2,1,0:T(8,128)} %qp_ref.1), custom_call_target="tpu_custom_call" | custom-call | bytes 3000000 | tf_op jit(solution)/shard_map/pallas_call | solution.py:459
  5.0 0.0 copy-start.1
  5.0 0.7 %copy-done.1 = s32[256]{0:T(256)S(1)} copy-done((s32[256]{0:T(256)S(1)}, s32[256]{0:T(256)}, u32[]{:S(2)}) %copy-start.1) | copy-done | bytes 1048
  5.6 0.7 %shard_map.60.refs_1_ = f32[5,2,32,256]{3,2,1,0:T(8,128)S(1)} custom-call(s32[1,256]{1,0:T(1,128)S(1)} %bitcast.5, f32[5,16,8,256]{3,2,1,0:T(8,128)S(1)} %get-tuple-element.14.refs_1_.refs_0_, f32[5,16,8,256]{3,2,1,0:T(8,128)S(1)} %get-tuple-element.15.refs_2_), custom_call_target="tpu_custom_call" | custom-call | flops 5000000 | bytes 2000000 | tf_op jit(solution)/shard_map/pallas_call | solution.py:468
  6.3 0.0 collective-permute-done.refs_2_.refs_3_
  6.3 0.1 shard_map.62
  6.4 2.6 %collective-permute-start.2 = (f32[168,256]{1,0:T(8,128)S(1)}, f32[168,256]{1,0:T(8,128)S(1)}, u32[]{:S(2)}, u32[]{:S(2)}) collective-permute-start(f32[168,256]{1,0:T(8,128)S(1)} %get-tuple-element.20), channel_id=1, source_target_pairs={{0,254},{2,4},{4,2},{6,8},{8,6},{10,12},{12,10},{14,16},{16,14},{1... | collective-permute-start | bytes 516104 | tf_op jit(solution)/shard_map/ppermute | solution.py:485
  9.0 8.0 %collective-permute-start.3 = (f32[168,256]{1,0:T(8,128)S(1)}, f32[168,256]{1,0:T(8,128)S(1)}, u32[]{:S(2)}, u32[]{:S(2)}) collective-permute-start(f32[168,256]{1,0:T(8,128)S(1)} %get-tuple-element.21), channel_id=1, source_target_pairs={{0,2},{2,0},{4,6},{6,4},{8,10},{10,8},{12,14},{14,12},{16,18},{18,... | collective-permute-start | bytes 516104 | tf_op jit(solution)/shard_map/ppermute | solution.py:484
  17.0 1.5 %shard_map.63 = (f32[5,16,8,256]{3,2,1,0:T(8,128)S(1)}, f32[5,8,256]{2,1,0:T(8,128)S(1)}, f32[5,16,8,256]{3,2,1,0:T(8,128)S(1)}) custom-call(s32[1,256]{1,0:T(1,128)S(1)} %bitcast.6, f32[5,16,8,256]{3,2,1,0:T(8,128)S(1)} %get-tuple-element.14.refs_1_.refs_0_, f32[5,16,8,256]{3,2,1,0:T(8,128)S(1)} %get-tuple-element.15.refs_2_, ...), custom_call_target="tpu_custom_call" | custom-call | flops 10000000 | bytes 3500000 | tf_op jit(solution)/shard_map/pallas_call | solution.py:486
  18.5 0.1 collective-permute-start.1
  18.6 2.8 %collective-permute-done.1.refs_6_ = f32[5,8,256]{2,1,0:T(8,128)S(1)} collective-permute-done((f32[5,8,256]{2,1,0:T(8,128)S(1)}, f32[5,8,256]{2,1,0:T(8,128)S(1)}, u32[]{:S(2)}, u32[]{:S(2)}) %collective-permute-start.1) | collective-permute-done | bytes 40992 | tf_op jit(solution)/shard_map/ppermute | solution.py:494
  21.4 0.0 collective-permute-done.2.refs_7_
  21.4 0.0 collective-permute-done.3.refs_8_
  21.4 1.9 %shard_map.64 = (f32[5,16,8,256]{3,2,1,0:T(8,128)S(1)}, f32[512,128]{1,0:T(8,128)S(1)}) custom-call(s32[1,256]{1,0:T(1,128)S(1)} %bitcast.7, f32[5,2,32,256]{3,2,1,0:T(8,128)S(1)} %shard_map.60.refs_1_, f32[5,2,16,256]{3,2,1,0:T(8,128)S(1)} %get-tuple-element.16.refs_2_, f32[5,8,256]{2,1,0:T(8,128)S(1)} %collective-permute-done.refs_2_.refs_3_, ...), custom_call_target="tpu_custom_call" | custom-call | tf_op jit(solution)/shard_map/pallas_call | solution.py:495
  23.3 0.0 copy-start
  23.3 24.8 %all_to_all.5 = f32[128,4,128]{2,1,0:T(4,128)S(1)} all-to-all(f32[128,4,128]{2,1,0:T(4,128)S(1)} %bitcast.4), channel_id=1, replica_groups=mesh['theta'=128,'rad'=2] {'theta'}, dimensions={0} | all-to-all | bytes 524288 | tf_op jit(solution)/shard_map/all_to_all | solution.py:508
  48.2 0.0 copy-done
  48.2 1.5 %shard_map.65 = (f32[2,16,256]{2,1,0:T(8,128)}, f32[5,16,8,256]{3,2,1,0:T(8,128)}) custom-call(f32[512,128]{1,0:T(8,128)S(1)} %bitcast.3, f32[1024,128]{1,0:T(8,128)S(1)} %copy-done, f32[5,16,8,256]{3,2,1,0:T(8,128)S(1)} %get-tuple-element.23.flow_ref), custom_call_target="tpu_custom_call" | custom-call | tf_op jit(solution)/shard_map/pallas_call | solution.py:509
Async XLA Ops:
  1.4 4.9 %collective-permute-start = (f32[5,8,256]{2,1,0:T(8,128)S(1)}, f32[5,8,256]{2,1,0:T(8,128)S(1)}, u32[]{:S(2)}, u32[]{:S(2)}) collective-permute-start(f32[5,8,256]{2,1,0:T(8,128)S(1)} %shard_map.61), channel_id=1, source_target_pairs={{0,1},{1,0},{2,3},{3,2},{4,5},{5,4},{6,7},{7,6},{8,9},{9,8},{10,11... | collective-permute-start | bytes 122888 | tf_op jit(solution)/shard_map/ppermute | solution.py:458
  5.0 0.7 %copy-start.1 = (s32[256]{0:T(256)S(1)}, s32[256]{0:T(256)}, u32[]{:S(2)}) copy-start(s32[256]{0:T(256)} %param.6) | copy-start | bytes 3076
  6.4 15.0 %collective-permute-start.2 = (f32[168,256]{1,0:T(8,128)S(1)}, f32[168,256]{1,0:T(8,128)S(1)}, u32[]{:S(2)}, u32[]{:S(2)}) collective-permute-start(f32[168,256]{1,0:T(8,128)S(1)} %get-tuple-element.20), channel_id=1, source_target_pairs={{0,254},{2,4},{4,2},{6,8},{8,6},{10,12},{12,10},{14,16},{16,14},{1... | collective-permute-start | bytes 516104 | tf_op jit(solution)/shard_map/ppermute | solution.py:485
  9.0 12.4 %collective-permute-start.3 = (f32[168,256]{1,0:T(8,128)S(1)}, f32[168,256]{1,0:T(8,128)S(1)}, u32[]{:S(2)}, u32[]{:S(2)}) collective-permute-start(f32[168,256]{1,0:T(8,128)S(1)} %get-tuple-element.21), channel_id=1, source_target_pairs={{0,2},{2,0},{4,6},{6,4},{8,10},{10,8},{12,14},{14,12},{16,18},{18,... | collective-permute-start | bytes 516104 | tf_op jit(solution)/shard_map/ppermute | solution.py:484
  18.5 2.9 %collective-permute-start.1 = (f32[5,8,256]{2,1,0:T(8,128)S(1)}, f32[5,8,256]{2,1,0:T(8,128)S(1)}, u32[]{:S(2)}, u32[]{:S(2)}) collective-permute-start(f32[5,8,256]{2,1,0:T(8,128)S(1)} %get-tuple-element.19), channel_id=1, source_target_pairs={{0,1},{1,0},{2,3},{3,2},{4,5},{5,4},{6,7},{7,6},{8,9},{9,8},{10,11... | collective-permute-start | bytes 122888 | tf_op jit(solution)/shard_map/ppermute | solution.py:494
  23.3 24.9 %copy-start = (f32[1024,128]{1,0:T(8,128)S(1)}, f32[1024,128]{1,0:T(8,128)}, u32[]{:S(2)}) copy-start(f32[1024,128]{1,0:T(8,128)} %constant.2.clone.basis_ref) | copy-start | bytes 1572868

commit v7 on v6

--- a/solution.py
+++ b/solution.py
@@ -382,33 +382,43 @@
         send_ref[pl.ds(f, AXIAL, stride=2), :] = turned
 
 
-def mode_kernel(got_ref, basis_ref, flow_ref, out_ref, flow_out_ref, turned, sem):
+def mode_kernel(got_ref, basis_ref, flow_ref, keep_ref, give_ref, flow_out_ref, turned, sem):
     copy = pltpu.make_async_copy(flow_ref, flow_out_ref, sem)
     copy.start()
-    sectors = got_ref.shape[0] // 4
+    chips = got_ref.shape[0] // 8
+    core = lax.axis_index("theta") % 2
+    left = lax.broadcasted_iota(jnp.int32, (BAND, 2 * chips), 1) < chips
     parts = []
+    for n in range(8):
+        cells = got_ref[pl.ds(n, chips, stride=8), :]
+        turned[n] = jnp.concatenate([cells, cells], axis=0).T
+        rows = [turned[n, pl.ds(m, BAND, stride=SECTOR), :] for m in range(SECTOR)]
+        parts.append(
+            jnp.concatenate([jnp.where(left, rows[m], rows[m + 1]) for m in range(0, SECTOR, 2)], axis=1)
+        )
+    product = jnp.dot(
+        jnp.concatenate(parts, axis=0), basis_ref[core], precision=lax.Precision.HIGHEST, preferred_element_type=F32
+    )
+    half = 4 * BAND
+    keep_ref[...] = jnp.where(core == 0, product[:half], product[half:])
+    give_ref[...] = jnp.where(core == 0, product[half:], product[:half])
+    copy.wait()
+
+
+def sum_kernel(keep_ref, got_ref, out_ref):
+    total = keep_ref[...] + got_ref[...]
     for e in (0, 1):
         for f in (0, 1):
             n = 2 * e + f
-            turned[n] = got_ref[pl.ds(n, sectors, stride=4), :].T
-            parts.append(
-                jnp.concatenate([turned[n, pl.ds(m, BAND, stride=SECTOR), :] for m in range(SECTOR)], axis=1)
-            )
-    product = jnp.dot(
-        jnp.concatenate(parts, axis=0), basis_ref[...], precision=lax.Precision.HIGHEST, preferred_element_type=F32
-    )
-    for e in (0, 1):
-        for f in (0, 1):
-            n = 2 * e + f
-            out_ref[e, :, 2 * MODES * f : 2 * MODES * (f + 1)] = product[BAND * n : BAND * (n + 1)]
-    copy.wait()
+            out_ref[e, :, 2 * MODES * f : 2 * MODES * (f + 1)] = total[BAND * n : BAND * (n + 1)]
 
 
 def mode_basis(sectors):
     circle = sectors * SECTOR
-    cell = (np.arange(SECTOR)[:, None] + SECTOR * np.arange(sectors)[None, :]).reshape(-1)
-    phase = (cell[:, None] * np.arange(1, MODES + 1)[None, :] % circle) * (2.0 * np.pi / circle)
-    return (np.concatenate([np.cos(phase), -np.sin(phase)], axis=1) / np.sqrt(circle)).astype(np.float32)
+    sector = 2 * np.arange(sectors // 2)[None, None, :] + np.arange(2)[:, None, None]
+    cell = (np.arange(SECTOR)[None, :, None] + SECTOR * sector).reshape(2, -1)
+    phase = (cell[:, :, None] * np.arange(1, MODES + 1) % circle) * (2.0 * np.pi / circle)
+    return (np.concatenate([np.cos(phase), -np.sin(phase)], axis=2) / np.sqrt(circle)).astype(np.float32)
 
 
 def shaped(*shape):
@@ -505,15 +515,30 @@
         ],
         compiler_params=limit(8),
     )(blade, edge_columns, own_columns, rad_in, part, source, next_in, other_in, core_in)
-    got = lax.all_to_all(send.reshape(sectors, 4, 128), "theta", split_axis=0, concat_axis=0, tiled=True)
-    spectra, flow_state = pl.pallas_call(
+    chips = sectors // 2
+    got = lax.all_to_all(
+        send.reshape(chips, 8, 128),
+        "theta",
+        split_axis=0,
+        concat_axis=0,
+        tiled=True,
+        axis_index_groups=[[2 * chip + c for chip in range(chips)] for c in (0, 1)],
+    )
+    keep, give, flow_state = pl.pallas_call(
         mode_kernel,
-        out_shape=[shaped(2, BAND, 4 * MODES), shaped(5, BAND, SECTOR, AXIAL)],
+        out_shape=[shaped(4 * BAND, 2 * MODES)] * 2 + [shaped(5, BAND, SECTOR, AXIAL)],
         in_specs=[vmem()] * 3,
-        out_specs=[vmem(), hbm],
-        scratch_shapes=[pltpu.VMEM((4, BAND * SECTOR, sectors), F32), pltpu.SemaphoreType.DMA],
+        out_specs=[vmem(), vmem(), hbm],
+        scratch_shapes=[pltpu.VMEM((8, BAND * SECTOR, 2 * chips), F32), pltpu.SemaphoreType.DMA],
         compiler_params=limit(4),
-    )(got.reshape(4 * sectors, 128), jnp.asarray(mode_basis(sectors)), flow_state)
+    )(got.reshape(8 * chips, 128), jnp.asarray(mode_basis(sectors)), flow_state)
+    spectra = pl.pallas_call(
+        sum_kernel,
+        out_shape=shaped(2, BAND, 4 * MODES),
+        in_specs=[vmem()] * 2,
+        out_specs=vmem(),
+        compiler_params=limit(2),
+    )(keep, lax.ppermute(give, "theta", core))
     return flow_state, spectra
 
 

time: 49.9 us -> 49.1 us (0.984)
  blocking collectives: 24.8 us -> 22.8 us
  waiting for transfers between devices: 2.85 us -> 4.04 us
    all_to_all x1, blocking collectives: 24.8 us -> 22.8 us  [per_device(): lax.all_to_all(send.reshape(chips, 8, 128), 'theta', split_axis=0, concat...]
    ppermute x0 -> x1, waiting for transfers between devices: none -> 1.19 us  [per_device(): lax.ppermute(give, 'theta', core)]
    pallas_call x1 -> x2, Pallas kernels: 1.47 us -> 1.48 us  [the longest x1 0.86 us: per_device(): pl.pallas_call(mode_kernel, out_shape=[shaped(4 * BAND, 2 * MODES)] * 2 +...]
  transfers between devices with their start and end apart: 4 -> 5, of which waited for: 1 -> 2; matrix products, arithmetic and copies ran while one was open for 0% -> 0% of each run, Pallas kernels for 7% -> 7%
where the time goes in v7:
time: 49.1 us; the launch traced here: 48.9 us
  blocking collectives  22.8 us (46%)
  starting transfers between devices  13 us (26%)
  Pallas kernels  7.7 us (16%)
  waiting for transfers between devices  4.04 us (8%)
  between operations  0.72 us (1%)
  local copies, waits for them, and re-layouts  0.68 us (1%)
    all_to_all x1, blocking collectives, per_device(): lax.all_to_all(send.reshape(chips, 8, 128), 'theta', split_axis=0, concat...  22.8 us
    ppermute x1, starting transfers between devices, per_device(): core_in = lax.ppermute(core_out, 'theta', core)  8.02 us
    ppermute x1, waiting for transfers between devices, per_device(): next_in = lax.ppermute(edge, 'rad', swap)  2.84 us
    ppermute x1, starting transfers between devices, per_device(): other_in = lax.ppermute(other_out, 'theta', other)  2.56 us
    ppermute x1, starting transfers between devices, per_device(): rad_in = lax.ppermute(near, 'rad', swap)  2.21 us
    pallas_call x1, Pallas kernels, per_device(): pl.pallas_call(final, out_shape=[shaped(5, BAND, SECTOR, AXIAL), shaped(2...  1.92 us
    pallas_call x1, Pallas kernels, per_device(): pl.pallas_call(early, out_shape=[shaped(5, BAND, SECTOR, AXIAL), shaped(5...  1.46 us
    pallas_call x1, Pallas kernels, per_device(): pl.pallas_call(load_kernel, out_shape=[shaped(5, BAND, SECTOR, AXIAL)] *...  1.3 us
  transfers between devices with their start and end apart: 5, of which 2 were waited for; matrix products, arithmetic and copies ran while one was open for 0% of the time, Pallas kernels for 7%

profile of v7, /device:TPU:1, one launch (start us, length us, event | category | flops | bytes accessed | tf_op | source)
XLA Modules:
  0.0 48.9 jit_solution(7502017750993042091)
XLA Ops:
  0.6 0.8 %shard_map.61 = f32[5,8,256]{2,1,0:T(8,128)S(1)} custom-call(f32[5,16,8,256]{3,2,1,0:T(8,128)} %q_ref.3), custom_call_target="tpu_custom_call" | custom-call | tf_op jit(solution)/shard_map/pallas_call | solution.py:460
  1.4 2.2 %collective-permute-start = (f32[5,8,256]{2,1,0:T(8,128)S(1)}, f32[5,8,256]{2,1,0:T(8,128)S(1)}, u32[]{:S(2)}, u32[]{:S(2)}) collective-permute-start(f32[5,8,256]{2,1,0:T(8,128)S(1)} %shard_map.61), channel_id=1, source_target_pairs={{0,1},{1,0},{2,3},{3,2},{4,5},{5,4},{6,7},{7,6},{8,9},{9,8},{10,11... | collective-permute-start | bytes 122888 | tf_op jit(solution)/shard_map/ppermute | solution.py:468
  3.6 1.3 %shard_map.59 = (f32[5,16,8,256]{3,2,1,0:T(8,128)S(1)}, f32[5,16,8,256]{3,2,1,0:T(8,128)S(1)}) custom-call(f32[5,16,8,256]{3,2,1,0:T(8,128)} %q_ref.3, f32[5,16,8,256]{3,2,1,0:T(8,128)} %qp_ref.1), custom_call_target="tpu_custom_call" | custom-call | bytes 3000000 | tf_op jit(solution)/shard_map/pallas_call | solution.py:469
  5.0 0.0 copy-start.1
  5.0 0.7 %copy-done.1 = s32[256]{0:T(256)S(1)} copy-done((s32[256]{0:T(256)S(1)}, s32[256]{0:T(256)}, u32[]{:S(2)}) %copy-start.1) | copy-done | bytes 1048
  5.6 0.7 %shard_map.60.refs_1_ = f32[5,2,32,256]{3,2,1,0:T(8,128)S(1)} custom-call(s32[1,256]{1,0:T(1,128)S(1)} %bitcast.5, f32[5,16,8,256]{3,2,1,0:T(8,128)S(1)} %get-tuple-element.15.refs_1_.refs_0_, f32[5,16,8,256]{3,2,1,0:T(8,128)S(1)} %get-tuple-element.16.refs_2_), custom_call_target="tpu_custom_call" | custom-call | flops 5000000 | bytes 2000000 | tf_op jit(solution)/shard_map/pallas_call | solution.py:478
  6.3 0.0 collective-permute-done.refs_2_.refs_3_
  6.3 0.1 shard_map.62
  6.4 2.6 %collective-permute-start.2 = (f32[168,256]{1,0:T(8,128)S(1)}, f32[168,256]{1,0:T(8,128)S(1)}, u32[]{:S(2)}, u32[]{:S(2)}) collective-permute-start(f32[168,256]{1,0:T(8,128)S(1)} %get-tuple-element.21), channel_id=1, source_target_pairs={{0,254},{2,4},{4,2},{6,8},{8,6},{10,12},{12,10},{14,16},{16,14},{1... | collective-permute-start | bytes 516104 | tf_op jit(solution)/shard_map/ppermute | solution.py:495
  9.0 8.0 %collective-permute-start.3 = (f32[168,256]{1,0:T(8,128)S(1)}, f32[168,256]{1,0:T(8,128)S(1)}, u32[]{:S(2)}, u32[]{:S(2)}) collective-permute-start(f32[168,256]{1,0:T(8,128)S(1)} %get-tuple-element.22), channel_id=1, source_target_pairs={{0,2},{2,0},{4,6},{6,4},{8,10},{10,8},{12,14},{14,12},{16,18},{18,... | collective-permute-start | bytes 516104 | tf_op jit(solution)/shard_map/ppermute | solution.py:494
  17.0 1.5 %shard_map.63 = (f32[5,16,8,256]{3,2,1,0:T(8,128)S(1)}, f32[5,8,256]{2,1,0:T(8,128)S(1)}, f32[5,16,8,256]{3,2,1,0:T(8,128)S(1)}) custom-call(s32[1,256]{1,0:T(1,128)S(1)} %bitcast.6, f32[5,16,8,256]{3,2,1,0:T(8,128)S(1)} %get-tuple-element.15.refs_1_.refs_0_, f32[5,16,8,256]{3,2,1,0:T(8,128)S(1)} %get-tuple-element.16.refs_2_, ...), custom_call_target="tpu_custom_call" | custom-call | flops 10000000 | bytes 3500000 | tf_op jit(solution)/shard_map/pallas_call | solution.py:496
  18.5 0.1 collective-permute-start.1
  18.6 2.8 %collective-permute-done.1.refs_6_ = f32[5,8,256]{2,1,0:T(8,128)S(1)} collective-permute-done((f32[5,8,256]{2,1,0:T(8,128)S(1)}, f32[5,8,256]{2,1,0:T(8,128)S(1)}, u32[]{:S(2)}, u32[]{:S(2)}) %collective-permute-start.1) | collective-permute-done | bytes 40992 | tf_op jit(solution)/shard_map/ppermute | solution.py:504
  21.4 0.0 collective-permute-done.2.refs_7_
  21.4 0.0 collective-permute-done.3.refs_8_
  21.4 1.9 %shard_map.64 = (f32[5,16,8,256]{3,2,1,0:T(8,128)S(1)}, f32[512,128]{1,0:T(8,128)S(1)}) custom-call(s32[1,256]{1,0:T(1,128)S(1)} %bitcast.7, f32[5,2,32,256]{3,2,1,0:T(8,128)S(1)} %shard_map.60.refs_1_, f32[5,2,16,256]{3,2,1,0:T(8,128)S(1)} %get-tuple-element.17.refs_2_, f32[5,8,256]{2,1,0:T(8,128)S(1)} %collective-permute-done.refs_2_.refs_3_, ...), custom_call_target="tpu_custom_call" | custom-call | tf_op jit(solution)/shard_map/pallas_call | solution.py:505
  23.3 0.0 copy-start
  23.3 22.8 %all_to_all.5 = f32[64,8,128]{2,1,0:T(8,128)S(1)} all-to-all(f32[64,8,128]{2,1,0:T(8,128)S(1)} %bitcast.4), channel_id=1, replica_groups={{0,4,8,12,16,20,24,28,32,36,40,44,48,52,56,60,64,68,72,76,80,84,88,92,9..., dimensions={0} | all-to-all | bytes 524288 | tf_op jit(solution)/shard_map/all_to_all | solution.py:519
  46.1 0.0 copy-done
  46.1 0.9 %shard_map.65 = (f32[64,128]{1,0:T(8,128)S(1)}, f32[64,128]{1,0:T(8,128)S(1)}, f32[5,16,8,256]{3,2,1,0:T(8,128)}) custom-call(f32[512,128]{1,0:T(8,128)S(1)} %bitcast.3, f32[2,512,128]{2,1,0:T(8,128)S(1)} %copy-done, f32[5,16,8,256]{3,2,1,0:T(8,128)S(1)} %get-tuple-element.24.flow_ref), custom_call_target="tpu_custom_call" | custom-call | tf_op jit(solution)/shard_map/pallas_call | solution.py:527
  47.0 0.1 collective-permute-start.4
  47.1 1.2 %collective-permute-done.4.got_ref = f32[64,128]{1,0:T(8,128)S(1)} collective-permute-done((f32[64,128]{1,0:T(8,128)S(1)}, f32[64,128]{1,0:T(8,128)S(1)}, u32[]{:S(2)}, u32[]{:S(2)}) %collective-permute-start.4) | collective-permute-done | bytes 32800 | tf_op jit(solution)/shard_map/ppermute | solution.py:541
  48.3 0.6 %shard_map.66 = f32[2,16,256]{2,1,0:T(8,128)} custom-call(f32[64,128]{1,0:T(8,128)S(1)} %get-tuple-element.26.keep_ref, f32[64,128]{1,0:T(8,128)S(1)} %collective-permute-done.4.got_ref), custom_call_target="tpu_custom_call" | custom-call | tf_op jit(solution)/shard_map/pallas_call | solution.py:535
Async XLA Ops:
  1.4 4.9 %collective-permute-start = (f32[5,8,256]{2,1,0:T(8,128)S(1)}, f32[5,8,256]{2,1,0:T(8,128)S(1)}, u32[]{:S(2)}, u32[]{:S(2)}) collective-permute-start(f32[5,8,256]{2,1,0:T(8,128)S(1)} %shard_map.61), channel_id=1, source_target_pairs={{0,1},{1,0},{2,3},{3,2},{4,5},{5,4},{6,7},{7,6},{8,9},{9,8},{10,11... | collective-permute-start | bytes 122888 | tf_op jit(solution)/shard_map/ppermute | solution.py:468
  5.0 0.7 %copy-start.1 = (s32[256]{0:T(256)S(1)}, s32[256]{0:T(256)}, u32[]{:S(2)}) copy-start(s32[256]{0:T(256)} %param.6) | copy-start | bytes 3076
  6.4 15.0 %collective-permute-start.2 = (f32[168,256]{1,0:T(8,128)S(1)}, f32[168,256]{1,0:T(8,128)S(1)}, u32[]{:S(2)}, u32[]{:S(2)}) collective-permute-start(f32[168,256]{1,0:T(8,128)S(1)} %get-tuple-element.21), channel_id=1, source_target_pairs={{0,254},{2,4},{4,2},{6,8},{8,6},{10,12},{12,10},{14,16},{16,14},{1... | collective-permute-start | bytes 516104 | tf_op jit(solution)/shard_map/ppermute | solution.py:495
  9.0 12.4 %collective-permute-start.3 = (f32[168,256]{1,0:T(8,128)S(1)}, f32[168,256]{1,0:T(8,128)S(1)}, u32[]{:S(2)}, u32[]{:S(2)}) collective-permute-start(f32[168,256]{1,0:T(8,128)S(1)} %get-tuple-element.22), channel_id=1, source_target_pairs={{0,2},{2,0},{4,6},{6,4},{8,10},{10,8},{12,14},{14,12},{16,18},{18,... | collective-permute-start | bytes 516104 | tf_op jit(solution)/shard_map/ppermute | solution.py:494
  18.5 2.9 %collective-permute-start.1 = (f32[5,8,256]{2,1,0:T(8,128)S(1)}, f32[5,8,256]{2,1,0:T(8,128)S(1)}, u32[]{:S(2)}, u32[]{:S(2)}) collective-permute-start(f32[5,8,256]{2,1,0:T(8,128)S(1)} %get-tuple-element.20), channel_id=1, source_target_pairs={{0,1},{1,0},{2,3},{3,2},{4,5},{5,4},{6,7},{7,6},{8,9},{9,8},{10,11... | collective-permute-start | bytes 122888 | tf_op jit(solution)/shard_map/ppermute | solution.py:504
  23.3 22.8 %copy-start = (f32[2,512,128]{2,1,0:T(8,128)S(1)}, f32[2,512,128]{2,1,0:T(8,128)}, u32[]{:S(2)}) copy-start(f32[2,512,128]{2,1,0:T(8,128)} %constant.2.clone.basis_ref) | copy-start | bytes 1572868
  47.0 1.3 %collective-permute-start.4 = (f32[64,128]{1,0:T(8,128)S(1)}, f32[64,128]{1,0:T(8,128)S(1)}, u32[]{:S(2)}, u32[]{:S(2)}) collective-permute-start(f32[64,128]{1,0:T(8,128)S(1)} %get-tuple-element.27), channel_id=1, source_target_pairs={{0,2},{2,0},{4,6},{6,4},{8,10},{10,8},{12,14},{14,12},{16,18},{18,... | collective-permute-start | bytes 98312 | tf_op jit(solution)/shard_map/ppermute | solution.py:541

commit v8 on v7

--- a/solution.py
+++ b/solution.py
@@ -265,9 +265,28 @@
         q, prim, g_in = above, above_prim, g_out
 
 
-def early_kernel(table, blade_ref, q_ref, qp_ref, rad_ref, p1_ref, edge_ref, source_ref):
+def next_kernel(table, blade_ref, q_ref, qp_ref, rad_ref, next_ref):
     band = lax.axis_index("rad")
     low = band == 0
+    edge_at = edge_row(band, BAND - 1, 0)
+    edge = [q_ref[v, edge_at] for v in ALL]
+    inner = [q_ref[v, edge_row(band, BAND - 2, 1)] for v in ALL]
+    near = [rad_ref[v] for v in ALL]
+    prim = primitives(edge)
+    f = flux(edge, prim, 2)
+    below = [jnp.where(low, inner[v], near[v]) for v in ALL]
+    above = [jnp.where(low, near[v], inner[v]) for v in ALL]
+    g_in = face(below, flux(below, primitives(below), 2), edge, f)
+    g_out = face(edge, f, above, flux(above, primitives(above), 2))
+    source = [40.0 * edge[v] - 10.0 * qp_ref[v, edge_at] for v in ALL]
+    coefs = [jnp.where(low, a, b) for a, b in zip(coefficients(low, table, BAND - 1), coefficients(low, table, 0))]
+    stepped = row_step(coefs, edge, prim, source, g_in, g_out, None, masks(), blades(blade_ref, SECTOR))
+    for v in ALL:
+        next_ref[v] = stepped[v]
+
+
+def early_kernel(table, blade_ref, q_ref, qp_ref, rad_ref, p1_ref, source_ref):
+    low = lax.axis_index("rad") == 0
     mask = masks()
     blade = blades(blade_ref, SECTOR)
 
@@ -289,8 +308,6 @@
             p1_ref[v, j] = q[v]
 
     sweep(load, step, store)
-    for v in ALL:
-        edge_ref[v] = p1_ref[v, edge_row(band, BAND - 1, 0)]
 
 
 def final_kernel(
@@ -450,6 +467,9 @@
 
     def pack(*refs):
         pack_kernel(table, *refs)
+
+    def neighbour(*refs):
+        next_kernel(table, *refs)
 
     def early(*refs):
         early_kernel(table, *refs)
@@ -493,15 +513,22 @@
     )(q_level, edge_columns, rad_in)
     core_in = lax.ppermute(core_out, "theta", core)
     other_in = lax.ppermute(other_out, "theta", other)
-    part, edge, source = pl.pallas_call(
+    next_out = pl.pallas_call(
+        neighbour,
+        out_shape=shaped(5, SECTOR, AXIAL),
+        in_specs=[vmem()] * 4,
+        out_specs=vmem(),
+        compiler_params=limit(4),
+    )(blade, q_level, q_prev, rad_in)
+    next_in = lax.ppermute(next_out, "rad", swap)
+    part, source = pl.pallas_call(
         early,
-        out_shape=[shaped(5, BAND, SECTOR, AXIAL), shaped(5, SECTOR, AXIAL), shaped(5, BAND, SECTOR, AXIAL)],
+        out_shape=[shaped(5, BAND, SECTOR, AXIAL)] * 2,
         in_specs=[vmem()] * 4,
-        out_specs=[vmem()] * 3,
+        out_specs=[vmem()] * 2,
         compiler_params=limit(8),
         cost_estimate=pl.CostEstimate(flops=10_000_000, bytes_accessed=3_500_000, transcendentals=100_000),
     )(blade, q_level, q_prev, rad_in)
-    next_in = lax.ppermute(edge, "rad", swap)
     flow_state, send = pl.pallas_call(
         final,
         out_shape=[shaped(5, BAND, SECTOR, AXIAL), shaped(2 * AXIAL, BAND * SECTOR)],

time: 49.1 us -> 48.5 us (0.988)
  waiting for transfers between devices: 4.04 us -> 2.58 us
  blocking collectives: 22.8 us -> 23.4 us
    ppermute x1, waiting for transfers between devices: 2.84 us -> 1.38 us  [per_device(): next_in = lax.ppermute(next_out, 'rad', swap)]
    all_to_all x1, blocking collectives: 22.8 us -> 23.4 us  [per_device(): lax.all_to_all(send.reshape(chips, 8, 128), 'theta', split_axis=0, concat...]
    pallas_call x1 -> x2, Pallas kernels: 1.46 us -> 1.63 us  [the longest x1 1.45 us: per_device(): pl.pallas_call(early, out_shape=[shaped(5, BAND, SECTOR, AXIAL)] * 2, in_...]
where the time goes in v8:
time: 48.5 us; the launch traced here: 48.3 us
  blocking collectives  23.4 us (48%)
  starting transfers between devices  13 us (27%)
  Pallas kernels  7.88 us (16%)
  waiting for transfers between devices  2.58 us (5%)
  between operations  0.73 us (2%)
  local copies, waits for them, and re-layouts  0.68 us (1%)
    all_to_all x1, blocking collectives, per_device(): lax.all_to_all(send.reshape(chips, 8, 128), 'theta', split_axis=0, concat...  23.4 us
    ppermute x1, starting transfers between devices, per_device(): core_in = lax.ppermute(core_out, 'theta', core)  8.02 us
    ppermute x1, starting transfers between devices, per_device(): other_in = lax.ppermute(other_out, 'theta', other)  2.56 us
    ppermute x1, starting transfers between devices, per_device(): rad_in = lax.ppermute(near, 'rad', swap)  2.21 us
    pallas_call x1, Pallas kernels, per_device(): pl.pallas_call(final, out_shape=[shaped(5, BAND, SECTOR, AXIAL), shaped(2...  1.92 us
    pallas_call x1, Pallas kernels, per_device(): pl.pallas_call(early, out_shape=[shaped(5, BAND, SECTOR, AXIAL)] * 2, in_...  1.45 us
    ppermute x1, waiting for transfers between devices, per_device(): next_in = lax.ppermute(next_out, 'rad', swap)  1.38 us
    pallas_call x1, Pallas kernels, per_device(): pl.pallas_call(load_kernel, out_shape=[shaped(5, BAND, SECTOR, AXIAL)] *...  1.3 us
  transfers between devices with their start and end apart: 5, of which 2 were waited for; matrix products, arithmetic and copies ran while one was open for 0% of the time, Pallas kernels for 7%

profile of v8, /device:TPU:1, one launch (start us, length us, event | category | flops | bytes accessed | tf_op | source)
XLA Modules:
  0.0 48.3 jit_solution(563232744339286117)
XLA Ops:
  0.6 0.8 %shard_map.61 = f32[5,8,256]{2,1,0:T(8,128)S(1)} custom-call(f32[5,16,8,256]{3,2,1,0:T(8,128)} %q_ref.3), custom_call_target="tpu_custom_call" | custom-call | tf_op jit(solution)/shard_map/pallas_call | solution.py:480
  1.4 2.2 %collective-permute-start = (f32[5,8,256]{2,1,0:T(8,128)S(1)}, f32[5,8,256]{2,1,0:T(8,128)S(1)}, u32[]{:S(2)}, u32[]{:S(2)}) collective-permute-start(f32[5,8,256]{2,1,0:T(8,128)S(1)} %shard_map.61), channel_id=1, source_target_pairs={{0,1},{1,0},{2,3},{3,2},{4,5},{5,4},{6,7},{7,6},{8,9},{9,8},{10,11... | collective-permute-start | bytes 122888 | tf_op jit(solution)/shard_map/ppermute | solution.py:488
  3.6 1.3 %shard_map.59 = (f32[5,16,8,256]{3,2,1,0:T(8,128)S(1)}, f32[5,16,8,256]{3,2,1,0:T(8,128)S(1)}) custom-call(f32[5,16,8,256]{3,2,1,0:T(8,128)} %q_ref.3, f32[5,16,8,256]{3,2,1,0:T(8,128)} %qp_ref.1), custom_call_target="tpu_custom_call" | custom-call | bytes 3000000 | tf_op jit(solution)/shard_map/pallas_call | solution.py:489
  5.0 0.0 copy-start.1
  5.0 0.7 %copy-done.1 = s32[256]{0:T(256)S(1)} copy-done((s32[256]{0:T(256)S(1)}, s32[256]{0:T(256)}, u32[]{:S(2)}) %copy-start.1) | copy-done | bytes 1048
  5.6 0.7 %shard_map.60.refs_1_ = f32[5,2,32,256]{3,2,1,0:T(8,128)S(1)} custom-call(s32[1,256]{1,0:T(1,128)S(1)} %bitcast.5, f32[5,16,8,256]{3,2,1,0:T(8,128)S(1)} %get-tuple-element.14.refs_1_.refs_0_, f32[5,16,8,256]{3,2,1,0:T(8,128)S(1)} %get-tuple-element.15.refs_2_), custom_call_target="tpu_custom_call" | custom-call | flops 5000000 | bytes 2000000 | tf_op jit(solution)/shard_map/pallas_call | solution.py:498
  6.3 0.0 collective-permute-done.refs_2_.refs_3_
  6.3 0.1 shard_map.62
  6.4 2.6 %collective-permute-start.2 = (f32[168,256]{1,0:T(8,128)S(1)}, f32[168,256]{1,0:T(8,128)S(1)}, u32[]{:S(2)}, u32[]{:S(2)}) collective-permute-start(f32[168,256]{1,0:T(8,128)S(1)} %get-tuple-element.19), channel_id=1, source_target_pairs={{0,254},{2,4},{4,2},{6,8},{8,6},{10,12},{12,10},{14,16},{16,14},{1... | collective-permute-start | bytes 516104 | tf_op jit(solution)/shard_map/ppermute | solution.py:515
  9.0 8.0 %collective-permute-start.3 = (f32[168,256]{1,0:T(8,128)S(1)}, f32[168,256]{1,0:T(8,128)S(1)}, u32[]{:S(2)}, u32[]{:S(2)}) collective-permute-start(f32[168,256]{1,0:T(8,128)S(1)} %get-tuple-element.20), channel_id=1, source_target_pairs={{0,2},{2,0},{4,6},{6,4},{8,10},{10,8},{12,14},{14,12},{16,18},{18,... | collective-permute-start | bytes 516104 | tf_op jit(solution)/shard_map/ppermute | solution.py:514
  17.0 0.2 shard_map.64
  17.2 0.1 collective-permute-start.1
  17.3 1.5 %shard_map.63 = (f32[5,16,8,256]{3,2,1,0:T(8,128)S(1)}, f32[5,16,8,256]{3,2,1,0:T(8,128)S(1)}) custom-call(s32[1,256]{1,0:T(1,128)S(1)} %bitcast.7, f32[5,16,8,256]{3,2,1,0:T(8,128)S(1)} %get-tuple-element.14.refs_1_.refs_0_, f32[5,16,8,256]{3,2,1,0:T(8,128)S(1)} %get-tuple-element.15.refs_2_, f32[5,8,256]{2,1,0:T(8,128)S(1)} %collective-permute-done.refs_2_.refs_3_), custom_call_target="tpu_custom_call" | custom-call | flops 10000000 | bytes 3500000 | tf_op jit(solution)/shard_map/pallas_call | solution.py:524
  18.7 1.4 %collective-permute-done.1.refs_6_ = f32[5,8,256]{2,1,0:T(8,128)S(1)} collective-permute-done((f32[5,8,256]{2,1,0:T(8,128)S(1)}, f32[5,8,256]{2,1,0:T(8,128)S(1)}, u32[]{:S(2)}, u32[]{:S(2)}) %collective-permute-start.1) | collective-permute-done | bytes 40992 | tf_op jit(solution)/shard_map/ppermute | solution.py:523
  20.1 0.0 collective-permute-done.2.refs_7_
  20.1 0.0 collective-permute-done.3.refs_8_
  20.1 1.9 %shard_map.65 = (f32[5,16,8,256]{3,2,1,0:T(8,128)S(1)}, f32[512,128]{1,0:T(8,128)S(1)}) custom-call(s32[1,256]{1,0:T(1,128)S(1)} %bitcast.8, f32[5,2,32,256]{3,2,1,0:T(8,128)S(1)} %shard_map.60.refs_1_, f32[5,2,16,256]{3,2,1,0:T(8,128)S(1)} %get-tuple-element.16.refs_2_, f32[5,8,256]{2,1,0:T(8,128)S(1)} %collective-permute-done.refs_2_.refs_3_, ...), custom_call_target="tpu_custom_call" | custom-call | tf_op jit(solution)/shard_map/pallas_call | solution.py:532
  22.1 0.0 copy-start
  22.1 23.4 %all_to_all.5 = f32[64,8,128]{2,1,0:T(8,128)S(1)} all-to-all(f32[64,8,128]{2,1,0:T(8,128)S(1)} %bitcast.4), channel_id=1, replica_groups={{0,4,8,12,16,20,24,28,32,36,40,44,48,52,56,60,64,68,72,76,80,84,88,92,9..., dimensions={0} | all-to-all | bytes 524288 | tf_op jit(solution)/shard_map/all_to_all | solution.py:546
  45.5 0.0 copy-done
  45.5 0.9 %shard_map.66 = (f32[64,128]{1,0:T(8,128)S(1)}, f32[64,128]{1,0:T(8,128)S(1)}, f32[5,16,8,256]{3,2,1,0:T(8,128)}) custom-call(f32[512,128]{1,0:T(8,128)S(1)} %bitcast.3, f32[2,512,128]{2,1,0:T(8,128)S(1)} %copy-done, f32[5,16,8,256]{3,2,1,0:T(8,128)S(1)} %get-tuple-element.22.flow_ref), custom_call_target="tpu_custom_call" | custom-call | tf_op jit(solution)/shard_map/pallas_call | solution.py:554
  46.4 0.1 collective-permute-start.4
  46.5 1.2 %collective-permute-done.4.got_ref = f32[64,128]{1,0:T(8,128)S(1)} collective-permute-done((f32[64,128]{1,0:T(8,128)S(1)}, f32[64,128]{1,0:T(8,128)S(1)}, u32[]{:S(2)}, u32[]{:S(2)}) %collective-permute-start.4) | collective-permute-done | bytes 32800 | tf_op jit(solution)/shard_map/ppermute | solution.py:568
  47.7 0.6 %shard_map.67 = f32[2,16,256]{2,1,0:T(8,128)} custom-call(f32[64,128]{1,0:T(8,128)S(1)} %get-tuple-element.24.keep_ref, f32[64,128]{1,0:T(8,128)S(1)} %collective-permute-done.4.got_ref), custom_call_target="tpu_custom_call" | custom-call | tf_op jit(solution)/shard_map/pallas_call | solution.py:562
Async XLA Ops:
  1.4 4.9 %collective-permute-start = (f32[5,8,256]{2,1,0:T(8,128)S(1)}, f32[5,8,256]{2,1,0:T(8,128)S(1)}, u32[]{:S(2)}, u32[]{:S(2)}) collective-permute-start(f32[5,8,256]{2,1,0:T(8,128)S(1)} %shard_map.61), channel_id=1, source_target_pairs={{0,1},{1,0},{2,3},{3,2},{4,5},{5,4},{6,7},{7,6},{8,9},{9,8},{10,11... | collective-permute-start | bytes 122888 | tf_op jit(solution)/shard_map/ppermute | solution.py:488
  5.0 0.7 %copy-start.1 = (s32[256]{0:T(256)S(1)}, s32[256]{0:T(256)}, u32[]{:S(2)}) copy-start(s32[256]{0:T(256)} %param.6) | copy-start | bytes 3076
  6.4 13.7 %collective-permute-start.2 = (f32[168,256]{1,0:T(8,128)S(1)}, f32[168,256]{1,0:T(8,128)S(1)}, u32[]{:S(2)}, u32[]{:S(2)}) collective-permute-start(f32[168,256]{1,0:T(8,128)S(1)} %get-tuple-element.19), channel_id=1, source_target_pairs={{0,254},{2,4},{4,2},{6,8},{8,6},{10,12},{12,10},{14,16},{16,14},{1... | collective-permute-start | bytes 516104 | tf_op jit(solution)/shard_map/ppermute | solution.py:515
  9.0 11.2 %collective-permute-start.3 = (f32[168,256]{1,0:T(8,128)S(1)}, f32[168,256]{1,0:T(8,128)S(1)}, u32[]{:S(2)}, u32[]{:S(2)}) collective-permute-start(f32[168,256]{1,0:T(8,128)S(1)} %get-tuple-element.20), channel_id=1, source_target_pairs={{0,2},{2,0},{4,6},{6,4},{8,10},{10,8},{12,14},{14,12},{16,18},{18,... | collective-permute-start | bytes 516104 | tf_op jit(solution)/shard_map/ppermute | solution.py:514
  17.2 2.9 %collective-permute-start.1 = (f32[5,8,256]{2,1,0:T(8,128)S(1)}, f32[5,8,256]{2,1,0:T(8,128)S(1)}, u32[]{:S(2)}, u32[]{:S(2)}) collective-permute-start(f32[5,8,256]{2,1,0:T(8,128)S(1)} %shard_map.64), channel_id=1, source_target_pairs={{0,1},{1,0},{2,3},{3,2},{4,5},{5,4},{6,7},{7,6},{8,9},{9,8},{10,11... | collective-permute-start | bytes 122888 | tf_op jit(solution)/shard_map/ppermute | solution.py:523
  22.1 23.5 %copy-start = (f32[2,512,128]{2,1,0:T(8,128)S(1)}, f32[2,512,128]{2,1,0:T(8,128)}, u32[]{:S(2)}) copy-start(f32[2,512,128]{2,1,0:T(8,128)} %constant.2.clone.basis_ref) | copy-start | bytes 1572868
  46.4 1.3 %collective-permute-start.4 = (f32[64,128]{1,0:T(8,128)S(1)}, f32[64,128]{1,0:T(8,128)S(1)}, u32[]{:S(2)}, u32[]{:S(2)}) collective-permute-start(f32[64,128]{1,0:T(8,128)S(1)} %get-tuple-element.25), channel_id=1, source_target_pairs={{0,2},{2,0},{4,6},{6,4},{8,10},{10,8},{12,14},{14,12},{16,18},{18,... | collective-permute-start | bytes 98312 | tf_op jit(solution)/shard_map/ppermute | solution.py:568

commit v9 on v8

--- a/solution.py
+++ b/solution.py
@@ -15,7 +15,6 @@
 BAND = 16
 SECTOR = 8
 AXIAL = 256
-RAD_VMEM = 56_200_000
 LOAD_VMEM = 55_000_000
 F32 = jnp.float32
 ALL = range(5)
@@ -121,16 +120,11 @@
     return bladed, rotor
 
 
-def rad_kernel(q_ref, near_ref, sem):
-    copy = pltpu.make_async_copy(q_ref.at[:, edge_row(lax.axis_index("rad"), BAND - 1, 0)], near_ref, sem)
-    copy.start()
-    copy.wait()
-
-
-def load_kernel(q_ref, qp_ref, q_out_ref, qp_out_ref, sems):
+def load_kernel(q_ref, qp_ref, near_ref, q_out_ref, qp_out_ref, sems):
     copies = [
-        pltpu.make_async_copy(q_ref, q_out_ref, sems.at[0]),
-        pltpu.make_async_copy(qp_ref, qp_out_ref, sems.at[1]),
+        pltpu.make_async_copy(q_ref.at[:, edge_row(lax.axis_index("rad"), BAND - 1, 0)], near_ref, sems.at[0]),
+        pltpu.make_async_copy(q_ref, q_out_ref, sems.at[1]),
+        pltpu.make_async_copy(qp_ref, qp_out_ref, sems.at[2]),
     ]
     for copy in copies:
         copy.start()
@@ -399,9 +393,13 @@
         send_ref[pl.ds(f, AXIAL, stride=2), :] = turned
 
 
-def mode_kernel(got_ref, basis_ref, flow_ref, keep_ref, give_ref, flow_out_ref, turned, sem):
-    copy = pltpu.make_async_copy(flow_ref, flow_out_ref, sem)
+def write_kernel(flow_ref, out_ref, sem):
+    copy = pltpu.make_async_copy(flow_ref, out_ref, sem)
     copy.start()
+    copy.wait()
+
+
+def mode_kernel(got_ref, basis_ref, keep_ref, give_ref, turned):
     chips = got_ref.shape[0] // 8
     core = lax.axis_index("theta") % 2
     left = lax.broadcasted_iota(jnp.int32, (BAND, 2 * chips), 1) < chips
@@ -419,7 +417,6 @@
     half = 4 * BAND
     keep_ref[...] = jnp.where(core == 0, product[:half], product[half:])
     give_ref[...] = jnp.where(core == 0, product[half:], product[:half])
-    copy.wait()
 
 
 def sum_kernel(keep_ref, got_ref, out_ref):
@@ -477,24 +474,16 @@
     def final(*refs):
         final_kernel(bands * BAND, circle, table, *refs)
 
-    near = pl.pallas_call(
-        rad_kernel,
-        out_shape=shaped(5, SECTOR, AXIAL),
-        in_specs=[hbm],
-        out_specs=vmem(),
-        scratch_shapes=[pltpu.SemaphoreType.DMA],
-        compiler_params=pltpu.CompilerParams(vmem_limit_bytes=RAD_VMEM),
-    )(q_level)
-    rad_in = lax.ppermute(near, "rad", swap)
-    q_level, q_prev = pl.pallas_call(
+    near, q_level, q_prev = pl.pallas_call(
         load_kernel,
-        out_shape=[shaped(5, BAND, SECTOR, AXIAL)] * 2,
+        out_shape=[shaped(5, SECTOR, AXIAL)] + [shaped(5, BAND, SECTOR, AXIAL)] * 2,
         in_specs=[hbm] * 2,
-        out_specs=[vmem()] * 2,
-        scratch_shapes=[pltpu.SemaphoreType.DMA((2,))],
+        out_specs=[vmem()] * 3,
+        scratch_shapes=[pltpu.SemaphoreType.DMA((3,))],
         compiler_params=pltpu.CompilerParams(vmem_limit_bytes=LOAD_VMEM),
         cost_estimate=pl.CostEstimate(flops=0, bytes_accessed=3_000_000, transcendentals=0),
     )(q_level, q_prev)
+    rad_in = lax.ppermute(near, "rad", swap)
     edge_columns = pl.pallas_call(
         edges,
         out_shape=shaped(5, 2, 32, AXIAL),
@@ -551,21 +540,31 @@
         tiled=True,
         axis_index_groups=[[2 * chip + c for chip in range(chips)] for c in (0, 1)],
     )
-    keep, give, flow_state = pl.pallas_call(
+    keep, give = pl.pallas_call(
         mode_kernel,
-        out_shape=[shaped(4 * BAND, 2 * MODES)] * 2 + [shaped(5, BAND, SECTOR, AXIAL)],
-        in_specs=[vmem()] * 3,
-        out_specs=[vmem(), vmem(), hbm],
-        scratch_shapes=[pltpu.VMEM((8, BAND * SECTOR, 2 * chips), F32), pltpu.SemaphoreType.DMA],
+        out_shape=[shaped(4 * BAND, 2 * MODES)] * 2,
+        in_specs=[vmem()] * 2,
+        out_specs=[vmem()] * 2,
+        scratch_shapes=[pltpu.VMEM((8, BAND * SECTOR, 2 * chips), F32)],
         compiler_params=limit(4),
-    )(got.reshape(8 * chips, 128), jnp.asarray(mode_basis(sectors)), flow_state)
+    )(got.reshape(8 * chips, 128), jnp.asarray(mode_basis(sectors)))
+    given = lax.ppermute(give, "theta", core)
+    flow_state = pl.pallas_call(
+        write_kernel,
+        out_shape=shaped(5, BAND, SECTOR, AXIAL),
+        in_specs=[vmem()],
+        out_specs=hbm,
+        scratch_shapes=[pltpu.SemaphoreType.DMA],
+        compiler_params=limit(2),
+        cost_estimate=pl.CostEstimate(flops=0, bytes_accessed=1_400_000, transcendentals=0),
+    )(flow_state)
     spectra = pl.pallas_call(
         sum_kernel,
         out_shape=shaped(2, BAND, 4 * MODES),
         in_specs=[vmem()] * 2,
         out_specs=vmem(),
         compiler_params=limit(2),
-    )(keep, lax.ppermute(give, "theta", core))
+    )(keep, given)
     return flow_state, spectra
 
 

time: 48.5 us -> 48.5 us (level)
  waiting for transfers between devices: 2.58 us -> 1.31 us
  starting transfers between devices: 13 us -> 13.8 us
  blocking collectives: 23.4 us -> 24.1 us
    ppermute x1, starting transfers between devices: 2.56 us -> 3.57 us  [per_device(): other_in = lax.ppermute(other_out, 'theta', other)]
    ppermute x1, waiting for transfers between devices: 1.19 us -> 0.34 us  [per_device(): given = lax.ppermute(give, 'theta', core)]
    all_to_all x1, blocking collectives: 23.4 us -> 24.1 us  [per_device(): lax.all_to_all(send.reshape(chips, 8, 128), 'theta', split_axis=0, concat...]
    ppermute x1, starting transfers between devices: 8.02 us -> 7.45 us  [per_device(): core_in = lax.ppermute(core_out, 'theta', core)]
where the time goes in v9:
time: 48.5 us; the launch traced here: 48.4 us
  blocking collectives  24.1 us (50%)
  starting transfers between devices  13.8 us (28%)
  Pallas kernels  7.77 us (16%)
  waiting for transfers between devices  1.31 us (3%)
  between operations  0.71 us (1%)
  local copies, waits for them, and re-layouts  0.69 us (1%)
    all_to_all x1, blocking collectives, per_device(): lax.all_to_all(send.reshape(chips, 8, 128), 'theta', split_axis=0, concat...  24.1 us
    ppermute x1, starting transfers between devices, per_device(): core_in = lax.ppermute(core_out, 'theta', core)  7.45 us
    ppermute x1, starting transfers between devices, per_device(): other_in = lax.ppermute(other_out, 'theta', other)  3.57 us
    ppermute x1, starting transfers between devices, per_device(): rad_in = lax.ppermute(near, 'rad', swap)  2.21 us
    pallas_call x1, Pallas kernels, per_device(): pl.pallas_call(final, out_shape=[shaped(5, BAND, SECTOR, AXIAL), shaped(2...  1.92 us
    pallas_call x1, Pallas kernels, per_device(): pl.pallas_call(early, out_shape=[shaped(5, BAND, SECTOR, AXIAL)] * 2, in_...  1.48 us
    pallas_call x1, Pallas kernels, per_device(): pl.pallas_call(load_kernel, out_shape=[shaped(5, SECTOR, AXIAL)] + [shape...  1.35 us
  transfers between devices with their start and end apart: 5, of which 2 were waited for; matrix products, arithmetic and copies ran while one was open for 0% of the time, Pallas kernels for 7%

profile of v9, /device:TPU:1, one launch (start us, length us, event | category | flops | bytes accessed | tf_op | source)
XLA Modules:
  0.0 48.4 jit_solution(14222785319411874959)
XLA Ops:
  0.6 1.3 %shard_map.59 = (f32[5,8,256]{2,1,0:T(8,128)S(1)}, f32[5,16,8,256]{3,2,1,0:T(8,128)S(1)}, f32[5,16,8,256]{3,2,1,0:T(8,128)S(1)}) custom-call(f32[5,16,8,256]{3,2,1,0:T(8,128)} %q_ref.1, f32[5,16,8,256]{3,2,1,0:T(8,128)} %qp_ref.1), custom_call_target="tpu_custom_call" | custom-call | bytes 3000000 | tf_op jit(solution)/shard_map/pallas_call | solution.py:477
  2.0 2.2 %collective-permute-start = (f32[5,8,256]{2,1,0:T(8,128)S(1)}, f32[5,8,256]{2,1,0:T(8,128)S(1)}, u32[]{:S(2)}, u32[]{:S(2)}) collective-permute-start(f32[5,8,256]{2,1,0:T(8,128)S(1)} %get-tuple-element.16), channel_id=1, source_target_pairs={{0,1},{1,0},{2,3},{3,2},{4,5},{5,4},{6,7},{7,6},{8,9},{9,8},{10,11... | collective-permute-start | bytes 122888 | tf_op jit(solution)/shard_map/ppermute | solution.py:486
  4.2 0.0 copy-start.1
  4.2 0.7 %copy-done.1 = s32[256]{0:T(256)S(1)} copy-done((s32[256]{0:T(256)S(1)}, s32[256]{0:T(256)}, u32[]{:S(2)}) %copy-start.1) | copy-done | bytes 1048
  4.9 0.7 %shard_map.60.refs_1_ = f32[5,2,32,256]{3,2,1,0:T(8,128)S(1)} custom-call(s32[1,256]{1,0:T(1,128)S(1)} %bitcast.5, f32[5,16,8,256]{3,2,1,0:T(8,128)S(1)} %get-tuple-element.14.refs_1_.refs_0_, f32[5,16,8,256]{3,2,1,0:T(8,128)S(1)} %get-tuple-element.15.refs_2_), custom_call_target="tpu_custom_call" | custom-call | flops 5000000 | bytes 2000000 | tf_op jit(solution)/shard_map/pallas_call | solution.py:487
  5.6 0.0 collective-permute-done.refs_2_.refs_3_
  5.6 0.1 shard_map.61
  5.7 3.6 %collective-permute-start.2 = (f32[168,256]{1,0:T(8,128)S(1)}, f32[168,256]{1,0:T(8,128)S(1)}, u32[]{:S(2)}, u32[]{:S(2)}) collective-permute-start(f32[168,256]{1,0:T(8,128)S(1)} %get-tuple-element.20), channel_id=1, source_target_pairs={{0,254},{2,4},{4,2},{6,8},{8,6},{10,12},{12,10},{14,16},{16,14},{1... | collective-permute-start | bytes 516104 | tf_op jit(solution)/shard_map/ppermute | solution.py:504
  9.3 7.4 %collective-permute-start.3 = (f32[168,256]{1,0:T(8,128)S(1)}, f32[168,256]{1,0:T(8,128)S(1)}, u32[]{:S(2)}, u32[]{:S(2)}) collective-permute-start(f32[168,256]{1,0:T(8,128)S(1)} %get-tuple-element.21), channel_id=1, source_target_pairs={{0,2},{2,0},{4,6},{6,4},{8,10},{10,8},{12,14},{14,12},{16,18},{18,... | collective-permute-start | bytes 516104 | tf_op jit(solution)/shard_map/ppermute | solution.py:503
  16.7 0.2 shard_map.63
  16.9 0.5 collective-permute-start.1
  17.4 1.5 %shard_map.62 = (f32[5,16,8,256]{3,2,1,0:T(8,128)S(1)}, f32[5,16,8,256]{3,2,1,0:T(8,128)S(1)}) custom-call(s32[1,256]{1,0:T(1,128)S(1)} %bitcast.7, f32[5,16,8,256]{3,2,1,0:T(8,128)S(1)} %get-tuple-element.14.refs_1_.refs_0_, f32[5,16,8,256]{3,2,1,0:T(8,128)S(1)} %get-tuple-element.15.refs_2_, f32[5,8,256]{2,1,0:T(8,128)S(1)} %collective-permute-done.refs_2_.refs_3_), custom_call_target="tpu_custom_call" | custom-call | flops 10000000 | bytes 3500000 | tf_op jit(solution)/shard_map/pallas_call | solution.py:513
  18.9 1.0 %collective-permute-done.1.refs_6_ = f32[5,8,256]{2,1,0:T(8,128)S(1)} collective-permute-done((f32[5,8,256]{2,1,0:T(8,128)S(1)}, f32[5,8,256]{2,1,0:T(8,128)S(1)}, u32[]{:S(2)}, u32[]{:S(2)}) %collective-permute-start.1) | collective-permute-done | bytes 40992 | tf_op jit(solution)/shard_map/ppermute | solution.py:512
  19.8 0.0 collective-permute-done.2.refs_7_
  19.9 0.0 collective-permute-done.3.refs_8_
  19.9 1.9 %shard_map.64 = (f32[5,16,8,256]{3,2,1,0:T(8,128)S(1)}, f32[512,128]{1,0:T(8,128)S(1)}) custom-call(s32[1,256]{1,0:T(1,128)S(1)} %bitcast.8, f32[5,2,32,256]{3,2,1,0:T(8,128)S(1)} %shard_map.60.refs_1_, f32[5,2,16,256]{3,2,1,0:T(8,128)S(1)} %get-tuple-element.17.refs_2_, f32[5,8,256]{2,1,0:T(8,128)S(1)} %collective-permute-done.refs_2_.refs_3_, ...), custom_call_target="tpu_custom_call" | custom-call | tf_op jit(solution)/shard_map/pallas_call | solution.py:521
  21.8 0.0 copy-start
  21.8 24.1 %all_to_all.5 = f32[64,8,128]{2,1,0:T(8,128)S(1)} all-to-all(f32[64,8,128]{2,1,0:T(8,128)S(1)} %bitcast.4), channel_id=1, replica_groups={{0,4,8,12,16,20,24,28,32,36,40,44,48,52,56,60,64,68,72,76,80,84,88,92,9..., dimensions={0} | all-to-all | bytes 524288 | tf_op jit(solution)/shard_map/all_to_all | solution.py:535
  45.9 0.0 copy-done
  45.9 0.6 %shard_map.66 = (f32[64,128]{1,0:T(8,128)S(1)}, f32[64,128]{1,0:T(8,128)S(1)}) custom-call(f32[512,128]{1,0:T(8,128)S(1)} %bitcast.3, f32[2,512,128]{2,1,0:T(8,128)S(1)} %copy-done), custom_call_target="tpu_custom_call" | custom-call | tf_op jit(solution)/shard_map/pallas_call | solution.py:543
  46.5 0.1 collective-permute-start.4
  46.6 0.8 %shard_map.65 = f32[5,16,8,256]{3,2,1,0:T(8,128)} custom-call(f32[5,16,8,256]{3,2,1,0:T(8,128)S(1)} %get-tuple-element.22.flow_ref), custom_call_target="tpu_custom_call" | custom-call | bytes 1400000 | tf_op jit(solution)/shard_map/pallas_call | solution.py:552
  47.4 0.3 collective-permute-done.4.got_ref
  47.8 0.6 %shard_map.67 = f32[2,16,256]{2,1,0:T(8,128)} custom-call(f32[64,128]{1,0:T(8,128)S(1)} %get-tuple-element.24.keep_ref, f32[64,128]{1,0:T(8,128)S(1)} %collective-permute-done.4.got_ref), custom_call_target="tpu_custom_call" | custom-call | tf_op jit(solution)/shard_map/pallas_call | solution.py:561
Async XLA Ops:
  2.0 3.6 %collective-permute-start = (f32[5,8,256]{2,1,0:T(8,128)S(1)}, f32[5,8,256]{2,1,0:T(8,128)S(1)}, u32[]{:S(2)}, u32[]{:S(2)}) collective-permute-start(f32[5,8,256]{2,1,0:T(8,128)S(1)} %get-tuple-element.16), channel_id=1, source_target_pairs={{0,1},{1,0},{2,3},{3,2},{4,5},{5,4},{6,7},{7,6},{8,9},{9,8},{10,11... | collective-permute-start | bytes 122888 | tf_op jit(solution)/shard_map/ppermute | solution.py:486
  4.2 0.7 %copy-start.1 = (s32[256]{0:T(256)S(1)}, s32[256]{0:T(256)}, u32[]{:S(2)}) copy-start(s32[256]{0:T(256)} %param.6) | copy-start | bytes 3076
  5.7 14.2 %collective-permute-start.2 = (f32[168,256]{1,0:T(8,128)S(1)}, f32[168,256]{1,0:T(8,128)S(1)}, u32[]{:S(2)}, u32[]{:S(2)}) collective-permute-start(f32[168,256]{1,0:T(8,128)S(1)} %get-tuple-element.20), channel_id=1, source_target_pairs={{0,254},{2,4},{4,2},{6,8},{8,6},{10,12},{12,10},{14,16},{16,14},{1... | collective-permute-start | bytes 516104 | tf_op jit(solution)/shard_map/ppermute | solution.py:504
  9.3 10.6 %collective-permute-start.3 = (f32[168,256]{1,0:T(8,128)S(1)}, f32[168,256]{1,0:T(8,128)S(1)}, u32[]{:S(2)}, u32[]{:S(2)}) collective-permute-start(f32[168,256]{1,0:T(8,128)S(1)} %get-tuple-element.21), channel_id=1, source_target_pairs={{0,2},{2,0},{4,6},{6,4},{8,10},{10,8},{12,14},{14,12},{16,18},{18,... | collective-permute-start | bytes 516104 | tf_op jit(solution)/shard_map/ppermute | solution.py:503
  16.9 2.9 %collective-permute-start.1 = (f32[5,8,256]{2,1,0:T(8,128)S(1)}, f32[5,8,256]{2,1,0:T(8,128)S(1)}, u32[]{:S(2)}, u32[]{:S(2)}) collective-permute-start(f32[5,8,256]{2,1,0:T(8,128)S(1)} %shard_map.63), channel_id=1, source_target_pairs={{0,1},{1,0},{2,3},{3,2},{4,5},{5,4},{6,7},{7,6},{8,9},{9,8},{10,11... | collective-permute-start | bytes 122888 | tf_op jit(solution)/shard_map/ppermute | solution.py:512
  21.8 24.1 %copy-start = (f32[2,512,128]{2,1,0:T(8,128)S(1)}, f32[2,512,128]{2,1,0:T(8,128)}, u32[]{:S(2)}) copy-start(f32[2,512,128]{2,1,0:T(8,128)} %constant.2.clone.basis_ref) | copy-start | bytes 1572868
  46.5 1.3 %collective-permute-start.4 = (f32[64,128]{1,0:T(8,128)S(1)}, f32[64,128]{1,0:T(8,128)S(1)}, u32[]{:S(2)}, u32[]{:S(2)}) collective-permute-start(f32[64,128]{1,0:T(8,128)S(1)} %get-tuple-element.25), channel_id=1, source_target_pairs={{0,2},{2,0},{4,6},{6,4},{8,10},{10,8},{12,14},{14,12},{16,18},{18,... | collective-permute-start | bytes 98312 | tf_op jit(solution)/shard_map/ppermute | solution.py:551

commit v10 on v9

--- a/solution.py
+++ b/solution.py
@@ -15,6 +15,7 @@
 BAND = 16
 SECTOR = 8
 AXIAL = 256
+RAD_VMEM = 56_200_000
 LOAD_VMEM = 55_000_000
 F32 = jnp.float32
 ALL = range(5)
@@ -74,13 +75,20 @@
     return rate, 1.0 / (rate + 30.0)
 
 
+def blade_force(q, spin_r, blade):
+    bladed, rotor = blade
+    return bladed * (q[3] - (rotor * spin_r) * q[0])
+
+
 def advance(q, prim, source, axial, radial, swirl, inv_r, inv_h, spin_r, blade):
     ux, ur, ut, pressure, sound = prim
     twice_r = 2.0 * inv_r
     rate, weight = step_weight(prim, inv_h)
-    bladed, rotor = blade
-    force = bladed * (q[3] - (rotor * spin_r) * q[0])
-    gains = [None, None, twice_r * (q[3] * ut + pressure), -twice_r * (q[2] * ut) - force, -ut * force]
+    gains = [None, None, twice_r * (q[3] * ut + pressure), -twice_r * (q[2] * ut), None]
+    if blade is not None:
+        force = blade_force(q, spin_r, blade)
+        gains[3] = gains[3] - force
+        gains[4] = -ut * force
     out = []
     for v in ALL:
         total = source[v] - axial[v] - radial[v] - swirl[v]
@@ -120,11 +128,16 @@
     return bladed, rotor
 
 
-def load_kernel(q_ref, qp_ref, near_ref, q_out_ref, qp_out_ref, sems):
+def rad_kernel(q_ref, near_ref, sem):
+    copy = pltpu.make_async_copy(q_ref.at[:, edge_row(lax.axis_index("rad"), BAND - 1, 0)], near_ref, sem)
+    copy.start()
+    copy.wait()
+
+
+def load_kernel(q_ref, qp_ref, q_out_ref, qp_out_ref, sems):
     copies = [
-        pltpu.make_async_copy(q_ref.at[:, edge_row(lax.axis_index("rad"), BAND - 1, 0)], near_ref, sems.at[0]),
-        pltpu.make_async_copy(q_ref, q_out_ref, sems.at[1]),
-        pltpu.make_async_copy(qp_ref, qp_out_ref, sems.at[2]),
+        pltpu.make_async_copy(q_ref, q_out_ref, sems.at[0]),
+        pltpu.make_async_copy(qp_ref, qp_out_ref, sems.at[1]),
     ]
     for copy in copies:
         copy.start()
@@ -145,11 +158,10 @@
         self.a_h = 0.25 * self.inv_h
 
 
-def edge_kernel(total_rows, circle, blade_ref, q_ref, qp_ref, edges_ref, ce, taken):
+def edge_kernel(total_rows, circle, q_ref, qp_ref, edges_ref, ce, taken):
     band = lax.axis_index("rad")
     low = band == 0
     geo = Columns(band * BAND, total_rows, circle)
-    blade = blades(blade_ref, BAND)
     lane = lax.broadcasted_iota(jnp.int32, (BAND, HALF), 1)
     row = lax.broadcasted_iota(jnp.int32, (BAND, AXIAL), 0)
     below_scale = jnp.where((row == 0) & jnp.logical_not(low), 0.0, geo.inv_r * geo.inner)
@@ -189,7 +201,7 @@
             geo.inv_r,
             geo.inv_h,
             geo.spin_r,
-            blade,
+            None,
         )
         for v in ALL:
             edges_ref[v, side, 0:16] = edge[v]
@@ -334,6 +346,7 @@
         nearby[v] = next_ref[v]
 
     geo = Columns(band * BAND, total_rows, circle)
+    column_blade = blades(blade_ref, BAND)
     near_inv_h = jnp.where(low, coefficients(low, table, BAND)[2], coefficients(low, table, -1)[2])
 
     for side in (0, 1):
@@ -353,10 +366,18 @@
         own = [edges_ref[v, side, 0:16] for v in ALL]
         own_prim, near_prim = primitives(own), primitives(near)
         shared = ordered(near, near_prim, own, own_prim)
-        own_scale = (sign * geo.inv_h) * step_weight(own_prim, geo.inv_h)[1]
-        near_scale = (-sign * geo.inv_h) * step_weight(near_prim, geo.inv_h)[1]
-        own_next = [own_ref[v, side] + own_scale * shared[v] for v in ALL]
-        near_next = [near_part[v] + near_scale * shared[v] for v in ALL]
+        own_part = [own_ref[v, side] for v in ALL]
+        own_next, near_next = [], []
+        for q, prim, part, scale, out in (
+            (own, own_prim, own_part, sign * geo.inv_h, own_next),
+            (near, near_prim, near_part, -sign * geo.inv_h, near_next),
+        ):
+            force = blade_force(q, geo.spin_r, column_blade)
+            change = [scale * x for x in shared]
+            change[3] = change[3] - force
+            change[4] = change[4] - prim[2] * force
+            weight = step_weight(prim, geo.inv_h)[1]
+            out.extend(part[v] + weight * change[v] for v in ALL)
 
         edge = [rad_ref[v, at : at + 1, :] for v in ALL]
         edge_prim = primitives(edge)
@@ -474,25 +495,33 @@
     def final(*refs):
         final_kernel(bands * BAND, circle, table, *refs)
 
-    near, q_level, q_prev = pl.pallas_call(
+    near = pl.pallas_call(
+        rad_kernel,
+        out_shape=shaped(5, SECTOR, AXIAL),
+        in_specs=[hbm],
+        out_specs=vmem(),
+        scratch_shapes=[pltpu.SemaphoreType.DMA],
+        compiler_params=pltpu.CompilerParams(vmem_limit_bytes=RAD_VMEM),
+    )(q_level)
+    rad_in = lax.ppermute(near, "rad", swap)
+    q_level, q_prev = pl.pallas_call(
         load_kernel,
-        out_shape=[shaped(5, SECTOR, AXIAL)] + [shaped(5, BAND, SECTOR, AXIAL)] * 2,
+        out_shape=[shaped(5, BAND, SECTOR, AXIAL)] * 2,
         in_specs=[hbm] * 2,
-        out_specs=[vmem()] * 3,
-        scratch_shapes=[pltpu.SemaphoreType.DMA((3,))],
+        out_specs=[vmem()] * 2,
+        scratch_shapes=[pltpu.SemaphoreType.DMA((2,))],
         compiler_params=pltpu.CompilerParams(vmem_limit_bytes=LOAD_VMEM),
         cost_estimate=pl.CostEstimate(flops=0, bytes_accessed=3_000_000, transcendentals=0),
     )(q_level, q_prev)
-    rad_in = lax.ppermute(near, "rad", swap)
     edge_columns = pl.pallas_call(
         edges,
         out_shape=shaped(5, 2, 32, AXIAL),
-        in_specs=[vmem()] * 3,
+        in_specs=[vmem()] * 2,
         out_specs=vmem(),
         scratch_shapes=[pltpu.VMEM((5, 2, 32, AXIAL), F32), pltpu.VMEM((5, 2, 2, BAND, AXIAL), F32)],
         compiler_params=limit(4),
         cost_estimate=pl.CostEstimate(flops=5_000_000, bytes_accessed=2_000_000, transcendentals=50_000),
-    )(blade, q_level, q_prev)
+    )(q_level, q_prev)
     own_columns, core_out, other_out = pl.pallas_call(
         pack,
         out_shape=[shaped(5, 2, BAND, AXIAL)] + [shaped(168, AXIAL)] * 2,

time: 48.5 us -> 48.1 us (level)
  local copies, waits for them, and re-layouts: 0.69 us -> 0.01 us
  Pallas kernels: 7.77 us -> 8.45 us
  starting transfers between devices: 13.8 us -> 13.2 us
    pallas_call x1 -> x2, Pallas kernels: 1.35 us -> 2.1 us  [the longest x1 1.3 us: per_device(): pl.pallas_call(load_kernel, out_shape=[shaped(5, BAND, SECTOR, AXIAL)] *...]
    unnamed x4, local copies, waits for them, and re-layouts: 0.69 us -> 0.01 us
    ppermute x1, starting transfers between devices: 3.57 us -> 3 us  [per_device(): other_in = lax.ppermute(other_out, 'theta', other)]
  transfers between devices with their start and end apart: 5 -> 5, of which waited for: 2 -> 2; matrix products, arithmetic and copies ran while one was open for 0% -> 0% of each run, Pallas kernels for 7% -> 9%
where the time goes in v10:
time: 48.1 us; the launch traced here: 47.9 us
  blocking collectives  24 us (50%)
  starting transfers between devices  13.2 us (27%)
  Pallas kernels  8.45 us (18%)
  waiting for transfers between devices  1.49 us (3%)
  between operations  0.72 us (1%)
    all_to_all x1, blocking collectives, per_device(): lax.all_to_all(send.reshape(chips, 8, 128), 'theta', split_axis=0, concat...  24 us
    ppermute x1, starting transfers between devices, per_device(): core_in = lax.ppermute(core_out, 'theta', core)  7.59 us
    ppermute x1, starting transfers between devices, per_device(): other_in = lax.ppermute(other_out, 'theta', other)  3 us
    ppermute x1, starting transfers between devices, per_device(): rad_in = lax.ppermute(near, 'rad', swap)  2.21 us
    pallas_call x1, Pallas kernels, per_device(): pl.pallas_call(final, out_shape=[shaped(5, BAND, SECTOR, AXIAL), shaped(2...  1.94 us
    pallas_call x1, Pallas kernels, per_device(): pl.pallas_call(early, out_shape=[shaped(5, BAND, SECTOR, AXIAL)] * 2, in_...  1.45 us
    pallas_call x1, Pallas kernels, per_device(): pl.pallas_call(load_kernel, out_shape=[shaped(5, BAND, SECTOR, AXIAL)] *...  1.3 us
    ppermute x1, waiting for transfers between devices, per_device(): next_in = lax.ppermute(next_out, 'rad', swap)  1.14 us
  transfers between devices with their start and end apart: 5, of which 2 were waited for; matrix products, arithmetic and copies ran while one was open for 0% of the time, Pallas kernels for 9%

profile of v10, /device:TPU:1, one launch (start us, length us, event | category | flops | bytes accessed | tf_op | source)
XLA Modules:
  0.0 47.9 jit_solution(2023281538256818095)
XLA Ops:
  0.6 0.8 %shard_map.61 = f32[5,8,256]{2,1,0:T(8,128)S(1)} custom-call(f32[5,16,8,256]{3,2,1,0:T(8,128)} %q_ref.3), custom_call_target="tpu_custom_call" | custom-call | tf_op jit(solution)/shard_map/pallas_call | solution.py:498
  1.4 2.2 %collective-permute-start = (f32[5,8,256]{2,1,0:T(8,128)S(1)}, f32[5,8,256]{2,1,0:T(8,128)S(1)}, u32[]{:S(2)}, u32[]{:S(2)}) collective-permute-start(f32[5,8,256]{2,1,0:T(8,128)S(1)} %shard_map.61), channel_id=1, source_target_pairs={{0,1},{1,0},{2,3},{3,2},{4,5},{5,4},{6,7},{7,6},{8,9},{9,8},{10,11... | collective-permute-start | bytes 122888 | tf_op jit(solution)/shard_map/ppermute | solution.py:506
  3.6 1.3 %shard_map.59 = (f32[5,16,8,256]{3,2,1,0:T(8,128)S(1)}, f32[5,16,8,256]{3,2,1,0:T(8,128)S(1)}) custom-call(f32[5,16,8,256]{3,2,1,0:T(8,128)} %q_ref.3, f32[5,16,8,256]{3,2,1,0:T(8,128)} %qp_ref.1), custom_call_target="tpu_custom_call" | custom-call | bytes 3000000 | tf_op jit(solution)/shard_map/pallas_call | solution.py:507
  5.0 0.7 %shard_map.60.refs_1_ = f32[5,2,32,256]{3,2,1,0:T(8,128)S(1)} custom-call(f32[5,16,8,256]{3,2,1,0:T(8,128)S(1)} %get-tuple-element.13.refs_0_.refs_1_, f32[5,16,8,256]{3,2,1,0:T(8,128)S(1)} %get-tuple-element.14.refs_1_.refs_2_), custom_call_target="tpu_custom_call" | custom-call | flops 5000000 | bytes 2000000 | tf_op jit(solution)/shard_map/pallas_call | solution.py:516
  5.6 0.0 collective-permute-done.refs_2_.refs_3_
  5.6 0.1 shard_map.62
  5.7 3.0 %collective-permute-start.2 = (f32[168,256]{1,0:T(8,128)S(1)}, f32[168,256]{1,0:T(8,128)S(1)}, u32[]{:S(2)}, u32[]{:S(2)}) collective-permute-start(f32[168,256]{1,0:T(8,128)S(1)} %get-tuple-element.18), channel_id=1, source_target_pairs={{0,254},{2,4},{4,2},{6,8},{8,6},{10,12},{12,10},{14,16},{16,14},{1... | collective-permute-start | bytes 516104 | tf_op jit(solution)/shard_map/ppermute | solution.py:533
  8.7 0.0 copy-start.1
  8.7 7.6 %collective-permute-start.3 = (f32[168,256]{1,0:T(8,128)S(1)}, f32[168,256]{1,0:T(8,128)S(1)}, u32[]{:S(2)}, u32[]{:S(2)}) collective-permute-start(f32[168,256]{1,0:T(8,128)S(1)} %get-tuple-element.19), channel_id=1, source_target_pairs={{0,2},{2,0},{4,6},{6,4},{8,10},{10,8},{12,14},{14,12},{16,18},{18,... | collective-permute-start | bytes 516104 | tf_op jit(solution)/shard_map/ppermute | solution.py:532
  16.3 0.0 copy-done.1
  16.3 0.2 shard_map.64
  16.5 0.3 collective-permute-start.1
  16.8 1.4 %shard_map.63 = (f32[5,16,8,256]{3,2,1,0:T(8,128)S(1)}, f32[5,16,8,256]{3,2,1,0:T(8,128)S(1)}) custom-call(s32[1,256]{1,0:T(1,128)S(1)} %bitcast.6, f32[5,16,8,256]{3,2,1,0:T(8,128)S(1)} %get-tuple-element.13.refs_0_.refs_1_, f32[5,16,8,256]{3,2,1,0:T(8,128)S(1)} %get-tuple-element.14.refs_1_.refs_2_, f32[5,8,256]{2,1,0:T(8,128)S(1)} %collective-permute-done.refs_2_.refs_3_), custom_call_target="tpu_custom_call" | custom-call | flops 10000000 | bytes 3500000 | tf_op jit(solution)/shard_map/pallas_call | solution.py:542
  18.3 1.1 %collective-permute-done.1.refs_6_ = f32[5,8,256]{2,1,0:T(8,128)S(1)} collective-permute-done((f32[5,8,256]{2,1,0:T(8,128)S(1)}, f32[5,8,256]{2,1,0:T(8,128)S(1)}, u32[]{:S(2)}, u32[]{:S(2)}) %collective-permute-start.1) | collective-permute-done | bytes 40992 | tf_op jit(solution)/shard_map/ppermute | solution.py:541
  19.4 0.0 collective-permute-done.2.refs_7_
  19.5 0.0 collective-permute-done.3.refs_8_
  19.5 1.9 %shard_map.65 = (f32[5,16,8,256]{3,2,1,0:T(8,128)S(1)}, f32[512,128]{1,0:T(8,128)S(1)}) custom-call(s32[1,256]{1,0:T(1,128)S(1)} %bitcast.7, f32[5,2,32,256]{3,2,1,0:T(8,128)S(1)} %shard_map.60.refs_1_, f32[5,2,16,256]{3,2,1,0:T(8,128)S(1)} %get-tuple-element.15.refs_2_, f32[5,8,256]{2,1,0:T(8,128)S(1)} %collective-permute-done.refs_2_.refs_3_, ...), custom_call_target="tpu_custom_call" | custom-call | tf_op jit(solution)/shard_map/pallas_call | solution.py:550
  21.4 0.0 copy-start
  21.4 24.0 %all_to_all.5 = f32[64,8,128]{2,1,0:T(8,128)S(1)} all-to-all(f32[64,8,128]{2,1,0:T(8,128)S(1)} %bitcast.4), channel_id=1, replica_groups={{0,4,8,12,16,20,24,28,32,36,40,44,48,52,56,60,64,68,72,76,80,84,88,92,9..., dimensions={0} | all-to-all | bytes 524288 | tf_op jit(solution)/shard_map/all_to_all | solution.py:564
  45.4 0.0 copy-done
  45.4 0.6 %shard_map.67 = (f32[64,128]{1,0:T(8,128)S(1)}, f32[64,128]{1,0:T(8,128)S(1)}) custom-call(f32[512,128]{1,0:T(8,128)S(1)} %bitcast.3, f32[2,512,128]{2,1,0:T(8,128)S(1)} %copy-done), custom_call_target="tpu_custom_call" | custom-call | tf_op jit(solution)/shard_map/pallas_call | solution.py:572
  46.0 0.1 collective-permute-start.4
  46.1 0.8 %shard_map.66 = f32[5,16,8,256]{3,2,1,0:T(8,128)} custom-call(f32[5,16,8,256]{3,2,1,0:T(8,128)S(1)} %get-tuple-element.20.flow_ref), custom_call_target="tpu_custom_call" | custom-call | bytes 1400000 | tf_op jit(solution)/shard_map/pallas_call | solution.py:581
  47.0 0.3 collective-permute-done.4.got_ref
  47.3 0.6 %shard_map.68 = f32[2,16,256]{2,1,0:T(8,128)} custom-call(f32[64,128]{1,0:T(8,128)S(1)} %get-tuple-element.22.keep_ref, f32[64,128]{1,0:T(8,128)S(1)} %collective-permute-done.4.got_ref), custom_call_target="tpu_custom_call" | custom-call | tf_op jit(solution)/shard_map/pallas_call | solution.py:590
Async XLA Ops:
  1.4 4.2 %collective-permute-start = (f32[5,8,256]{2,1,0:T(8,128)S(1)}, f32[5,8,256]{2,1,0:T(8,128)S(1)}, u32[]{:S(2)}, u32[]{:S(2)}) collective-permute-start(f32[5,8,256]{2,1,0:T(8,128)S(1)} %shard_map.61), channel_id=1, source_target_pairs={{0,1},{1,0},{2,3},{3,2},{4,5},{5,4},{6,7},{7,6},{8,9},{9,8},{10,11... | collective-permute-start | bytes 122888 | tf_op jit(solution)/shard_map/ppermute | solution.py:506
  5.7 13.7 %collective-permute-start.2 = (f32[168,256]{1,0:T(8,128)S(1)}, f32[168,256]{1,0:T(8,128)S(1)}, u32[]{:S(2)}, u32[]{:S(2)}) collective-permute-start(f32[168,256]{1,0:T(8,128)S(1)} %get-tuple-element.18), channel_id=1, source_target_pairs={{0,254},{2,4},{4,2},{6,8},{8,6},{10,12},{12,10},{14,16},{16,14},{1... | collective-permute-start | bytes 516104 | tf_op jit(solution)/shard_map/ppermute | solution.py:533
  8.7 7.6 %copy-start.1 = (s32[256]{0:T(256)S(1)}, s32[256]{0:T(256)}, u32[]{:S(2)}) copy-start(s32[256]{0:T(256)} %param.6) | copy-start | bytes 3076
  8.7 10.7 %collective-permute-start.3 = (f32[168,256]{1,0:T(8,128)S(1)}, f32[168,256]{1,0:T(8,128)S(1)}, u32[]{:S(2)}, u32[]{:S(2)}) collective-permute-start(f32[168,256]{1,0:T(8,128)S(1)} %get-tuple-element.19), channel_id=1, source_target_pairs={{0,2},{2,0},{4,6},{6,4},{8,10},{10,8},{12,14},{14,12},{16,18},{18,... | collective-permute-start | bytes 516104 | tf_op jit(solution)/shard_map/ppermute | solution.py:532
  16.5 2.9 %collective-permute-start.1 = (f32[5,8,256]{2,1,0:T(8,128)S(1)}, f32[5,8,256]{2,1,0:T(8,128)S(1)}, u32[]{:S(2)}, u32[]{:S(2)}) collective-permute-start(f32[5,8,256]{2,1,0:T(8,128)S(1)} %shard_map.64), channel_id=1, source_target_pairs={{0,1},{1,0},{2,3},{3,2},{4,5},{5,4},{6,7},{7,6},{8,9},{9,8},{10,11... | collective-permute-start | bytes 122888 | tf_op jit(solution)/shard_map/ppermute | solution.py:541
  21.4 24.0 %copy-start = (f32[2,512,128]{2,1,0:T(8,128)S(1)}, f32[2,512,128]{2,1,0:T(8,128)}, u32[]{:S(2)}) copy-start(f32[2,512,128]{2,1,0:T(8,128)} %constant.2.clone.basis_ref) | copy-start | bytes 1572868
  46.0 1.3 %collective-permute-start.4 = (f32[64,128]{1,0:T(8,128)S(1)}, f32[64,128]{1,0:T(8,128)S(1)}, u32[]{:S(2)}, u32[]{:S(2)}) collective-permute-start(f32[64,128]{1,0:T(8,128)S(1)} %get-tuple-element.23), channel_id=1, source_target_pairs={{0,2},{2,0},{4,6},{6,4},{8,10},{10,8},{12,14},{14,12},{16,18},{18,... | collective-permute-start | bytes 98312 | tf_op jit(solution)/shard_map/ppermute | solution.py:580

commit v11 on v10

--- a/solution.py
+++ b/solution.py
@@ -15,7 +15,7 @@
 BAND = 16
 SECTOR = 8
 AXIAL = 256
-RAD_VMEM = 56_200_000
+RING = 16
 LOAD_VMEM = 55_000_000
 F32 = jnp.float32
 ALL = range(5)
@@ -128,21 +128,20 @@
     return bladed, rotor
 
 
-def rad_kernel(q_ref, near_ref, sem):
-    copy = pltpu.make_async_copy(q_ref.at[:, edge_row(lax.axis_index("rad"), BAND - 1, 0)], near_ref, sem)
-    copy.start()
-    copy.wait()
-
-
-def load_kernel(q_ref, qp_ref, q_out_ref, qp_out_ref, sems):
+def load_kernel(q_ref, qp_ref, near_ref, q_out_ref, qp_out_ref, sems):
     copies = [
-        pltpu.make_async_copy(q_ref, q_out_ref, sems.at[0]),
-        pltpu.make_async_copy(qp_ref, qp_out_ref, sems.at[1]),
+        pltpu.make_async_copy(q_ref.at[:, edge_row(lax.axis_index("rad"), BAND - 1, 0)], near_ref, sems.at[0]),
+        pltpu.make_async_copy(q_ref, q_out_ref, sems.at[1]),
+        pltpu.make_async_copy(qp_ref, qp_out_ref, sems.at[2]),
     ]
     for copy in copies:
         copy.start()
     for copy in copies:
         copy.wait()
+
+
+def is_late():
+    return lax.axis_index("theta") % RING == RING - 1
 
 
 class Columns:
@@ -208,30 +207,64 @@
             edges_ref[v, side, 16:32] = part[v]
 
 
-def pack_kernel(table, q_ref, edges_ref, rad_ref, own_ref, core_ref, other_ref):
-    odd = lax.axis_index("theta") % 2 == 1
-    band = lax.axis_index("rad")
-    low = band == 0
-    edge_at = edge_row(band, BAND - 1, 0)
-    below_coefs, above_coefs = coefficients(low, table, 0), coefficients(low, table, BAND - 1)
-    edge = [q_ref[v, edge_at] for v in ALL]
-    near = [rad_ref[v] for v in ALL]
+def closing(table, low, edge, near):
+    coefs = [coefficients(low, table, j) for j in (0, BAND - 1)]
     edge_prim, near_prim = primitives(edge), primitives(near)
     (fe, se), (fn, sn) = flux(edge, edge_prim, 2), flux(near, near_prim, 2)
     fastest = jnp.where(low, np.float32(1.0), np.float32(-1.0)) * jnp.maximum(se, sn)
-    _, weight = step_weight(edge_prim, jnp.where(low, above_coefs[2], below_coefs[2]))
-    scale = jnp.where(low, -above_coefs[0], below_coefs[1]) * weight
-    change = [scale * ((fe[v] + fn[v]) - fastest * (near[v] - edge[v])) for v in ALL]
+    _, weight = step_weight(edge_prim, jnp.where(low, coefs[1][2], coefs[0][2]))
+    scale = jnp.where(low, -coefs[1][0], coefs[0][1]) * weight
+    return [scale * ((fe[v] + fn[v]) - fastest * (near[v] - edge[v])) for v in ALL]
+
+
+def closed_columns(table, q_ref, edges_ref, near, skip):
+    band = lax.axis_index("rad")
+    edge_at = edge_row(band, BAND - 1, 0)
+    change = closing(table, band == 0, [q_ref[v, edge_at] for v in ALL], near)
     here = lax.broadcasted_iota(jnp.int32, (BAND, AXIAL), 0) == edge_at
+    if skip is not None:
+        here = here & jnp.logical_not(skip)
+    return [
+        [
+            edges_ref[v, side, 16:32] + jnp.where(here, jnp.broadcast_to(change[v][at : at + 1], (BAND, AXIAL)), 0.0)
+            for v in ALL
+        ]
+        for side, at in ((0, 0), (1, SECTOR - 1))
+    ]
+
+
+def put_message(ref, flip, edges_ref, closed, near):
     for v in ALL:
+        at = 32 * v
+        ref[at : at + 16] = jnp.where(flip, edges_ref[v, 1, 0:16], edges_ref[v, 0, 0:16])
+        ref[at + 16 : at + 32] = jnp.where(flip, closed[1][v], closed[0][v])
+        ref[160 + v : 161 + v] = jnp.where(flip, near[v][SECTOR - 1 : SECTOR], near[v][0:1])
+
+
+def other_kernel(table, q_ref, edges_ref, rad_ref, other_ref):
+    odd = lax.axis_index("theta") % 2 == 1
+    near = [rad_ref[v] for v in ALL]
+    closed = closed_columns(table, q_ref, edges_ref, near, is_late())
+    put_message(other_ref, odd, edges_ref, closed, near)
+
+
+def core_kernel(table, q_ref, edges_ref, first_ref, second_ref, own_ref, core_ref, rad_ref):
+    odd = lax.axis_index("theta") % 2 == 1
+    near = [jnp.where(is_late(), second_ref[v], first_ref[v]) for v in ALL]
+    closed = closed_columns(table, q_ref, edges_ref, near, None)
+    put_message(core_ref, jnp.logical_not(odd), edges_ref, closed, near)
+    for v in ALL:
+        rad_ref[v] = near[v]
         for side in (0, 1):
-            at = 0 if side == 0 else SECTOR - 1
-            own_ref[v, side] = edges_ref[v, side, 16:32] + jnp.where(here, change[v][at : at + 1], 0.0)
-        for ref, flip in ((core_ref, jnp.logical_not(odd)), (other_ref, odd)):
-            at = 32 * v
-            ref[at : at + 16] = jnp.where(flip, edges_ref[v, 1, 0:16], edges_ref[v, 0, 0:16])
-            ref[at + 16 : at + 32] = jnp.where(flip, own_ref[v, 1], own_ref[v, 0])
-            ref[160 + v : 161 + v] = jnp.where(flip, near[v][SECTOR - 1 : SECTOR], near[v][0:1])
+            own_ref[v, side] = closed[side][v]
+
+
+def corner_kernel(other_ref, part_ref, corner_ref):
+    del part_ref
+    edge_at = edge_row(lax.axis_index("rad"), BAND - 1, 0)
+    corner_ref[...] = jnp.zeros((8, AXIAL), F32)
+    for v in ALL:
+        corner_ref[v : v + 1] = other_ref[pl.ds(32 * v + edge_at, 1), :]
 
 
 def masks():
@@ -251,12 +284,16 @@
     between = face(q, (f, speed), qn, (fn, ahead(speed)))
     swirl = []
     for v in ALL:
-        end = 0.0 if ends is None else ends[v]
-        right = jnp.where(sub == SECTOR - 1, end, between[v])
-        left = jnp.where(sub == 0, end, pltpu.roll(between[v], 1, 0))
+        first, last = (0.0, 0.0) if ends is None else ends[v]
+        right = jnp.where(sub == SECTOR - 1, last, between[v])
+        left = jnp.where(sub == 0, first, pltpu.roll(between[v], 1, 0))
         swirl.append(inv_h * (right - left))
     radial = [a_out * g_out[v] - a_in * g_in[v] for v in ALL]
     return advance(q, prim, source, axial_difference(q, prim, lane), radial, swirl, inv_r, inv_h, spin_r, blade)
+
+
+def column_rows(ref, v, j):
+    return [ref[v, 2 * side + j // SECTOR, j % SECTOR : j % SECTOR + 1, :] for side in (0, 1)]
 
 
 def sweep(load, step, store):
@@ -329,9 +366,10 @@
     next_ref,
     other_ref,
     core_ref,
+    corner_ref,
     flow_ref,
     send_ref,
-    p1,
+    own_rows,
     nearby,
     ends,
     fields,
@@ -342,7 +380,6 @@
     mask = masks()
     blade = blades(blade_ref, SECTOR)
     for v in ALL:
-        p1[v] = p1_ref[v]
         nearby[v] = next_ref[v]
 
     geo = Columns(band * BAND, total_rows, circle)
@@ -363,6 +400,16 @@
             return face(halo, a, own, b) if side == 0 else face(own, b, halo, a)
 
         near, near_part, corner = pick(0, 32, 16), pick(16, 32, 16), pick(160, 1, 1)
+        if side == 0:
+            first = lax.axis_index("theta") % RING == 0
+            corner = [jnp.where(first, corner_ref[v : v + 1], corner[v]) for v in ALL]
+            edge_at = edge_row(band, BAND - 1, 0)
+            cell = [jnp.where(low, near[v][BAND - 1 : BAND], near[v][0:1]) for v in ALL]
+            change = closing(table, low, cell, corner)
+            here = (lax.broadcasted_iota(jnp.int32, (BAND, AXIAL), 0) == edge_at) & first
+            near_part = [
+                near_part[v] + jnp.where(here, jnp.broadcast_to(change[v], (BAND, AXIAL)), 0.0) for v in ALL
+            ]
         own = [edges_ref[v, side, 0:16] for v in ALL]
         own_prim, near_prim = primitives(own), primitives(near)
         shared = ordered(near, near_prim, own, own_prim)
@@ -386,19 +433,25 @@
 
         faces = ordered(near_next, primitives(near_next), own_next, primitives(own_next))
         for v in ALL:
-            p1[v, :, at, :] = own_next[v]
+            own_rows[v, 2 * side : 2 * side + 2] = own_next[v].reshape(2, SECTOR, AXIAL)
             nearby[v, at : at + 1, :] = next_ref[v, at : at + 1, :] + corner_scale * corner_face[v]
-            ends[v, :, at, :] = faces[v]
+            ends[v, 2 * side : 2 * side + 2] = faces[v].reshape(2, SECTOR, AXIAL)
+
+    sub = mask[1]
+
+    def row(v, j):
+        first, last = column_rows(own_rows, v, j)
+        return jnp.where(sub == 0, first, jnp.where(sub == SECTOR - 1, last, p1_ref[v, j]))
 
     def load(j):
         if j < 0:
-            return [jnp.where(low, MIRROR[v] * p1[v, 0], nearby[v]) for v in ALL]
+            return [jnp.where(low, MIRROR[v] * row(v, 0), nearby[v]) for v in ALL]
         if j == BAND:
-            return [jnp.where(low, nearby[v], MIRROR[v] * p1[v, BAND - 1]) for v in ALL]
-        return [p1[v, j] for v in ALL]
+            return [jnp.where(low, nearby[v], MIRROR[v] * row(v, BAND - 1)) for v in ALL]
+        return [row(v, j) for v in ALL]
 
     def step(j, q, prim, g_in, g_out):
-        source, end = [source_ref[v, j] for v in ALL], [ends[v, j] for v in ALL]
+        source, end = [source_ref[v, j] for v in ALL], [column_rows(ends, v, j) for v in ALL]
         return row_step(coefficients(low, table, j), q, prim, source, g_in, g_out, end, mask, blade)
 
     def store(j, q):
@@ -483,8 +536,11 @@
     def edges(*refs):
         edge_kernel(bands * BAND, circle, *refs)
 
-    def pack(*refs):
-        pack_kernel(table, *refs)
+    def for_other(*refs):
+        other_kernel(table, *refs)
+
+    def for_core(*refs):
+        core_kernel(table, *refs)
 
     def neighbour(*refs):
         next_kernel(table, *refs)
@@ -495,24 +551,21 @@
     def final(*refs):
         final_kernel(bands * BAND, circle, table, *refs)
 
-    near = pl.pallas_call(
-        rad_kernel,
-        out_shape=shaped(5, SECTOR, AXIAL),
-        in_specs=[hbm],
-        out_specs=vmem(),
-        scratch_shapes=[pltpu.SemaphoreType.DMA],
-        compiler_params=pltpu.CompilerParams(vmem_limit_bytes=RAD_VMEM),
-    )(q_level)
-    rad_in = lax.ppermute(near, "rad", swap)
-    q_level, q_prev = pl.pallas_call(
+    def rad_swap(x, chosen):
+        pairs = [(bands * t + b, bands * t + 1 - b) for t in range(sectors) if chosen(t % RING) for b in range(bands)]
+        return lax.ppermute(x, ("theta", "rad"), pairs)
+
+    near, q_level, q_prev = pl.pallas_call(
         load_kernel,
-        out_shape=[shaped(5, BAND, SECTOR, AXIAL)] * 2,
+        out_shape=[shaped(5, SECTOR, AXIAL)] + [shaped(5, BAND, SECTOR, AXIAL)] * 2,
         in_specs=[hbm] * 2,
-        out_specs=[vmem()] * 2,
-        scratch_shapes=[pltpu.SemaphoreType.DMA((2,))],
+        out_specs=[vmem()] * 3,
+        scratch_shapes=[pltpu.SemaphoreType.DMA((3,))],
         compiler_params=pltpu.CompilerParams(vmem_limit_bytes=LOAD_VMEM),
         cost_estimate=pl.CostEstimate(flops=0, bytes_accessed=3_000_000, transcendentals=0),
     )(q_level, q_prev)
+    first_in = rad_swap(near, lambda place: place != RING - 1)
+    second_in = rad_swap(near, lambda place: place == RING - 1)
     edge_columns = pl.pallas_call(
         edges,
         out_shape=shaped(5, 2, 32, AXIAL),
@@ -522,15 +575,22 @@
         compiler_params=limit(4),
         cost_estimate=pl.CostEstimate(flops=5_000_000, bytes_accessed=2_000_000, transcendentals=50_000),
     )(q_level, q_prev)
-    own_columns, core_out, other_out = pl.pallas_call(
-        pack,
-        out_shape=[shaped(5, 2, BAND, AXIAL)] + [shaped(168, AXIAL)] * 2,
+    other_out = pl.pallas_call(
+        for_other,
+        out_shape=shaped(168, AXIAL),
         in_specs=[vmem()] * 3,
+        out_specs=vmem(),
+        compiler_params=limit(4),
+    )(q_level, edge_columns, first_in)
+    other_in = lax.ppermute(other_out, "theta", other)
+    own_columns, core_out, rad_in = pl.pallas_call(
+        for_core,
+        out_shape=[shaped(5, 2, BAND, AXIAL), shaped(168, AXIAL), shaped(5, SECTOR, AXIAL)],
+        in_specs=[vmem()] * 4,
         out_specs=[vmem()] * 3,
         compiler_params=limit(4),
-    )(q_level, edge_columns, rad_in)
+    )(q_level, edge_columns, first_in, second_in)
     core_in = lax.ppermute(core_out, "theta", core)
-    other_in = lax.ppermute(other_out, "theta", other)
     next_out = pl.pallas_call(
         neighbour,
         out_shape=shaped(5, SECTOR, AXIAL),
@@ -547,19 +607,27 @@
         compiler_params=limit(8),
         cost_estimate=pl.CostEstimate(flops=10_000_000, bytes_accessed=3_500_000, transcendentals=100_000),
     )(blade, q_level, q_prev, rad_in)
+    corner = pl.pallas_call(
+        corner_kernel,
+        out_shape=shaped(8, AXIAL),
+        in_specs=[vmem()] * 2,
+        out_specs=vmem(),
+        compiler_params=limit(4),
+    )(other_in, part)
+    corner_in = rad_swap(corner, lambda place: place == 0)
     flow_state, send = pl.pallas_call(
         final,
         out_shape=[shaped(5, BAND, SECTOR, AXIAL), shaped(2 * AXIAL, BAND * SECTOR)],
-        in_specs=[vmem()] * 9,
+        in_specs=[vmem()] * 10,
         out_specs=[vmem()] * 2,
         scratch_shapes=[
-            pltpu.VMEM((5, BAND, SECTOR, AXIAL), F32),
+            pltpu.VMEM((5, 4, SECTOR, AXIAL), F32),
             pltpu.VMEM((5, SECTOR, AXIAL), F32),
-            pltpu.VMEM((5, BAND, SECTOR, AXIAL), F32),
+            pltpu.VMEM((5, 4, SECTOR, AXIAL), F32),
             pltpu.VMEM((2, BAND, SECTOR, AXIAL), F32),
         ],
         compiler_params=limit(8),
-    )(blade, edge_columns, own_columns, rad_in, part, source, next_in, other_in, core_in)
+    )(blade, edge_columns, own_columns, rad_in, part, source, next_in, other_in, core_in, corner_in)
     chips = sectors // 2
     got = lax.all_to_all(
         send.reshape(chips, 8, 128),

time: 48.1 us -> 51.4 us (1.069)
  starting transfers between devices: 13.2 us -> 18 us
  waiting for transfers between devices: 1.49 us -> 0.66 us
  blocking collectives: 24 us -> 23.3 us
  local copies, waits for them, and re-layouts: 0.01 us -> 0.69 us
  Pallas kernels: 8.45 us -> 7.78 us
    ppermute x1 -> x3, starting transfers between devices: 2.21 us -> 5.36 us  [rad_swap(): return lax.ppermute(x, ('theta', 'rad'), pairs)]
    ppermute x1, starting transfers between devices: 0.09 us -> 1.91 us  [per_device(): given = lax.ppermute(give, 'theta', core)]
    all_to_all x1, blocking collectives: 24 us -> 23.3 us  [per_device(): lax.all_to_all(send.reshape(chips, 8, 128), 'theta', split_axis=0, concat...]
    pallas_call x3 -> x4, Pallas kernels: 2.18 us -> 1.5 us  [the longest x1 1.35 us: per_device(): pl.pallas_call(load_kernel, out_shape=[shaped(5, SECTOR, AXIAL)] + [shape...]
    unnamed x4, local copies, waits for them, and re-layouts: 0.01 us -> 0.69 us
    ppermute x1, starting transfers between devices: 3 us -> 3.56 us  [per_device(): other_in = lax.ppermute(other_out, 'theta', other)]
  transfers between devices with their start and end apart: 5 -> 7, of which waited for: 2 -> 1; matrix products, arithmetic and copies ran while one was open for 0% -> 0% of each run, Pallas kernels for 9% -> 7%
where the time goes in v11:
time: 51.4 us; the launch traced here: 51.2 us
  blocking collectives  23.3 us (45%)
  starting transfers between devices  18 us (35%)
  Pallas kernels  7.78 us (15%)
  between operations  0.76 us (1%)
  local copies, waits for them, and re-layouts  0.69 us (1%)
  waiting for transfers between devices  0.66 us (1%)
    all_to_all x1, blocking collectives, per_device(): lax.all_to_all(send.reshape(chips, 8, 128), 'theta', split_axis=0, concat...  23.3 us
    ppermute x1, starting transfers between devices, per_device(): core_in = lax.ppermute(core_out, 'theta', core)  7.12 us
    ppermute x3, starting transfers between devices, rad_swap(): return lax.ppermute(x, ('theta', 'rad'), pairs)  5.36 us
    ppermute x1, starting transfers between devices, per_device(): other_in = lax.ppermute(other_out, 'theta', other)  3.56 us
    ppermute x1, starting transfers between devices, per_device(): given = lax.ppermute(give, 'theta', core)  1.91 us
    pallas_call x1, Pallas kernels, per_device(): pl.pallas_call(final, out_shape=[shaped(5, BAND, SECTOR, AXIAL), shaped(2...  1.85 us
    pallas_call x1, Pallas kernels, per_device(): pl.pallas_call(early, out_shape=[shaped(5, BAND, SECTOR, AXIAL)] * 2, in_...  1.49 us
    pallas_call x1, Pallas kernels, per_device(): pl.pallas_call(load_kernel, out_shape=[shaped(5, SECTOR, AXIAL)] + [shape...  1.35 us
  transfers between devices with their start and end apart: 7, of which 1 were waited for; matrix products, arithmetic and copies ran while one was open for 0% of the time, Pallas kernels for 7%

profile of v11, /device:TPU:1, one launch (start us, length us, event | category | flops | bytes accessed | tf_op | source)
XLA Modules:
  0.0 51.2 jit_solution(8541332581887162325)
XLA Ops:
  0.6 1.3 %shard_map.59 = (f32[5,8,256]{2,1,0:T(8,128)S(1)}, f32[5,16,8,256]{3,2,1,0:T(8,128)S(1)}, f32[5,16,8,256]{3,2,1,0:T(8,128)S(1)}) custom-call(f32[5,16,8,256]{3,2,1,0:T(8,128)} %q_ref.1, f32[5,16,8,256]{3,2,1,0:T(8,128)} %qp_ref.1), custom_call_target="tpu_custom_call" | custom-call | bytes 3000000 | tf_op jit(solution)/shard_map/pallas_call | solution.py:558
  2.0 4.0 %collective-permute-start = (f32[5,8,256]{2,1,0:T(8,128)S(1)}, f32[5,8,256]{2,1,0:T(8,128)S(1)}, u32[]{:S(2)}, u32[]{:S(2)}) collective-permute-start(f32[5,8,256]{2,1,0:T(8,128)S(1)} %get-tuple-element.16), channel_id=1, source_target_pairs={{0,1},{1,0},{2,3},{3,2},{4,5},{5,4},{6,7},{7,6},{8,9},{9,8},{10,11... | collective-permute-start | bytes 122888 | tf_op jit(solution)/shard_map/ppermute | solution.py:556
  6.0 0.7 %collective-permute-start.1 = (f32[5,8,256]{2,1,0:T(8,128)S(1)}, f32[5,8,256]{2,1,0:T(8,128)S(1)}, u32[]{:S(2)}, u32[]{:S(2)}) collective-permute-start(f32[5,8,256]{2,1,0:T(8,128)S(1)} %get-tuple-element.16), channel_id=1, source_target_pairs={{30,31},{31,30},{62,63},{63,62},{94,95},{95,94},{126,127},{127,126... | collective-permute-start | bytes 122888 | tf_op jit(solution)/shard_map/ppermute | solution.py:556
  6.7 0.7 %shard_map.60.refs_1_ = f32[5,2,32,256]{3,2,1,0:T(8,128)S(1)} custom-call(f32[5,16,8,256]{3,2,1,0:T(8,128)S(1)} %get-tuple-element.14.refs_0_.refs_1_, f32[5,16,8,256]{3,2,1,0:T(8,128)S(1)} %get-tuple-element.15.refs_1_.refs_2_), custom_call_target="tpu_custom_call" | custom-call | flops 5000000 | bytes 2000000 | tf_op jit(solution)/shard_map/pallas_call | solution.py:569
  7.4 0.0 collective-permute-done.refs_2_
  7.4 0.1 shard_map.64
  7.5 3.6 %collective-permute-start.3 = (f32[168,256]{1,0:T(8,128)S(1)}, f32[168,256]{1,0:T(8,128)S(1)}, u32[]{:S(2)}, u32[]{:S(2)}) collective-permute-start(f32[168,256]{1,0:T(8,128)S(1)} %shard_map.64), channel_id=1, source_target_pairs={{0,254},{2,4},{4,2},{6,8},{8,6},{10,12},{12,10},{14,16},{16,14},{1... | collective-permute-start | bytes 516104 | tf_op jit(solution)/shard_map/ppermute | solution.py:585
  11.1 0.0 collective-permute-done.1.refs_3_
  11.1 0.1 shard_map.61
  11.1 7.1 %collective-permute-start.4 = (f32[168,256]{1,0:T(8,128)S(1)}, f32[168,256]{1,0:T(8,128)S(1)}, u32[]{:S(2)}, u32[]{:S(2)}) collective-permute-start(f32[168,256]{1,0:T(8,128)S(1)} %get-tuple-element.21), channel_id=1, source_target_pairs={{0,2},{2,0},{4,6},{6,4},{8,10},{10,8},{12,14},{14,12},{16,18},{18,... | collective-permute-start | bytes 516104 | tf_op jit(solution)/shard_map/ppermute | solution.py:593
  18.3 0.0 copy-start.1
  18.3 0.7 %copy-done.1 = s32[256]{0:T(256)S(1)} copy-done((s32[256]{0:T(256)S(1)}, s32[256]{0:T(256)}, u32[]{:S(2)}) %copy-start.1) | copy-done | bytes 1048
  18.9 0.2 shard_map.63
  19.1 0.1 collective-permute-start.2
  19.2 1.5 %shard_map.62 = (f32[5,16,8,256]{3,2,1,0:T(8,128)S(1)}, f32[5,16,8,256]{3,2,1,0:T(8,128)S(1)}) custom-call(s32[1,256]{1,0:T(1,128)S(1)} %bitcast.6, f32[5,16,8,256]{3,2,1,0:T(8,128)S(1)} %get-tuple-element.14.refs_0_.refs_1_, f32[5,16,8,256]{3,2,1,0:T(8,128)S(1)} %get-tuple-element.15.refs_1_.refs_2_, f32[5,8,256]{2,1,0:T(8,128)S(1)} %get-tuple-element.18.refs_3_), custom_call_target="tpu_custom_call" | custom-call | flops 10000000 | bytes 3500000 | tf_op jit(solution)/shard_map/pallas_call | solution.py:602
  20.7 0.0 collective-permute-done.3.other_ref.refs_7_
  20.8 0.7 %collective-permute-start.5 = (f32[8,256]{1,0:T(8,128)S(1)}, f32[8,256]{1,0:T(8,128)S(1)}, u32[]{:S(2)}, u32[]{:S(2)}) collective-permute-start(f32[8,256]{1,0:T(8,128)S(1)} %shard_map.65), channel_id=1, source_target_pairs={{0,1},{1,0},{32,33},{33,32},{64,65},{65,64},{96,97},{97,96},{128,1... | collective-permute-start | bytes 24584 | tf_op jit(solution)/shard_map/ppermute | solution.py:556
  21.4 0.6 %collective-permute-done.2.refs_6_ = f32[5,8,256]{2,1,0:T(8,128)S(1)} collective-permute-done((f32[5,8,256]{2,1,0:T(8,128)S(1)}, f32[5,8,256]{2,1,0:T(8,128)S(1)}, u32[]{:S(2)}, u32[]{:S(2)}) %collective-permute-start.2) | collective-permute-done | bytes 40992 | tf_op jit(solution)/shard_map/ppermute | solution.py:601
  22.1 0.0 collective-permute-done.4.refs_8_
  22.1 0.0 collective-permute-done.5.refs_9_
  22.1 1.9 %shard_map.66 = (f32[5,16,8,256]{3,2,1,0:T(8,128)S(1)}, f32[512,128]{1,0:T(8,128)S(1)}) custom-call(s32[1,256]{1,0:T(1,128)S(1)} %bitcast.7, f32[5,2,32,256]{3,2,1,0:T(8,128)S(1)} %shard_map.60.refs_1_, f32[5,2,16,256]{3,2,1,0:T(8,128)S(1)} %get-tuple-element.17.refs_2_, f32[5,8,256]{2,1,0:T(8,128)S(1)} %get-tuple-element.18.refs_3_, ...), custom_call_target="tpu_custom_call" | custom-call | tf_op jit(solution)/shard_map/pallas_call | solution.py:618
  23.9 0.0 copy-start
  24.0 23.3 %all_to_all.5 = f32[64,8,128]{2,1,0:T(8,128)S(1)} all-to-all(f32[64,8,128]{2,1,0:T(8,128)S(1)} %bitcast.4), channel_id=1, replica_groups={{0,4,8,12,16,20,24,28,32,36,40,44,48,52,56,60,64,68,72,76,80,84,88,92,9..., dimensions={0} | all-to-all | bytes 524288 | tf_op jit(solution)/shard_map/all_to_all | solution.py:632
  47.2 0.0 copy-done
  47.2 0.6 %shard_map.68 = (f32[64,128]{1,0:T(8,128)S(1)}, f32[64,128]{1,0:T(8,128)S(1)}) custom-call(f32[512,128]{1,0:T(8,128)S(1)} %bitcast.3, f32[2,512,128]{2,1,0:T(8,128)S(1)} %copy-done), custom_call_target="tpu_custom_call" | custom-call | tf_op jit(solution)/shard_map/pallas_call | solution.py:640
  47.8 1.9 %collective-permute-start.6 = (f32[64,128]{1,0:T(8,128)S(1)}, f32[64,128]{1,0:T(8,128)S(1)}, u32[]{:S(2)}, u32[]{:S(2)}) collective-permute-start(f32[64,128]{1,0:T(8,128)S(1)} %get-tuple-element.25), channel_id=1, source_target_pairs={{0,2},{2,0},{4,6},{6,4},{8,10},{10,8},{12,14},{14,12},{16,18},{18,... | collective-permute-start | bytes 98312 | tf_op jit(solution)/shard_map/ppermute | solution.py:648
  49.7 0.8 %shard_map.67 = f32[5,16,8,256]{3,2,1,0:T(8,128)} custom-call(f32[5,16,8,256]{3,2,1,0:T(8,128)S(1)} %get-tuple-element.22.flow_ref), custom_call_target="tpu_custom_call" | custom-call | bytes 1400000 | tf_op jit(solution)/shard_map/pallas_call | solution.py:649
  50.6 0.0 collective-permute-done.6.got_ref
  50.6 0.6 %shard_map.69 = f32[2,16,256]{2,1,0:T(8,128)} custom-call(f32[64,128]{1,0:T(8,128)S(1)} %get-tuple-element.24.keep_ref, f32[64,128]{1,0:T(8,128)S(1)} %collective-permute-done.6.got_ref), custom_call_target="tpu_custom_call" | custom-call | tf_op jit(solution)/shard_map/pallas_call | solution.py:658
  (1 shorter events, 0.0 us)
Async XLA Ops:
  2.0 5.4 %collective-permute-start = (f32[5,8,256]{2,1,0:T(8,128)S(1)}, f32[5,8,256]{2,1,0:T(8,128)S(1)}, u32[]{:S(2)}, u32[]{:S(2)}) collective-permute-start(f32[5,8,256]{2,1,0:T(8,128)S(1)} %get-tuple-element.16), channel_id=1, source_target_pairs={{0,1},{1,0},{2,3},{3,2},{4,5},{5,4},{6,7},{7,6},{8,9},{9,8},{10,11... | collective-permute-start | bytes 122888 | tf_op jit(solution)/shard_map/ppermute | solution.py:556
  6.0 5.0 %collective-permute-start.1 = (f32[5,8,256]{2,1,0:T(8,128)S(1)}, f32[5,8,256]{2,1,0:T(8,128)S(1)}, u32[]{:S(2)}, u32[]{:S(2)}) collective-permute-start(f32[5,8,256]{2,1,0:T(8,128)S(1)} %get-tuple-element.16), channel_id=1, source_target_pairs={{30,31},{31,30},{62,63},{63,62},{94,95},{95,94},{126,127},{127,126... | collective-permute-start | bytes 122888 | tf_op jit(solution)/shard_map/ppermute | solution.py:556
  7.5 13.2 %collective-permute-start.3 = (f32[168,256]{1,0:T(8,128)S(1)}, f32[168,256]{1,0:T(8,128)S(1)}, u32[]{:S(2)}, u32[]{:S(2)}) collective-permute-start(f32[168,256]{1,0:T(8,128)S(1)} %shard_map.64), channel_id=1, source_target_pairs={{0,254},{2,4},{4,2},{6,8},{8,6},{10,12},{12,10},{14,16},{16,14},{1... | collective-permute-start | bytes 516104 | tf_op jit(solution)/shard_map/ppermute | solution.py:585
  11.1 10.9 %collective-permute-start.4 = (f32[168,256]{1,0:T(8,128)S(1)}, f32[168,256]{1,0:T(8,128)S(1)}, u32[]{:S(2)}, u32[]{:S(2)}) collective-permute-start(f32[168,256]{1,0:T(8,128)S(1)} %get-tuple-element.21), channel_id=1, source_target_pairs={{0,2},{2,0},{4,6},{6,4},{8,10},{10,8},{12,14},{14,12},{16,18},{18,... | collective-permute-start | bytes 516104 | tf_op jit(solution)/shard_map/ppermute | solution.py:593
  18.3 0.7 %copy-start.1 = (s32[256]{0:T(256)S(1)}, s32[256]{0:T(256)}, u32[]{:S(2)}) copy-start(s32[256]{0:T(256)} %param.6) | copy-start | bytes 3076
  19.1 2.9 %collective-permute-start.2 = (f32[5,8,256]{2,1,0:T(8,128)S(1)}, f32[5,8,256]{2,1,0:T(8,128)S(1)}, u32[]{:S(2)}, u32[]{:S(2)}) collective-permute-start(f32[5,8,256]{2,1,0:T(8,128)S(1)} %shard_map.63), channel_id=1, source_target_pairs={{0,1},{1,0},{2,3},{3,2},{4,5},{5,4},{6,7},{7,6},{8,9},{9,8},{10,11... | collective-permute-start | bytes 122888 | tf_op jit(solution)/shard_map/ppermute | solution.py:601
  20.8 1.3 %collective-permute-start.5 = (f32[8,256]{1,0:T(8,128)S(1)}, f32[8,256]{1,0:T(8,128)S(1)}, u32[]{:S(2)}, u32[]{:S(2)}) collective-permute-start(f32[8,256]{1,0:T(8,128)S(1)} %shard_map.65), channel_id=1, source_target_pairs={{0,1},{1,0},{32,33},{33,32},{64,65},{65,64},{96,97},{97,96},{128,1... | collective-permute-start | bytes 24584 | tf_op jit(solution)/shard_map/ppermute | solution.py:556
  23.9 23.3 %copy-start = (f32[2,512,128]{2,1,0:T(8,128)S(1)}, f32[2,512,128]{2,1,0:T(8,128)}, u32[]{:S(2)}) copy-start(f32[2,512,128]{2,1,0:T(8,128)} %constant.2.clone.basis_ref) | copy-start | bytes 1572868
  47.8 2.8 %collective-permute-start.6 = (f32[64,128]{1,0:T(8,128)S(1)}, f32[64,128]{1,0:T(8,128)S(1)}, u32[]{:S(2)}, u32[]{:S(2)}) collective-permute-start(f32[64,128]{1,0:T(8,128)S(1)} %get-tuple-element.25), channel_id=1, source_target_pairs={{0,2},{2,0},{4,6},{6,4},{8,10},{10,8},{12,14},{14,12},{16,18},{18,... | collective-permute-start | bytes 98312 | tf_op jit(solution)/shard_map/ppermute | solution.py:648

commit v12 on v10

--- a/solution.py
+++ b/solution.py
@@ -251,12 +251,16 @@
     between = face(q, (f, speed), qn, (fn, ahead(speed)))
     swirl = []
     for v in ALL:
-        end = 0.0 if ends is None else ends[v]
-        right = jnp.where(sub == SECTOR - 1, end, between[v])
-        left = jnp.where(sub == 0, end, pltpu.roll(between[v], 1, 0))
+        first, last = (0.0, 0.0) if ends is None else ends[v]
+        right = jnp.where(sub == SECTOR - 1, last, between[v])
+        left = jnp.where(sub == 0, first, pltpu.roll(between[v], 1, 0))
         swirl.append(inv_h * (right - left))
     radial = [a_out * g_out[v] - a_in * g_in[v] for v in ALL]
     return advance(q, prim, source, axial_difference(q, prim, lane), radial, swirl, inv_r, inv_h, spin_r, blade)
+
+
+def column_rows(ref, v, j):
+    return [ref[v, 2 * side + j // SECTOR, j % SECTOR : j % SECTOR + 1, :] for side in (0, 1)]
 
 
 def sweep(load, step, store):
@@ -331,7 +335,7 @@
     core_ref,
     flow_ref,
     send_ref,
-    p1,
+    own_rows,
     nearby,
     ends,
     fields,
@@ -342,7 +346,6 @@
     mask = masks()
     blade = blades(blade_ref, SECTOR)
     for v in ALL:
-        p1[v] = p1_ref[v]
         nearby[v] = next_ref[v]
 
     geo = Columns(band * BAND, total_rows, circle)
@@ -386,19 +389,25 @@
 
         faces = ordered(near_next, primitives(near_next), own_next, primitives(own_next))
         for v in ALL:
-            p1[v, :, at, :] = own_next[v]
+            own_rows[v, 2 * side : 2 * side + 2] = own_next[v].reshape(2, SECTOR, AXIAL)
             nearby[v, at : at + 1, :] = next_ref[v, at : at + 1, :] + corner_scale * corner_face[v]
-            ends[v, :, at, :] = faces[v]
+            ends[v, 2 * side : 2 * side + 2] = faces[v].reshape(2, SECTOR, AXIAL)
+
+    sub = mask[1]
+
+    def row(v, j):
+        first, last = column_rows(own_rows, v, j)
+        return jnp.where(sub == 0, first, jnp.where(sub == SECTOR - 1, last, p1_ref[v, j]))
 
     def load(j):
         if j < 0:
-            return [jnp.where(low, MIRROR[v] * p1[v, 0], nearby[v]) for v in ALL]
+            return [jnp.where(low, MIRROR[v] * row(v, 0), nearby[v]) for v in ALL]
         if j == BAND:
-            return [jnp.where(low, nearby[v], MIRROR[v] * p1[v, BAND - 1]) for v in ALL]
-        return [p1[v, j] for v in ALL]
+            return [jnp.where(low, nearby[v], MIRROR[v] * row(v, BAND - 1)) for v in ALL]
+        return [row(v, j) for v in ALL]
 
     def step(j, q, prim, g_in, g_out):
-        source, end = [source_ref[v, j] for v in ALL], [ends[v, j] for v in ALL]
+        source, end = [source_ref[v, j] for v in ALL], [column_rows(ends, v, j) for v in ALL]
         return row_step(coefficients(low, table, j), q, prim, source, g_in, g_out, end, mask, blade)
 
     def store(j, q):
@@ -553,9 +562,9 @@
         in_specs=[vmem()] * 9,
         out_specs=[vmem()] * 2,
         scratch_shapes=[
-            pltpu.VMEM((5, BAND, SECTOR, AXIAL), F32),
+            pltpu.VMEM((5, 4, SECTOR, AXIAL), F32),
             pltpu.VMEM((5, SECTOR, AXIAL), F32),
-            pltpu.VMEM((5, BAND, SECTOR, AXIAL), F32),
+            pltpu.VMEM((5, 4, SECTOR, AXIAL), F32),
             pltpu.VMEM((2, BAND, SECTOR, AXIAL), F32),
         ],
         compiler_params=limit(8),

time: 48.1 us -> 48 us (level)
  no operation moved by 1% of the time
where the time goes in v12:
time: 48 us; the launch traced here: 47.8 us
  blocking collectives  24 us (50%)
  starting transfers between devices  13.2 us (28%)
  Pallas kernels  8.32 us (17%)
  waiting for transfers between devices  1.49 us (3%)
  between operations  0.72 us (2%)
    all_to_all x1, blocking collectives, per_device(): lax.all_to_all(send.reshape(chips, 8, 128), 'theta', split_axis=0, concat...  24 us
    ppermute x1, starting transfers between devices, per_device(): core_in = lax.ppermute(core_out, 'theta', core)  7.59 us
    ppermute x1, starting transfers between devices, per_device(): other_in = lax.ppermute(other_out, 'theta', other)  3 us
    ppermute x1, starting transfers between devices, per_device(): rad_in = lax.ppermute(near, 'rad', swap)  2.21 us
    pallas_call x1, Pallas kernels, per_device(): pl.pallas_call(final, out_shape=[shaped(5, BAND, SECTOR, AXIAL), shaped(2...  1.82 us
    pallas_call x1, Pallas kernels, per_device(): pl.pallas_call(early, out_shape=[shaped(5, BAND, SECTOR, AXIAL)] * 2, in_...  1.45 us
    pallas_call x1, Pallas kernels, per_device(): pl.pallas_call(load_kernel, out_shape=[shaped(5, BAND, SECTOR, AXIAL)] *...  1.3 us
    ppermute x1, waiting for transfers between devices, per_device(): next_in = lax.ppermute(next_out, 'rad', swap)  1.14 us
  transfers between devices with their start and end apart: 5, of which 2 were waited for; matrix products, arithmetic and copies ran while one was open for 0% of the time, Pallas kernels for 9%

profile of v12, /device:TPU:1, one launch (start us, length us, event | category | flops | bytes accessed | tf_op | source)
XLA Modules:
  0.0 47.8 jit_solution(7783980318148684576)
XLA Ops:
  0.6 0.8 %shard_map.61 = f32[5,8,256]{2,1,0:T(8,128)S(1)} custom-call(f32[5,16,8,256]{3,2,1,0:T(8,128)} %q_ref.3), custom_call_target="tpu_custom_call" | custom-call | tf_op jit(solution)/shard_map/pallas_call | solution.py:507
  1.4 2.2 %collective-permute-start = (f32[5,8,256]{2,1,0:T(8,128)S(1)}, f32[5,8,256]{2,1,0:T(8,128)S(1)}, u32[]{:S(2)}, u32[]{:S(2)}) collective-permute-start(f32[5,8,256]{2,1,0:T(8,128)S(1)} %shard_map.61), channel_id=1, source_target_pairs={{0,1},{1,0},{2,3},{3,2},{4,5},{5,4},{6,7},{7,6},{8,9},{9,8},{10,11... | collective-permute-start | bytes 122888 | tf_op jit(solution)/shard_map/ppermute | solution.py:515
  3.6 1.3 %shard_map.59 = (f32[5,16,8,256]{3,2,1,0:T(8,128)S(1)}, f32[5,16,8,256]{3,2,1,0:T(8,128)S(1)}) custom-call(f32[5,16,8,256]{3,2,1,0:T(8,128)} %q_ref.3, f32[5,16,8,256]{3,2,1,0:T(8,128)} %qp_ref.1), custom_call_target="tpu_custom_call" | custom-call | bytes 3000000 | tf_op jit(solution)/shard_map/pallas_call | solution.py:516
  5.0 0.7 %shard_map.60.refs_1_ = f32[5,2,32,256]{3,2,1,0:T(8,128)S(1)} custom-call(f32[5,16,8,256]{3,2,1,0:T(8,128)S(1)} %get-tuple-element.13.refs_0_.refs_1_, f32[5,16,8,256]{3,2,1,0:T(8,128)S(1)} %get-tuple-element.14.refs_1_.refs_2_), custom_call_target="tpu_custom_call" | custom-call | flops 5000000 | bytes 2000000 | tf_op jit(solution)/shard_map/pallas_call | solution.py:525
  5.6 0.0 collective-permute-done.refs_2_.refs_3_
  5.6 0.1 shard_map.62
  5.7 3.0 %collective-permute-start.2 = (f32[168,256]{1,0:T(8,128)S(1)}, f32[168,256]{1,0:T(8,128)S(1)}, u32[]{:S(2)}, u32[]{:S(2)}) collective-permute-start(f32[168,256]{1,0:T(8,128)S(1)} %get-tuple-element.18), channel_id=1, source_target_pairs={{0,254},{2,4},{4,2},{6,8},{8,6},{10,12},{12,10},{14,16},{16,14},{1... | collective-permute-start | bytes 516104 | tf_op jit(solution)/shard_map/ppermute | solution.py:542
  8.7 0.0 copy-start.1
  8.7 7.6 %collective-permute-start.3 = (f32[168,256]{1,0:T(8,128)S(1)}, f32[168,256]{1,0:T(8,128)S(1)}, u32[]{:S(2)}, u32[]{:S(2)}) collective-permute-start(f32[168,256]{1,0:T(8,128)S(1)} %get-tuple-element.19), channel_id=1, source_target_pairs={{0,2},{2,0},{4,6},{6,4},{8,10},{10,8},{12,14},{14,12},{16,18},{18,... | collective-permute-start | bytes 516104 | tf_op jit(solution)/shard_map/ppermute | solution.py:541
  16.3 0.0 copy-done.1
  16.3 0.2 shard_map.64
  16.5 0.3 collective-permute-start.1
  16.8 1.4 %shard_map.63 = (f32[5,16,8,256]{3,2,1,0:T(8,128)S(1)}, f32[5,16,8,256]{3,2,1,0:T(8,128)S(1)}) custom-call(s32[1,256]{1,0:T(1,128)S(1)} %bitcast.6, f32[5,16,8,256]{3,2,1,0:T(8,128)S(1)} %get-tuple-element.13.refs_0_.refs_1_, f32[5,16,8,256]{3,2,1,0:T(8,128)S(1)} %get-tuple-element.14.refs_1_.refs_2_, f32[5,8,256]{2,1,0:T(8,128)S(1)} %collective-permute-done.refs_2_.refs_3_), custom_call_target="tpu_custom_call" | custom-call | flops 10000000 | bytes 3500000 | tf_op jit(solution)/shard_map/pallas_call | solution.py:551
  18.3 1.1 %collective-permute-done.1.refs_6_ = f32[5,8,256]{2,1,0:T(8,128)S(1)} collective-permute-done((f32[5,8,256]{2,1,0:T(8,128)S(1)}, f32[5,8,256]{2,1,0:T(8,128)S(1)}, u32[]{:S(2)}, u32[]{:S(2)}) %collective-permute-start.1) | collective-permute-done | bytes 40992 | tf_op jit(solution)/shard_map/ppermute | solution.py:550
  19.4 0.0 collective-permute-done.2.refs_7_
  19.5 0.0 collective-permute-done.3.refs_8_
  19.5 1.8 %shard_map.65 = (f32[5,16,8,256]{3,2,1,0:T(8,128)S(1)}, f32[512,128]{1,0:T(8,128)S(1)}) custom-call(s32[1,256]{1,0:T(1,128)S(1)} %bitcast.7, f32[5,2,32,256]{3,2,1,0:T(8,128)S(1)} %shard_map.60.refs_1_, f32[5,2,16,256]{3,2,1,0:T(8,128)S(1)} %get-tuple-element.15.refs_2_, f32[5,8,256]{2,1,0:T(8,128)S(1)} %collective-permute-done.refs_2_.refs_3_, ...), custom_call_target="tpu_custom_call" | custom-call | tf_op jit(solution)/shard_map/pallas_call | solution.py:559
  21.3 0.0 copy-start
  21.3 24.0 %all_to_all.5 = f32[64,8,128]{2,1,0:T(8,128)S(1)} all-to-all(f32[64,8,128]{2,1,0:T(8,128)S(1)} %bitcast.4), channel_id=1, replica_groups={{0,4,8,12,16,20,24,28,32,36,40,44,48,52,56,60,64,68,72,76,80,84,88,92,9..., dimensions={0} | all-to-all | bytes 524288 | tf_op jit(solution)/shard_map/all_to_all | solution.py:573
  45.3 0.0 copy-done
  45.3 0.6 %shard_map.67 = (f32[64,128]{1,0:T(8,128)S(1)}, f32[64,128]{1,0:T(8,128)S(1)}) custom-call(f32[512,128]{1,0:T(8,128)S(1)} %bitcast.3, f32[2,512,128]{2,1,0:T(8,128)S(1)} %copy-done), custom_call_target="tpu_custom_call" | custom-call | tf_op jit(solution)/shard_map/pallas_call | solution.py:581
  45.9 0.1 collective-permute-start.4
  46.0 0.8 %shard_map.66 = f32[5,16,8,256]{3,2,1,0:T(8,128)} custom-call(f32[5,16,8,256]{3,2,1,0:T(8,128)S(1)} %get-tuple-element.20.flow_ref), custom_call_target="tpu_custom_call" | custom-call | bytes 1400000 | tf_op jit(solution)/shard_map/pallas_call | solution.py:590
  46.8 0.3 collective-permute-done.4.got_ref
  47.2 0.6 %shard_map.68 = f32[2,16,256]{2,1,0:T(8,128)} custom-call(f32[64,128]{1,0:T(8,128)S(1)} %get-tuple-element.22.keep_ref, f32[64,128]{1,0:T(8,128)S(1)} %collective-permute-done.4.got_ref), custom_call_target="tpu_custom_call" | custom-call | tf_op jit(solution)/shard_map/pallas_call | solution.py:599
Async XLA Ops:
  1.4 4.2 %collective-permute-start = (f32[5,8,256]{2,1,0:T(8,128)S(1)}, f32[5,8,256]{2,1,0:T(8,128)S(1)}, u32[]{:S(2)}, u32[]{:S(2)}) collective-permute-start(f32[5,8,256]{2,1,0:T(8,128)S(1)} %shard_map.61), channel_id=1, source_target_pairs={{0,1},{1,0},{2,3},{3,2},{4,5},{5,4},{6,7},{7,6},{8,9},{9,8},{10,11... | collective-permute-start | bytes 122888 | tf_op jit(solution)/shard_map/ppermute | solution.py:515
  5.7 13.7 %collective-permute-start.2 = (f32[168,256]{1,0:T(8,128)S(1)}, f32[168,256]{1,0:T(8,128)S(1)}, u32[]{:S(2)}, u32[]{:S(2)}) collective-permute-start(f32[168,256]{1,0:T(8,128)S(1)} %get-tuple-element.18), channel_id=1, source_target_pairs={{0,254},{2,4},{4,2},{6,8},{8,6},{10,12},{12,10},{14,16},{16,14},{1... | collective-permute-start | bytes 516104 | tf_op jit(solution)/shard_map/ppermute | solution.py:542
  8.7 7.6 %copy-start.1 = (s32[256]{0:T(256)S(1)}, s32[256]{0:T(256)}, u32[]{:S(2)}) copy-start(s32[256]{0:T(256)} %param.6) | copy-start | bytes 3076
  8.7 10.7 %collective-permute-start.3 = (f32[168,256]{1,0:T(8,128)S(1)}, f32[168,256]{1,0:T(8,128)S(1)}, u32[]{:S(2)}, u32[]{:S(2)}) collective-permute-start(f32[168,256]{1,0:T(8,128)S(1)} %get-tuple-element.19), channel_id=1, source_target_pairs={{0,2},{2,0},{4,6},{6,4},{8,10},{10,8},{12,14},{14,12},{16,18},{18,... | collective-permute-start | bytes 516104 | tf_op jit(solution)/shard_map/ppermute | solution.py:541
  16.5 2.9 %collective-permute-start.1 = (f32[5,8,256]{2,1,0:T(8,128)S(1)}, f32[5,8,256]{2,1,0:T(8,128)S(1)}, u32[]{:S(2)}, u32[]{:S(2)}) collective-permute-start(f32[5,8,256]{2,1,0:T(8,128)S(1)} %shard_map.64), channel_id=1, source_target_pairs={{0,1},{1,0},{2,3},{3,2},{4,5},{5,4},{6,7},{7,6},{8,9},{9,8},{10,11... | collective-permute-start | bytes 122888 | tf_op jit(solution)/shard_map/ppermute | solution.py:550
  21.3 24.0 %copy-start = (f32[2,512,128]{2,1,0:T(8,128)S(1)}, f32[2,512,128]{2,1,0:T(8,128)}, u32[]{:S(2)}) copy-start(f32[2,512,128]{2,1,0:T(8,128)} %constant.2.clone.basis_ref) | copy-start | bytes 1572868
  45.9 1.3 %collective-permute-start.4 = (f32[64,128]{1,0:T(8,128)S(1)}, f32[64,128]{1,0:T(8,128)S(1)}, u32[]{:S(2)}, u32[]{:S(2)}) collective-permute-start(f32[64,128]{1,0:T(8,128)S(1)} %get-tuple-element.23), channel_id=1, source_target_pairs={{0,2},{2,0},{4,6},{6,4},{8,10},{10,8},{12,14},{14,12},{16,18},{18,... | collective-permute-start | bytes 98312 | tf_op jit(solution)/shard_map/ppermute | solution.py:589

commit v13 on v12

--- a/solution.py
+++ b/solution.py
@@ -13,6 +13,7 @@
 KAPPA = 2.0
 
 BAND = 16
+HALF_BAND = BAND // 2
 SECTOR = 8
 AXIAL = 256
 RAD_VMEM = 56_200_000
@@ -414,13 +415,13 @@
         for v in ALL:
             flow_ref[v, j] = q[v]
         ux, _, _, pressure, _ = primitives(q)
-        fields[0, j] = pressure
-        fields[1, j] = ux
+        fields[j // HALF_BAND, 0, j % HALF_BAND] = pressure
+        fields[j // HALF_BAND, 1, j % HALF_BAND] = ux
+        if j % HALF_BAND == HALF_BAND - 1:
+            half = j // HALF_BAND
+            send_ref[pl.ds(half, AXIAL, stride=2), :] = fields[half].reshape(BAND * SECTOR, AXIAL).T
 
     sweep(load, step, store)
-    for f in (0, 1):
-        turned = fields[f].reshape(BAND * SECTOR, AXIAL).T
-        send_ref[pl.ds(f, AXIAL, stride=2), :] = turned
 
 
 def write_kernel(flow_ref, out_ref, sem):
@@ -429,32 +430,32 @@
     copy.wait()
 
 
-def mode_kernel(got_ref, basis_ref, keep_ref, give_ref, turned):
+def mode_kernel(mine, got_ref, basis_ref, out_ref, turned):
     chips = got_ref.shape[0] // 8
     core = lax.axis_index("theta") % 2
+    first = 4 * (core if mine else 1 - core)
     left = lax.broadcasted_iota(jnp.int32, (BAND, 2 * chips), 1) < chips
     parts = []
-    for n in range(8):
-        cells = got_ref[pl.ds(n, chips, stride=8), :]
+    for n in range(4):
+        cells = got_ref[pl.ds(first + n, chips, stride=8), :]
         turned[n] = jnp.concatenate([cells, cells], axis=0).T
         rows = [turned[n, pl.ds(m, BAND, stride=SECTOR), :] for m in range(SECTOR)]
         parts.append(
             jnp.concatenate([jnp.where(left, rows[m], rows[m + 1]) for m in range(0, SECTOR, 2)], axis=1)
         )
-    product = jnp.dot(
+    out_ref[...] = jnp.dot(
         jnp.concatenate(parts, axis=0), basis_ref[core], precision=lax.Precision.HIGHEST, preferred_element_type=F32
     )
-    half = 4 * BAND
-    keep_ref[...] = jnp.where(core == 0, product[:half], product[half:])
-    give_ref[...] = jnp.where(core == 0, product[half:], product[:half])
 
 
 def sum_kernel(keep_ref, got_ref, out_ref):
     total = keep_ref[...] + got_ref[...]
     for e in (0, 1):
-        for f in (0, 1):
-            n = 2 * e + f
-            out_ref[e, :, 2 * MODES * f : 2 * MODES * (f + 1)] = total[BAND * n : BAND * (n + 1)]
+        for half in (0, 1):
+            for f in (0, 1):
+                at = (2 * e + half) * BAND + f * HALF_BAND
+                rows = slice(half * HALF_BAND, (half + 1) * HALF_BAND)
+                out_ref[e, rows, 2 * MODES * f : 2 * MODES * (f + 1)] = total[at : at + HALF_BAND]
 
 
 def mode_basis(sectors):
@@ -565,7 +566,7 @@
             pltpu.VMEM((5, 4, SECTOR, AXIAL), F32),
             pltpu.VMEM((5, SECTOR, AXIAL), F32),
             pltpu.VMEM((5, 4, SECTOR, AXIAL), F32),
-            pltpu.VMEM((2, BAND, SECTOR, AXIAL), F32),
+            pltpu.VMEM((2, 2, HALF_BAND, SECTOR, AXIAL), F32),
         ],
         compiler_params=limit(8),
     )(blade, edge_columns, own_columns, rad_in, part, source, next_in, other_in, core_in)
@@ -578,15 +579,25 @@
         tiled=True,
         axis_index_groups=[[2 * chip + c for chip in range(chips)] for c in (0, 1)],
     )
-    keep, give = pl.pallas_call(
-        mode_kernel,
-        out_shape=[shaped(4 * BAND, 2 * MODES)] * 2,
-        in_specs=[vmem()] * 2,
-        out_specs=[vmem()] * 2,
-        scratch_shapes=[pltpu.VMEM((8, BAND * SECTOR, 2 * chips), F32)],
-        compiler_params=limit(4),
-    )(got.reshape(8 * chips, 128), jnp.asarray(mode_basis(sectors)))
-    given = lax.ppermute(give, "theta", core)
+    got = got.reshape(8 * chips, 128)
+    basis = jnp.asarray(mode_basis(sectors))
+
+    def modes(mine):
+        def kernel(*refs):
+            mode_kernel(mine, *refs)
+
+        return pl.pallas_call(
+            kernel,
+            out_shape=shaped(4 * BAND, 2 * MODES),
+            in_specs=[vmem()] * 2,
+            out_specs=vmem(),
+            scratch_shapes=[pltpu.VMEM((4, BAND * SECTOR, 2 * chips), F32)],
+            compiler_params=limit(4),
+            cost_estimate=pl.CostEstimate(flops=20_000_000, bytes_accessed=800_000, transcendentals=0),
+        )(got, basis)
+
+    given = lax.ppermute(modes(False), "theta", core)
+    keep = modes(True)
     flow_state = pl.pallas_call(
         write_kernel,
         out_shape=shaped(5, BAND, SECTOR, AXIAL),

time: 48 us -> 47.9 us (level)
  transfers between devices with their start and end apart: 5 -> 5, of which waited for: 2 -> 1; matrix products, arithmetic and copies ran while one was open for 0% -> 0% of each run, Pallas kernels for 9% -> 10%
where the time goes in v13:
time: 47.9 us; the launch traced here: 47.6 us
  blocking collectives  24 us (50%)
  starting transfers between devices  13.2 us (28%)
  Pallas kernels  8.5 us (18%)
  waiting for transfers between devices  1.15 us (2%)
  between operations  0.73 us (2%)
    all_to_all x1, blocking collectives, per_device(): lax.all_to_all(send.reshape(chips, 8, 128), 'theta', split_axis=0, concat...  24 us
    ppermute x1, starting transfers between devices, per_device(): core_in = lax.ppermute(core_out, 'theta', core)  7.59 us
    ppermute x1, starting transfers between devices, per_device(): other_in = lax.ppermute(other_out, 'theta', other)  3 us
    ppermute x1, starting transfers between devices, per_device(): rad_in = lax.ppermute(near, 'rad', swap)  2.21 us
    pallas_call x1, Pallas kernels, per_device(): pl.pallas_call(final, out_shape=[shaped(5, BAND, SECTOR, AXIAL), shaped(2...  1.77 us
    pallas_call x1, Pallas kernels, per_device(): pl.pallas_call(early, out_shape=[shaped(5, BAND, SECTOR, AXIAL)] * 2, in_...  1.45 us
    pallas_call x1, Pallas kernels, per_device(): pl.pallas_call(load_kernel, out_shape=[shaped(5, BAND, SECTOR, AXIAL)] *...  1.3 us
    ppermute x1, waiting for transfers between devices, per_device(): next_in = lax.ppermute(next_out, 'rad', swap)  1.14 us
  transfers between devices with their start and end apart: 5, of which 1 were waited for; matrix products, arithmetic and copies ran while one was open for 0% of the time, Pallas kernels for 10%

profile of v13, /device:TPU:1, one launch (start us, length us, event | category | flops | bytes accessed | tf_op | source)
XLA Modules:
  0.0 47.6 jit_solution(8436597707321234777)
XLA Ops:
  0.6 0.8 %shard_map.61 = f32[5,8,256]{2,1,0:T(8,128)S(1)} custom-call(f32[5,16,8,256]{3,2,1,0:T(8,128)} %q_ref.3), custom_call_target="tpu_custom_call" | custom-call | tf_op jit(solution)/shard_map/pallas_call | solution.py:508
  1.4 2.2 %collective-permute-start = (f32[5,8,256]{2,1,0:T(8,128)S(1)}, f32[5,8,256]{2,1,0:T(8,128)S(1)}, u32[]{:S(2)}, u32[]{:S(2)}) collective-permute-start(f32[5,8,256]{2,1,0:T(8,128)S(1)} %shard_map.61), channel_id=1, source_target_pairs={{0,1},{1,0},{2,3},{3,2},{4,5},{5,4},{6,7},{7,6},{8,9},{9,8},{10,11... | collective-permute-start | bytes 122888 | tf_op jit(solution)/shard_map/ppermute | solution.py:516
  3.6 1.3 %shard_map.59 = (f32[5,16,8,256]{3,2,1,0:T(8,128)S(1)}, f32[5,16,8,256]{3,2,1,0:T(8,128)S(1)}) custom-call(f32[5,16,8,256]{3,2,1,0:T(8,128)} %q_ref.3, f32[5,16,8,256]{3,2,1,0:T(8,128)} %qp_ref.1), custom_call_target="tpu_custom_call" | custom-call | bytes 3000000 | tf_op jit(solution)/shard_map/pallas_call | solution.py:517
  5.0 0.7 %shard_map.60.refs_1_ = f32[5,2,32,256]{3,2,1,0:T(8,128)S(1)} custom-call(f32[5,16,8,256]{3,2,1,0:T(8,128)S(1)} %get-tuple-element.11.refs_0_.refs_1_, f32[5,16,8,256]{3,2,1,0:T(8,128)S(1)} %get-tuple-element.12.refs_1_.refs_2_), custom_call_target="tpu_custom_call" | custom-call | flops 5000000 | bytes 2000000 | tf_op jit(solution)/shard_map/pallas_call | solution.py:526
  5.6 0.0 collective-permute-done.refs_2_.refs_3_
  5.6 0.1 shard_map.62
  5.7 3.0 %collective-permute-start.2 = (f32[168,256]{1,0:T(8,128)S(1)}, f32[168,256]{1,0:T(8,128)S(1)}, u32[]{:S(2)}, u32[]{:S(2)}) collective-permute-start(f32[168,256]{1,0:T(8,128)S(1)} %get-tuple-element.16), channel_id=1, source_target_pairs={{0,254},{2,4},{4,2},{6,8},{8,6},{10,12},{12,10},{14,16},{16,14},{1... | collective-permute-start | bytes 516104 | tf_op jit(solution)/shard_map/ppermute | solution.py:543
  8.7 0.0 copy-start.1
  8.7 7.6 %collective-permute-start.3 = (f32[168,256]{1,0:T(8,128)S(1)}, f32[168,256]{1,0:T(8,128)S(1)}, u32[]{:S(2)}, u32[]{:S(2)}) collective-permute-start(f32[168,256]{1,0:T(8,128)S(1)} %get-tuple-element.17), channel_id=1, source_target_pairs={{0,2},{2,0},{4,6},{6,4},{8,10},{10,8},{12,14},{14,12},{16,18},{18,... | collective-permute-start | bytes 516104 | tf_op jit(solution)/shard_map/ppermute | solution.py:542
  16.3 0.0 copy-done.1
  16.3 0.2 shard_map.64
  16.5 0.3 collective-permute-start.1
  16.8 1.4 %shard_map.63 = (f32[5,16,8,256]{3,2,1,0:T(8,128)S(1)}, f32[5,16,8,256]{3,2,1,0:T(8,128)S(1)}) custom-call(s32[1,256]{1,0:T(1,128)S(1)} %bitcast.7, f32[5,16,8,256]{3,2,1,0:T(8,128)S(1)} %get-tuple-element.11.refs_0_.refs_1_, f32[5,16,8,256]{3,2,1,0:T(8,128)S(1)} %get-tuple-element.12.refs_1_.refs_2_, f32[5,8,256]{2,1,0:T(8,128)S(1)} %collective-permute-done.refs_2_.refs_3_), custom_call_target="tpu_custom_call" | custom-call | flops 10000000 | bytes 3500000 | tf_op jit(solution)/shard_map/pallas_call | solution.py:552
  18.3 1.1 %collective-permute-done.1.refs_6_ = f32[5,8,256]{2,1,0:T(8,128)S(1)} collective-permute-done((f32[5,8,256]{2,1,0:T(8,128)S(1)}, f32[5,8,256]{2,1,0:T(8,128)S(1)}, u32[]{:S(2)}, u32[]{:S(2)}) %collective-permute-start.1) | collective-permute-done | bytes 40992 | tf_op jit(solution)/shard_map/ppermute | solution.py:551
  19.4 0.0 collective-permute-done.2.refs_7_
  19.5 0.0 collective-permute-done.3.refs_8_
  19.5 1.8 %shard_map.65 = (f32[5,16,8,256]{3,2,1,0:T(8,128)S(1)}, f32[512,128]{1,0:T(8,128)S(1)}) custom-call(s32[1,256]{1,0:T(1,128)S(1)} %bitcast.8, f32[5,2,32,256]{3,2,1,0:T(8,128)S(1)} %shard_map.60.refs_1_, f32[5,2,16,256]{3,2,1,0:T(8,128)S(1)} %get-tuple-element.13.refs_2_, f32[5,8,256]{2,1,0:T(8,128)S(1)} %collective-permute-done.refs_2_.refs_3_, ...), custom_call_target="tpu_custom_call" | custom-call | tf_op jit(solution)/shard_map/pallas_call | solution.py:560
  21.2 0.0 copy-start
  21.2 24.0 %all_to_all.5 = f32[64,8,128]{2,1,0:T(8,128)S(1)} all-to-all(f32[64,8,128]{2,1,0:T(8,128)S(1)} %bitcast.5), channel_id=1, replica_groups={{0,4,8,12,16,20,24,28,32,36,40,44,48,52,56,60,64,68,72,76,80,84,88,92,9..., dimensions={0} | all-to-all | bytes 524288 | tf_op jit(solution)/shard_map/all_to_all | solution.py:574
  45.3 0.0 copy-done
  45.3 0.4 shard_map.68
  45.6 0.1 collective-permute-start.4
  45.7 0.8 %shard_map.66 = f32[5,16,8,256]{3,2,1,0:T(8,128)} custom-call(f32[5,16,8,256]{3,2,1,0:T(8,128)S(1)} %get-tuple-element.18.flow_ref), custom_call_target="tpu_custom_call" | custom-call | bytes 1400000 | tf_op jit(solution)/shard_map/pallas_call | solution.py:601
  46.6 0.4 shard_map.67.keep_ref
  47.0 0.0 collective-permute-done.4.got_ref
  47.0 0.6 %shard_map.69 = f32[2,16,256]{2,1,0:T(8,128)} custom-call(f32[64,128]{1,0:T(8,128)S(1)} %shard_map.67.keep_ref, f32[64,128]{1,0:T(8,128)S(1)} %collective-permute-done.4.got_ref), custom_call_target="tpu_custom_call" | custom-call | tf_op jit(solution)/shard_map/pallas_call | solution.py:610
Async XLA Ops:
  1.4 4.2 %collective-permute-start = (f32[5,8,256]{2,1,0:T(8,128)S(1)}, f32[5,8,256]{2,1,0:T(8,128)S(1)}, u32[]{:S(2)}, u32[]{:S(2)}) collective-permute-start(f32[5,8,256]{2,1,0:T(8,128)S(1)} %shard_map.61), channel_id=1, source_target_pairs={{0,1},{1,0},{2,3},{3,2},{4,5},{5,4},{6,7},{7,6},{8,9},{9,8},{10,11... | collective-permute-start | bytes 122888 | tf_op jit(solution)/shard_map/ppermute | solution.py:516
  5.7 13.7 %collective-permute-start.2 = (f32[168,256]{1,0:T(8,128)S(1)}, f32[168,256]{1,0:T(8,128)S(1)}, u32[]{:S(2)}, u32[]{:S(2)}) collective-permute-start(f32[168,256]{1,0:T(8,128)S(1)} %get-tuple-element.16), channel_id=1, source_target_pairs={{0,254},{2,4},{4,2},{6,8},{8,6},{10,12},{12,10},{14,16},{16,14},{1... | collective-permute-start | bytes 516104 | tf_op jit(solution)/shard_map/ppermute | solution.py:543
  8.7 7.6 %copy-start.1 = (s32[256]{0:T(256)S(1)}, s32[256]{0:T(256)}, u32[]{:S(2)}) copy-start(s32[256]{0:T(256)} %param.6) | copy-start | bytes 3076
  8.7 10.7 %collective-permute-start.3 = (f32[168,256]{1,0:T(8,128)S(1)}, f32[168,256]{1,0:T(8,128)S(1)}, u32[]{:S(2)}, u32[]{:S(2)}) collective-permute-start(f32[168,256]{1,0:T(8,128)S(1)} %get-tuple-element.17), channel_id=1, source_target_pairs={{0,2},{2,0},{4,6},{6,4},{8,10},{10,8},{12,14},{14,12},{16,18},{18,... | collective-permute-start | bytes 516104 | tf_op jit(solution)/shard_map/ppermute | solution.py:542
  16.5 2.9 %collective-permute-start.1 = (f32[5,8,256]{2,1,0:T(8,128)S(1)}, f32[5,8,256]{2,1,0:T(8,128)S(1)}, u32[]{:S(2)}, u32[]{:S(2)}) collective-permute-start(f32[5,8,256]{2,1,0:T(8,128)S(1)} %shard_map.64), channel_id=1, source_target_pairs={{0,1},{1,0},{2,3},{3,2},{4,5},{5,4},{6,7},{7,6},{8,9},{9,8},{10,11... | collective-permute-start | bytes 122888 | tf_op jit(solution)/shard_map/ppermute | solution.py:551
  21.2 24.0 %copy-start = (f32[2,512,128]{2,1,0:T(8,128)S(1)}, f32[2,512,128]{2,1,0:T(8,128)}, u32[]{:S(2)}) copy-start(f32[2,512,128]{2,1,0:T(8,128)} %constant.2.clone.refs_1_) | copy-start | bytes 1572868
  45.6 1.4 %collective-permute-start.4 = (f32[64,128]{1,0:T(8,128)S(1)}, f32[64,128]{1,0:T(8,128)S(1)}, u32[]{:S(2)}, u32[]{:S(2)}) collective-permute-start(f32[64,128]{1,0:T(8,128)S(1)} %shard_map.68), channel_id=1, source_target_pairs={{0,2},{2,0},{4,6},{6,4},{8,10},{10,8},{12,14},{14,12},{16,18},{18,... | collective-permute-start | bytes 98312 | tf_op jit(solution)/shard_map/ppermute | solution.py:599

commit v14 on v13

--- a/solution.py
+++ b/solution.py
@@ -424,12 +424,6 @@
     sweep(load, step, store)
 
 
-def write_kernel(flow_ref, out_ref, sem):
-    copy = pltpu.make_async_copy(flow_ref, out_ref, sem)
-    copy.start()
-    copy.wait()
-
-
 def mode_kernel(mine, got_ref, basis_ref, out_ref, turned):
     chips = got_ref.shape[0] // 8
     core = lax.axis_index("theta") % 2
@@ -446,6 +440,13 @@
     out_ref[...] = jnp.dot(
         jnp.concatenate(parts, axis=0), basis_ref[core], precision=lax.Precision.HIGHEST, preferred_element_type=F32
     )
+
+
+def keep_kernel(got_ref, basis_ref, flow_ref, out_ref, flow_out_ref, turned, sem):
+    copy = pltpu.make_async_copy(flow_ref, flow_out_ref, sem)
+    copy.start()
+    mode_kernel(True, got_ref, basis_ref, out_ref, turned)
+    copy.wait()
 
 
 def sum_kernel(keep_ref, got_ref, out_ref):
@@ -582,31 +583,28 @@
     got = got.reshape(8 * chips, 128)
     basis = jnp.asarray(mode_basis(sectors))
 
-    def modes(mine):
-        def kernel(*refs):
-            mode_kernel(mine, *refs)
-
-        return pl.pallas_call(
-            kernel,
-            out_shape=shaped(4 * BAND, 2 * MODES),
-            in_specs=[vmem()] * 2,
-            out_specs=vmem(),
-            scratch_shapes=[pltpu.VMEM((4, BAND * SECTOR, 2 * chips), F32)],
-            compiler_params=limit(4),
-            cost_estimate=pl.CostEstimate(flops=20_000_000, bytes_accessed=800_000, transcendentals=0),
-        )(got, basis)
-
-    given = lax.ppermute(modes(False), "theta", core)
-    keep = modes(True)
-    flow_state = pl.pallas_call(
-        write_kernel,
-        out_shape=shaped(5, BAND, SECTOR, AXIAL),
-        in_specs=[vmem()],
-        out_specs=hbm,
-        scratch_shapes=[pltpu.SemaphoreType.DMA],
-        compiler_params=limit(2),
-        cost_estimate=pl.CostEstimate(flops=0, bytes_accessed=1_400_000, transcendentals=0),
-    )(flow_state)
+    def give_kernel(*refs):
+        mode_kernel(False, *refs)
+
+    turned = pltpu.VMEM((4, BAND * SECTOR, 2 * chips), F32)
+    give = pl.pallas_call(
+        give_kernel,
+        out_shape=shaped(4 * BAND, 2 * MODES),
+        in_specs=[vmem()] * 2,
+        out_specs=vmem(),
+        scratch_shapes=[turned],
+        compiler_params=limit(4),
+    )(got, basis)
+    given = lax.ppermute(give, "theta", core)
+    keep, flow_state = pl.pallas_call(
+        keep_kernel,
+        out_shape=[shaped(4 * BAND, 2 * MODES), shaped(5, BAND, SECTOR, AXIAL)],
+        in_specs=[vmem()] * 3,
+        out_specs=[vmem(), hbm],
+        scratch_shapes=[turned, pltpu.SemaphoreType.DMA],
+        compiler_params=limit(4),
+        cost_estimate=pl.CostEstimate(flops=20_000_000, bytes_accessed=2_000_000, transcendentals=0),
+    )(got, basis, flow_state)
     spectra = pl.pallas_call(
         sum_kernel,
         out_shape=shaped(2, BAND, 4 * MODES),

time: 47.9 us -> 47.8 us (level)
    pallas_call x3 -> x2, Pallas kernels: 1.63 us -> 1.23 us  [the longest x1 0.85 us: per_device(): pl.pallas_call(keep_kernel, out_shape=[shaped(4 * BAND, 2 * MODES), shape...]
  transfers between devices with their start and end apart: 5 -> 5, of which waited for: 1 -> 2; matrix products, arithmetic and copies ran while one was open for 0% -> 0% of each run, Pallas kernels for 10% -> 9%
where the time goes in v14:
time: 47.8 us; the launch traced here: 47.6 us
  blocking collectives  24 us (50%)
  starting transfers between devices  13.2 us (28%)
  Pallas kernels  8.1 us (17%)
  waiting for transfers between devices  1.49 us (3%)
  between operations  0.72 us (2%)
    all_to_all x1, blocking collectives, per_device(): lax.all_to_all(send.reshape(chips, 8, 128), 'theta', split_axis=0, concat...  24 us
    ppermute x1, starting transfers between devices, per_device(): core_in = lax.ppermute(core_out, 'theta', core)  7.59 us
    ppermute x1, starting transfers between devices, per_device(): other_in = lax.ppermute(other_out, 'theta', other)  3 us
    ppermute x1, starting transfers between devices, per_device(): rad_in = lax.ppermute(near, 'rad', swap)  2.21 us
    pallas_call x1, Pallas kernels, per_device(): pl.pallas_call(final, out_shape=[shaped(5, BAND, SECTOR, AXIAL), shaped(2...  1.77 us
    pallas_call x1, Pallas kernels, per_device(): pl.pallas_call(early, out_shape=[shaped(5, BAND, SECTOR, AXIAL)] * 2, in_...  1.45 us
    pallas_call x1, Pallas kernels, per_device(): pl.pallas_call(load_kernel, out_shape=[shaped(5, BAND, SECTOR, AXIAL)] *...  1.3 us
    ppermute x1, waiting for transfers between devices, per_device(): next_in = lax.ppermute(next_out, 'rad', swap)  1.14 us
  transfers between devices with their start and end apart: 5, of which 2 were waited for; matrix products, arithmetic and copies ran while one was open for 0% of the time, Pallas kernels for 9%

profile of v14, /device:TPU:1, one launch (start us, length us, event | category | flops | bytes accessed | tf_op | source)
XLA Modules:
  0.0 47.6 jit_solution(15315198884811313493)
XLA Ops:
  0.6 0.8 %shard_map.61 = f32[5,8,256]{2,1,0:T(8,128)S(1)} custom-call(f32[5,16,8,256]{3,2,1,0:T(8,128)} %q_ref.3), custom_call_target="tpu_custom_call" | custom-call | tf_op jit(solution)/shard_map/pallas_call | solution.py:509
  1.4 2.2 %collective-permute-start = (f32[5,8,256]{2,1,0:T(8,128)S(1)}, f32[5,8,256]{2,1,0:T(8,128)S(1)}, u32[]{:S(2)}, u32[]{:S(2)}) collective-permute-start(f32[5,8,256]{2,1,0:T(8,128)S(1)} %shard_map.61), channel_id=1, source_target_pairs={{0,1},{1,0},{2,3},{3,2},{4,5},{5,4},{6,7},{7,6},{8,9},{9,8},{10,11... | collective-permute-start | bytes 122888 | tf_op jit(solution)/shard_map/ppermute | solution.py:517
  3.6 1.3 %shard_map.59 = (f32[5,16,8,256]{3,2,1,0:T(8,128)S(1)}, f32[5,16,8,256]{3,2,1,0:T(8,128)S(1)}) custom-call(f32[5,16,8,256]{3,2,1,0:T(8,128)} %q_ref.3, f32[5,16,8,256]{3,2,1,0:T(8,128)} %qp_ref.1), custom_call_target="tpu_custom_call" | custom-call | bytes 3000000 | tf_op jit(solution)/shard_map/pallas_call | solution.py:518
  5.0 0.7 %shard_map.60.refs_1_ = f32[5,2,32,256]{3,2,1,0:T(8,128)S(1)} custom-call(f32[5,16,8,256]{3,2,1,0:T(8,128)S(1)} %get-tuple-element.13.refs_0_.refs_1_, f32[5,16,8,256]{3,2,1,0:T(8,128)S(1)} %get-tuple-element.14.refs_1_.refs_2_), custom_call_target="tpu_custom_call" | custom-call | flops 5000000 | bytes 2000000 | tf_op jit(solution)/shard_map/pallas_call | solution.py:527
  5.6 0.0 collective-permute-done.refs_2_.refs_3_
  5.6 0.1 shard_map.62
  5.7 3.0 %collective-permute-start.2 = (f32[168,256]{1,0:T(8,128)S(1)}, f32[168,256]{1,0:T(8,128)S(1)}, u32[]{:S(2)}, u32[]{:S(2)}) collective-permute-start(f32[168,256]{1,0:T(8,128)S(1)} %get-tuple-element.18), channel_id=1, source_target_pairs={{0,254},{2,4},{4,2},{6,8},{8,6},{10,12},{12,10},{14,16},{16,14},{1... | collective-permute-start | bytes 516104 | tf_op jit(solution)/shard_map/ppermute | solution.py:544
  8.7 0.0 copy-start.1
  8.7 7.6 %collective-permute-start.3 = (f32[168,256]{1,0:T(8,128)S(1)}, f32[168,256]{1,0:T(8,128)S(1)}, u32[]{:S(2)}, u32[]{:S(2)}) collective-permute-start(f32[168,256]{1,0:T(8,128)S(1)} %get-tuple-element.19), channel_id=1, source_target_pairs={{0,2},{2,0},{4,6},{6,4},{8,10},{10,8},{12,14},{14,12},{16,18},{18,... | collective-permute-start | bytes 516104 | tf_op jit(solution)/shard_map/ppermute | solution.py:543
  16.3 0.0 copy-done.1
  16.3 0.2 shard_map.64
  16.5 0.3 collective-permute-start.1
  16.8 1.4 %shard_map.63 = (f32[5,16,8,256]{3,2,1,0:T(8,128)S(1)}, f32[5,16,8,256]{3,2,1,0:T(8,128)S(1)}) custom-call(s32[1,256]{1,0:T(1,128)S(1)} %bitcast.7, f32[5,16,8,256]{3,2,1,0:T(8,128)S(1)} %get-tuple-element.13.refs_0_.refs_1_, f32[5,16,8,256]{3,2,1,0:T(8,128)S(1)} %get-tuple-element.14.refs_1_.refs_2_, f32[5,8,256]{2,1,0:T(8,128)S(1)} %collective-permute-done.refs_2_.refs_3_), custom_call_target="tpu_custom_call" | custom-call | flops 10000000 | bytes 3500000 | tf_op jit(solution)/shard_map/pallas_call | solution.py:553
  18.3 1.1 %collective-permute-done.1.refs_6_ = f32[5,8,256]{2,1,0:T(8,128)S(1)} collective-permute-done((f32[5,8,256]{2,1,0:T(8,128)S(1)}, f32[5,8,256]{2,1,0:T(8,128)S(1)}, u32[]{:S(2)}, u32[]{:S(2)}) %collective-permute-start.1) | collective-permute-done | bytes 40992 | tf_op jit(solution)/shard_map/ppermute | solution.py:552
  19.4 0.0 collective-permute-done.2.refs_7_
  19.5 0.0 collective-permute-done.3.refs_8_
  19.5 1.8 %shard_map.65 = (f32[5,16,8,256]{3,2,1,0:T(8,128)S(1)}, f32[512,128]{1,0:T(8,128)S(1)}) custom-call(s32[1,256]{1,0:T(1,128)S(1)} %bitcast.8, f32[5,2,32,256]{3,2,1,0:T(8,128)S(1)} %shard_map.60.refs_1_, f32[5,2,16,256]{3,2,1,0:T(8,128)S(1)} %get-tuple-element.15.refs_2_, f32[5,8,256]{2,1,0:T(8,128)S(1)} %collective-permute-done.refs_2_.refs_3_, ...), custom_call_target="tpu_custom_call" | custom-call | tf_op jit(solution)/shard_map/pallas_call | solution.py:561
  21.2 0.0 copy-start
  21.2 24.0 %all_to_all.5 = f32[64,8,128]{2,1,0:T(8,128)S(1)} all-to-all(f32[64,8,128]{2,1,0:T(8,128)S(1)} %bitcast.5), channel_id=1, replica_groups={{0,4,8,12,16,20,24,28,32,36,40,44,48,52,56,60,64,68,72,76,80,84,88,92,9..., dimensions={0} | all-to-all | bytes 524288 | tf_op jit(solution)/shard_map/all_to_all | solution.py:575
  45.3 0.0 copy-done
  45.3 0.4 shard_map.67
  45.6 0.1 collective-permute-start.4
  45.7 0.8 %shard_map.66 = (f32[64,128]{1,0:T(8,128)S(1)}, f32[5,16,8,256]{3,2,1,0:T(8,128)}) custom-call(f32[512,128]{1,0:T(8,128)S(1)} %bitcast.4, f32[2,512,128]{2,1,0:T(8,128)S(1)} %copy-done, f32[5,16,8,256]{3,2,1,0:T(8,128)S(1)} %get-tuple-element.21.flow_ref), custom_call_target="tpu_custom_call" | custom-call | flops 20000000 | bytes 2000000 | tf_op jit(solution)/shard_map/pallas_call | solution.py:599
  46.6 0.3 collective-permute-done.4.got_ref
  46.9 0.6 %shard_map.68 = f32[2,16,256]{2,1,0:T(8,128)} custom-call(f32[64,128]{1,0:T(8,128)S(1)} %get-tuple-element.23.keep_ref, f32[64,128]{1,0:T(8,128)S(1)} %collective-permute-done.4.got_ref), custom_call_target="tpu_custom_call" | custom-call | tf_op jit(solution)/shard_map/pallas_call | solution.py:608
Async XLA Ops:
  1.4 4.2 %collective-permute-start = (f32[5,8,256]{2,1,0:T(8,128)S(1)}, f32[5,8,256]{2,1,0:T(8,128)S(1)}, u32[]{:S(2)}, u32[]{:S(2)}) collective-permute-start(f32[5,8,256]{2,1,0:T(8,128)S(1)} %shard_map.61), channel_id=1, source_target_pairs={{0,1},{1,0},{2,3},{3,2},{4,5},{5,4},{6,7},{7,6},{8,9},{9,8},{10,11... | collective-permute-start | bytes 122888 | tf_op jit(solution)/shard_map/ppermute | solution.py:517
  5.7 13.7 %collective-permute-start.2 = (f32[168,256]{1,0:T(8,128)S(1)}, f32[168,256]{1,0:T(8,128)S(1)}, u32[]{:S(2)}, u32[]{:S(2)}) collective-permute-start(f32[168,256]{1,0:T(8,128)S(1)} %get-tuple-element.18), channel_id=1, source_target_pairs={{0,254},{2,4},{4,2},{6,8},{8,6},{10,12},{12,10},{14,16},{16,14},{1... | collective-permute-start | bytes 516104 | tf_op jit(solution)/shard_map/ppermute | solution.py:544
  8.7 7.6 %copy-start.1 = (s32[256]{0:T(256)S(1)}, s32[256]{0:T(256)}, u32[]{:S(2)}) copy-start(s32[256]{0:T(256)} %param.6) | copy-start | bytes 3076
  8.7 10.7 %collective-permute-start.3 = (f32[168,256]{1,0:T(8,128)S(1)}, f32[168,256]{1,0:T(8,128)S(1)}, u32[]{:S(2)}, u32[]{:S(2)}) collective-permute-start(f32[168,256]{1,0:T(8,128)S(1)} %get-tuple-element.19), channel_id=1, source_target_pairs={{0,2},{2,0},{4,6},{6,4},{8,10},{10,8},{12,14},{14,12},{16,18},{18,... | collective-permute-start | bytes 516104 | tf_op jit(solution)/shard_map/ppermute | solution.py:543
  16.5 2.9 %collective-permute-start.1 = (f32[5,8,256]{2,1,0:T(8,128)S(1)}, f32[5,8,256]{2,1,0:T(8,128)S(1)}, u32[]{:S(2)}, u32[]{:S(2)}) collective-permute-start(f32[5,8,256]{2,1,0:T(8,128)S(1)} %shard_map.64), channel_id=1, source_target_pairs={{0,1},{1,0},{2,3},{3,2},{4,5},{5,4},{6,7},{7,6},{8,9},{9,8},{10,11... | collective-permute-start | bytes 122888 | tf_op jit(solution)/shard_map/ppermute | solution.py:552
  21.2 24.0 %copy-start = (f32[2,512,128]{2,1,0:T(8,128)S(1)}, f32[2,512,128]{2,1,0:T(8,128)}, u32[]{:S(2)}) copy-start(f32[2,512,128]{2,1,0:T(8,128)} %constant.2.clone.basis_ref.refs_1_) | copy-start | bytes 1572868
  45.6 1.3 %collective-permute-start.4 = (f32[64,128]{1,0:T(8,128)S(1)}, f32[64,128]{1,0:T(8,128)S(1)}, u32[]{:S(2)}, u32[]{:S(2)}) collective-permute-start(f32[64,128]{1,0:T(8,128)S(1)} %shard_map.67), channel_id=1, source_target_pairs={{0,2},{2,0},{4,6},{6,4},{8,10},{10,8},{12,14},{14,12},{16,18},{18,... | collective-permute-start | bytes 98312 | tf_op jit(solution)/shard_map/ppermute | solution.py:598
